TPU v7x, 32 devices: a whole 2x2x4 slice. The times are simulated.
32 devices in a mesh: dp: 8 (over y, x, core), tensor: 4 (over z).
Axes of the slice: x: 2, y: 2, z: 4, core: 2. Of those that a mesh axis runs over, the one named last changes fastest.
Arguments:
- layer_input: bfloat16 [8192, 2048], P('dp'), may hold values from -6 to 6
- lengths: int32 [8], P('dp'), may hold values from 128 to 1024, as said below
- ln1_gain: float32 [2048], replicated, may hold values from 0.5 to 1.5
- ln1_shift: float32 [2048], replicated, may hold values from -1.2 to 1.2
- w_qkv: bfloat16 [2048, 3, 2048], P(None, None, 'tensor'), may hold values from -0.125 to 0.125
- b_qkv: float32 [3, 2048], P(None, 'tensor'), may hold values from -3 to 3
- w_dense: bfloat16 [2048, 2048], P('tensor'), may hold values from -1 to 1
- b_dense: float32 [2048], replicated, may hold values from -1.2 to 1.2
- ln2_gain: float32 [2048], replicated, may hold values from 0.5 to 1.5
- ln2_shift: float32 [2048], replicated, may hold values from -1.2 to 1.2
- w_in: bfloat16 [2048, 8192], P(None, 'tensor'), may hold values from -0.125 to 0.125
- b_in: float32 [8192], P('tensor'), may hold values from -3 to 3
- w_out: bfloat16 [8192, 2048], P('tensor'), may hold values from -0.0625 to 0.0625
- b_out: float32 [2048], replicated, may hold values from -1.2 to 1.2
- grad_out: bfloat16 [8192, 2048], P('dp'), may hold values from -6 to 6
Outputs:
- layer_output: bfloat16 [8192, 2048], P('dp')
- input_grad: bfloat16 [8192, 2048], P('dp')
- ln1_gain_grad: float32 [2048], replicated
- ln1_shift_grad: float32 [2048], replicated
- w_qkv_grad: float32 [2048, 3, 2048], P('dp', None, 'tensor')
- b_qkv_grad: float32 [3, 2048], P(None, 'tensor')
- w_dense_grad: float32 [2048, 2048], P('tensor', 'dp')
- b_dense_grad: float32 [2048], replicated
- ln2_gain_grad: float32 [2048], replicated
- ln2_shift_grad: float32 [2048], replicated
- w_in_grad: float32 [2048, 8192], P('dp', 'tensor')
- b_in_grad: float32 [8192], P('tensor')
- w_out_grad: float32 [8192, 2048], P('tensor', 'dp')
- b_out_grad: float32 [2048], replicated
Inputs may be any that keep to these rules, and one draw needn't show every extreme that they name: `lengths`: valid tokens of each sequence, counted from its first position; in every draw some sequence has all 1024.
All inputs are finite; a program needn't handle non-finite values.
Results may differ from a plain program's by a relative error of at most 0.011.
Values sent between devices are 32-bit elements; how exact they have to be, the bound alone decides.
No kernel may reach another device: no remote copies, remote signals or barrier semaphores. Data moves between devices by JAX's collectives and lax.ppermute only.
A program may use at most 320 MiB of HBM per device.

v0:
```python
from functools import partial
import math

import jax
import jax.numpy as jnp
from jax import lax
from jax.sharding import PartitionSpec as P

HD = 256
ROT = 64


EPS = 1e-05


def layer_norm(values, gain, shift):
    center = values - jnp.mean(values, -1, keepdims=True)
    spread = jnp.mean(center * center, -1, keepdims=True)
    return center * lax.rsqrt(spread + EPS) * gain + shift


def turn(values, cosine, sine):
    half = ROT // 2
    first = values[..., :half]
    second = values[..., half:ROT]
    rest = values[..., ROT:]
    return jnp.concatenate(
        [first * cosine - second * sine, second * cosine + first * sine, rest], -1
    )


def gelu_slope(values):
    return 0.5 * (1.0 + lax.erf(values / math.sqrt(2.0))) + values * jnp.exp(
        -0.5 * values * values
    ) / math.sqrt(2.0 * math.pi)


def local(
    layer_input,
    lengths,
    ln1_gain,
    ln1_shift,
    w_qkv,
    b_qkv,
    w_dense,
    b_dense,
    ln2_gain,
    ln2_shift,
    w_in,
    b_in,
    w_out,
    b_out,
    grad_out,
):
    rows = layer_input.shape[0]
    seqs = lengths.shape[0]
    span = rows // seqs
    heads_here = w_dense.shape[0] // HD
    block = min(512, span)
    scale = 1.0 / math.sqrt(HD)
    positions = jnp.arange(span)
    half = ROT // 2
    inverse = 10000.0 ** (-(2.0 * jnp.arange(half).astype(jnp.float32)) / ROT)
    angle = positions.astype(jnp.float32)[:, None] * inverse[None, :]
    cosine = jnp.cos(angle)[None, :, None, :]
    sine = jnp.sin(angle)[None, :, None, :]
    valid = (positions[None, :] < lengths[:, None]).astype(jnp.float32).reshape(rows, 1)

    def block_mask(start):
        query_pos = positions[start : start + block]
        causal = positions[None, :] <= query_pos[:, None]
        inside = positions[None, None, :] < lengths[:, None, None]
        return (causal[None] & inside)[:, None]

    def front(x_float):
        a_one = layer_norm(x_float, ln1_gain, ln1_shift).astype(jnp.bfloat16)
        qkv = jnp.einsum("td,dcf->tcf", a_one, w_qkv, preferred_element_type=jnp.float32) + b_qkv
        shaped = qkv.reshape(seqs, span, 3, heads_here, HD)
        query = turn(shaped[:, :, 0], cosine, sine).astype(jnp.bfloat16)
        key_rows = turn(shaped[:, :, 1], cosine, sine).astype(jnp.bfloat16)
        value = shaped[:, :, 2].astype(jnp.bfloat16)
        a_two = layer_norm(x_float, ln2_gain, ln2_shift).astype(jnp.bfloat16)
        hpre = jnp.dot(a_two, w_in, preferred_element_type=jnp.float32) + b_in
        hidden = jax.nn.gelu(hpre, approximate=False).astype(jnp.bfloat16)
        mixed_parts = []
        logsum_parts = []
        for start in range(0, span, block):
            query_block = query[:, start : start + block]
            scores = (
                jnp.einsum(
                    "sqhd,skhd->shqk", query_block, key_rows, preferred_element_type=jnp.float32
                )
                * scale
            )
            scores = jnp.where(block_mask(start), scores, -1e30)
            top = jnp.max(scores, -1, keepdims=True)
            expo = jnp.exp(scores - top)
            total = jnp.sum(expo, -1, keepdims=True)
            probs = (expo / total).astype(jnp.bfloat16)
            mixed_parts.append(
                jnp.einsum("shqk,skhd->sqhd", probs, value, preferred_element_type=jnp.float32)
            )
            logsum_parts.append(top + jnp.log(total))
        mixed = jnp.concatenate(mixed_parts, 1).reshape(rows, heads_here * HD).astype(jnp.bfloat16)
        return (a_one, a_two, query, key_rows, value, hpre, hidden, mixed, logsum_parts)

    x_float = layer_input.astype(jnp.float32)
    a_one, a_two, query, key_rows, value, hpre, hidden, mixed, logsum_parts = front(x_float)
    part = jnp.dot(mixed, w_dense, preferred_element_type=jnp.float32) + jnp.dot(
        hidden, w_out, preferred_element_type=jnp.float32
    )
    total_branch = lax.psum(part, "tensor")
    layer_output = (x_float + total_branch + b_dense + b_out).astype(jnp.bfloat16)
    x_again, output_after = lax.optimization_barrier((x_float, layer_output))
    a_one, a_two, query, key_rows, value, hpre, hidden, mixed, logsum_parts = front(x_again)
    cotan = grad_out.astype(jnp.float32) * valid
    cotan_low = cotan.astype(jnp.bfloat16)
    bias_out_grad = jnp.sum(cotan, 0)
    w_out_grad = jnp.einsum("tf,td->fd", hidden, cotan_low, preferred_element_type=jnp.float32)
    dhidden = jnp.einsum("td,fd->tf", cotan_low, w_out, preferred_element_type=jnp.float32)
    dhpre = (dhidden * gelu_slope(hpre)).astype(jnp.bfloat16)
    b_in_grad = jnp.sum(dhpre.astype(jnp.float32), 0)
    w_in_grad = jnp.einsum("td,tf->df", a_two, dhpre, preferred_element_type=jnp.float32)
    da_two = jnp.einsum("tf,df->td", dhpre, w_in, preferred_element_type=jnp.float32)
    w_dense_grad = jnp.einsum("te,td->ed", mixed, cotan_low, preferred_element_type=jnp.float32)
    dmixed = jnp.einsum("td,ed->te", cotan_low, w_dense, preferred_element_type=jnp.float32)
    dmixed = dmixed.astype(jnp.bfloat16).reshape(seqs, span, heads_here, HD)
    dquery_parts = []
    dkey = jnp.zeros((seqs, span, heads_here, HD), jnp.float32)
    dvalue = jnp.zeros((seqs, span, heads_here, HD), jnp.float32)
    for index, start in enumerate(range(0, span, block)):
        query_block = query[:, start : start + block]
        dmixed_block = dmixed[:, start : start + block]
        scores = (
            jnp.einsum("sqhd,skhd->shqk", query_block, key_rows, preferred_element_type=jnp.float32)
            * scale
        )
        scores = jnp.where(block_mask(start), scores, -1e30)
        probs = jnp.exp(scores - logsum_parts[index])
        dprobs = jnp.einsum(
            "sqhd,skhd->shqk", dmixed_block, value, preferred_element_type=jnp.float32
        )
        delta = jnp.sum(probs * dprobs, -1, keepdims=True)
        dscores = (probs * (dprobs - delta)).astype(jnp.bfloat16)
        dquery_parts.append(
            jnp.einsum("shqk,skhd->sqhd", dscores, key_rows, preferred_element_type=jnp.float32)
            * scale
        )
        dkey = (
            dkey
            + jnp.einsum(
                "shqk,sqhd->skhd", dscores, query_block, preferred_element_type=jnp.float32
            )
            * scale
        )
        dvalue = dvalue + jnp.einsum(
            "shqk,sqhd->skhd",
            probs.astype(jnp.bfloat16),
            dmixed_block,
            preferred_element_type=jnp.float32,
        )
    dquery = jnp.concatenate(dquery_parts, 1)
    turned, pull_turn = jax.vjp(partial(turn, cosine=cosine, sine=sine), dquery)
    dquery_pre = pull_turn(dquery)[0]
    dkey_pre = pull_turn(dkey)[0]
    dqkv = (
        jnp.stack([dquery_pre, dkey_pre, dvalue], 2)
        .reshape(rows, 3, heads_here * HD)
        .astype(jnp.bfloat16)
    )
    b_qkv_grad = jnp.sum(dqkv.astype(jnp.float32), 0)
    w_qkv_grad = jnp.einsum("td,tcf->dcf", a_one, dqkv, preferred_element_type=jnp.float32)
    da_one = jnp.einsum("tcf,dcf->td", dqkv, w_qkv, preferred_element_type=jnp.float32)
    w_qkv_grad, w_dense_grad, w_in_grad, w_out_grad = (
        lax.psum_scatter(w_qkv_grad, "dp", scatter_dimension=0, tiled=True),
        lax.psum_scatter(w_dense_grad, "dp", scatter_dimension=1, tiled=True),
        lax.psum_scatter(w_in_grad, "dp", scatter_dimension=0, tiled=True),
        lax.psum_scatter(w_out_grad, "dp", scatter_dimension=1, tiled=True),
    )
    norm_one, pull_one = jax.vjp(layer_norm, x_float, ln1_gain, ln1_shift)
    dx_one, gain_one, shift_one = pull_one(da_one)
    norm_two, pull_two = jax.vjp(layer_norm, x_float, ln2_gain, ln2_shift)
    dx_two, gain_two, shift_two = pull_two(da_two)
    dx_total, gain_one, shift_one, gain_two, shift_two = lax.psum(
        (dx_one + dx_two, gain_one, shift_one, gain_two, shift_two), "tensor"
    )
    input_grad = (cotan + dx_total).astype(jnp.bfloat16)
    gain_one, shift_one, gain_two, shift_two, b_qkv_grad, bias_out_grad, b_in_grad = lax.psum(
        (gain_one, shift_one, gain_two, shift_two, b_qkv_grad, bias_out_grad, b_in_grad), "dp"
    )
    return (
        layer_output,
        input_grad,
        gain_one,
        shift_one,
        w_qkv_grad,
        b_qkv_grad,
        w_dense_grad,
        bias_out_grad,
        gain_two,
        shift_two,
        w_in_grad,
        b_in_grad,
        w_out_grad,
        bias_out_grad,
    )


def solution(mesh):
    return jax.shard_map(
        local,
        mesh=mesh,
        in_specs=(
            P("dp", None),
            P("dp"),
            P(),
            P(),
            P(None, None, "tensor"),
            P(None, "tensor"),
            P("tensor", None),
            P(),
            P(),
            P(),
            P(None, "tensor"),
            P("tensor"),
            P("tensor", None),
            P(),
            P("dp", None),
        ),
        out_specs=(
            P("dp", None),
            P("dp", None),
            P(),
            P(),
            P("dp", None, "tensor"),
            P(None, "tensor"),
            P("tensor", "dp"),
            P(),
            P(),
            P(),
            P("dp", "tensor"),
            P("tensor"),
            P("tensor", "dp"),
            P(),
        ),
        check_vma=False,
    )
```

profile of v0, /device:TPU:0, one launch (start us, length us, event | category | flops | bytes accessed | tf_op | source)
XLA Modules:
  0.0 1275.3 jit_solution(16554896059630057701)
XLA Ops:
  14.4 10.4 broadcast_add_fusion.1
  56.2 5.6 fusion.262
  61.9 51.6 %fusion.37 = f32[1024,2048]{1,0:T(8,128)} fusion(f32[1024,2048]{1,0:T(8,128)} %fusion.262, bf16[2048,2048]{1,0:T(8,128)(2,1)} %param.27, bf16[2048,2048]{1,0:T(8,128)(2,1)} %param.25, bf16[1024,2048]{1,0:T(8,128)(2,1)} %param.15, f32[2048]{0:T(1024)S(1)} %copy-done.57, f32[2048]{0:T(1024)S(1)} %copy-done.55, f32[2048]{0:T(1024)S(1)} %copy-done.41, ...), kind=kOutput, calls=%fused_computation.75 | convolution fusion | flops 17332961280 | bytes 37781504 | tf_op jit(solution)/shard_map/dot_general | solution.py:109
  113.5 6.6 convert_element_type.249
  123.6 283.5 %all-reduce.11.cloned.1.call-done = f32[1024,2048]{1,0:T(8,128)} async-done(((f32[1024,2048]{1,0:T(8,128)}), f32[1024,2048]{1,0:T(8,128)}) %all-reduce.11.cloned.1.call-update) | async-done | bytes 8388624 | tf_op jit(solution)/shard_map/psum | solution.py:112
  407.1 8.4 add_convert_fusion.3
  415.5 3.8 reduce_sum.190
  419.4 4.5 multiply_reduce_fusion.3
  423.9 16.3 %fusion.254 = f32[1024,2048]{1,0:T(8,128)} fusion(bf16[2048,2048]{1,0:T(8,128)(2,1)} %param.25, f32[1024,2048]{1,0:T(8,128)} %convert_element_type.249, f32[1024]{0:T(1024)S(1)} %add_rsqrt_fusion, f32[1024]{0:T(1024)S(1)} %broadcast_multiply_fusion, f32[2048]{0:T(1024)S(1)} %copy-done.55, f32[2048]{0:T(1024)S(1)} %copy-done.41), kind=kOutput, calls=%fused_computation.351 | convolution fusion | flops 8600420352 | bytes 25190400 | tf_op jit(solution)/shard_map/dot_general | solution.py:83
  440.3 10.1 broadcast_add_fusion
  450.4 4.9 fusion.256
  480.6 3.6 multiply_reduce_fusion.6
  497.9 16.9 %convert_reduce_fusion = (f32[2048]{0:T(1024)}, bf16[1024,2048]{1,0:T(8,128)(2,1)}) fusion(f32[1024,2048]{1,0:T(8,128)} %fusion.254, f32[2048]{0:T(1024)S(1)} %copy-done.57, bf16[2048,2048]{1,0:T(8,128)(2,1)} %param.27, bf16[1024,2048]{1,0:T(8,128)(2,1)S(1)} %copy-done.28, f32[1024]{0:T(1024)S(1)} %copy-done.44), kind=kOutput, calls=%fused_computation.36 | convolution fusion | flops 8623486976 | bytes 25186304 | tf_op jit(solution)/shard_map/td,fd->tf/dot_general | solution.py:120
  522.1 4.4 add_convert_fusion.9
  531.0 4.1 add_convert_fusion.8
  536.6 15.0 %fusion.263 = f32[1024,2048]{1,0:T(8,128)} fusion(bf16[1024,2048]{1,0:T(8,128)(2,1)} %get-tuple-element.83, bf16[2048,2048]{1,0:T(8,128)(2,1)} %param.25), kind=kOutput, calls=%fused_computation.360 | convolution fusion | flops 8589934592 | bytes 20971520 | tf_op jit(solution)/shard_map/tf,df->td/dot_general | solution.py:124
  551.7 14.7 %bitcast_reduce_fusion = (f32[2048]{0:T(1024)}, f32[1024]{0:T(1024)S(1)}, f32[1024]{0:T(1024)S(1)}, f32[2048]{0:T(1024)}, f32[1024,2048,1]{1,0,2:T(8,128)}) fusion(f32[2048]{0:T(1024)S(1)} %copy-done.40, f32[1024]{0:T(1024)S(1)} %broadcast_multiply_fusion.1, bf16[1024,2048]{1,0:T(8,128)(2,1)S(1)} %copy-done.3, f32[1024,2048]{1,0:T(8,128)} %fusion.263, ...), kind=kOutput, calls=%fused_computation.19 | convolution fusion | flops 6466562048 | bytes 30453760 | tf_op jit(solution)/shard_map/tcf,dcf->td/dot_general | solution.py:173
  566.5 11.0 multiply_reduce_fusion
  577.5 6.8 add_add_fusion.2
  585.5 3.7 fusion.155
  591.6 4.4 fusion.249
  596.1 14.8 %fusion.242 = f32[2048,3,512]{2,0,1:T(8,128)} fusion(bf16[1024,1,512]{2,0,1:T(8,128)(2,1)S(1)} %copy-done.24, bf16[1024,1,512]{2,0,1:T(8,128)(2,1)S(1)} %copy-done.22, bf16[1024,1,512]{2,0,1:T(8,128)(2,1)S(1)} %copy-done.21, f32[1024,2048]{1,0:T(8,128)} %convert_element_type.249, f32[1024]{0:T(1024)S(1)} %add_rsqrt_fusion, ...), kind=kOutput, calls=%fused_computation.345 | convolution fusion | flops 6462373888 | bytes 24141824 | tf_op jit(solution)/shard_map/td,tcf->dcf/dot_general | solution.py:172
  611.6 16.3 %fusion.253 = f32[2048,2048]{1,0:T(8,128)} fusion(bf16[1024,2048]{1,0:T(8,128)(2,1)} %get-tuple-element.83, f32[1024,2048]{1,0:T(8,128)} %convert_element_type.249, f32[1024]{0:T(1024)S(1)} %add_rsqrt_fusion, f32[1024]{0:T(1024)S(1)} %broadcast_multiply_fusion, f32[2048]{0:T(1024)S(1)} %copy-done.56, f32[2048]{0:T(1024)S(1)} %copy-done.41), kind=kOutput, calls=%fused_computation.350 | convolution fusion | flops 8600420352 | bytes 29384704 | tf_op jit(solution)/shard_map/td,tf->df/dot_general | solution.py:123
  628.0 34.2 %fusion.31 = f32[2048,2048]{1,0:T(8,128)} fusion(f32[1024,2048]{1,0:T(8,128)} %fusion.254, f32[2048]{0:T(1024)S(1)} %copy-done.57, bf16[1024,2048]{1,0:T(8,128)(2,1)} %param.29, f32[1024]{0:T(1024)S(1)} %copy-done.44), kind=kOutput, calls=%fused_computation.72 | convolution fusion | flops 8734638080 | bytes 29372416 | tf_op jit(solution)/shard_map/tf,td->fd/dot_general | solution.py:119
  663.0 19.3 %all-reduce.7 = (f32[2048]{0:T(1024)S(1)}, f32[2048]{0:T(1024)S(1)}, f32[2048]{0:T(1024)S(1)}, f32[2048]{0:T(1024)S(1)}) all-reduce(f32[2048]{0:T(1024)S(1)} %copy-done.43, f32[2048]{0:T(1024)S(1)} %copy-done.49, f32[2048]{0:T(1024)S(1)} %copy-done.42, f32[2048]{0:T(1024)S(1)} %copy-done.50), channel_id=1, replica_groups=mesh['dp'=8,'tensor'=4] {'tensor'}, use_global_device_ids=true, to_apply=%region_21.22 | all-reduce | flops 8192 | bytes 65536 | tf_op jit(solution)/shard_map/psum | solution.py:184
  684.5 190.9 %all-reduce.13.cloned.1.call-done = f32[1024,2048]{1,0:T(8,128)} async-done(((f32[1024,2048]{1,0:T(8,128)}), f32[1024,2048]{1,0:T(8,128)}) %all-reduce.13.cloned.1.call-update) | async-done | bytes 8388624 | tf_op jit(solution)/shard_map/psum | solution.py:184
  875.4 6.8 fusion.21
  882.2 25.4 %all-reduce.6 = (f32[2048]{0:T(1024)}, f32[2048]{0:T(1024)}, f32[3,512]{1,0:T(4,128)}, f32[2048]{0:T(1024)S(1)}, f32[2048]{0:T(1024)}, /*index=5*/f32[2048]{0:T(1024)}, f32[2048]{0:T(1024)}) all-reduce(f32[2048]{0:T(1024)S(1)} %get-tuple-element.33, f32[2048]{0:T(1024)S(1)} %get-tuple-element.34, ...), channel_id=1, replica_groups=mesh['dp'=8,'tensor'=4] {'dp'}, use_global_device_ids=true, to_apply=%region_22.23 | all-reduce | flops 13824 | bytes 110592 | tf_op jit(solution)/shard_map/psum | solution.py:188
  907.6 22.1 %reduce-scatter.7.cloned.1.call-done = f32[512,256]{1,0:T(8,128)} async-done(((f32[512,2048]{1,0:T(8,128)}), f32[512,256]{1,0:T(8,128)}) %reduce-scatter.7.cloned.1.call-update) | async-done | bytes 524304 | tf_op jit(solution)/shard_map/reduce_scatter | solution.py:176
  929.8 96.8 %reduce-scatter.5.cloned.1.call-done = f32[256,3,512]{2,0,1:T(8,128)} async-done(((f32[2048,3,512]{2,0,1:T(8,128)}), f32[256,3,512]{2,0,1:T(8,128)}) %reduce-scatter.5.cloned.1.call-update) | async-done | bytes 1572880 | tf_op jit(solution)/shard_map/reduce_scatter | solution.py:175
  1026.5 120.4 %reduce-scatter.9.cloned.1.call-done = f32[256,2048]{1,0:T(8,128)} async-done(((f32[2048,2048]{1,0:T(8,128)}), f32[256,2048]{1,0:T(8,128)}) %reduce-scatter.9.cloned.1.call-update) | async-done | bytes 2097168 | tf_op jit(solution)/shard_map/reduce_scatter | solution.py:177
  1146.9 120.4 %reduce-scatter.11.cloned.1.call-done = f32[2048,256]{1,0:T(8,128)} async-done(((f32[2048,2048]{1,0:T(8,128)}), f32[2048,256]{1,0:T(8,128)}) %reduce-scatter.11.cloned.1.call-update) | async-done | bytes 2097168 | tf_op jit(solution)/shard_map/reduce_scatter | solution.py:178
  (212 shorter events, 100.9 us)
Async XLA Ops:
  7.2 49.0 %copy-start = (bf16[512,2048]{1,0:T(8,128)(2,1)S(1)}, bf16[512,2048]{1,0:T(8,128)(2,1)}, u32[]{:S(2)}) copy-start(bf16[512,2048]{1,0:T(8,128)(2,1)} %param.21) | copy-start | bytes 6291460
  7.2 399.9 %all-reduce.11.cloned.1.call-start = ((), (), s32[]{:S(2)}) async-start(), calls=%async_computation.4 | async-start | bytes 16777216 | tf_op jit(solution)/shard_map/psum | solution.py:112
  14.4 47.5 %copy-start.37 = (f32[1024]{0:T(1024)}, f32[1024]{0:T(1024)S(1)}, u32[]{:S(2)}) copy-start(f32[1024]{0:T(1024)S(1)} %fusion.176) | copy-start | bytes 12292
  113.5 761.9 %all-reduce.13.cloned.1.call-start = ((), (), s32[]{:S(2)}) async-start(), calls=%async_computation.5 | async-start | bytes 16777216 | tf_op jit(solution)/shard_map/psum | solution.py:184
  120.2 287.0 %copy-start.45 = (f32[2048]{0:T(1024)S(1)}, f32[2048]{0:T(1024)}, u32[]{:S(2)}) copy-start(f32[2048]{0:T(1024)} %param.28) | copy-start | bytes 24580
  120.2 287.0 %copy-start.46 = (f32[2048]{0:T(1024)S(1)}, f32[2048]{0:T(1024)}, u32[]{:S(2)}) copy-start(f32[2048]{0:T(1024)} %param.22) | copy-start | bytes 24580
  419.4 20.8 %slice-start = ((s8[8388608]{0:T(1024)(128)(4,1)}), s8[4194304]{0:T(1024)(128)(4,1)S(1)}, s32[]{:S(2)}) async-start(s8[8388608]{0:T(1024)(128)(4,1)} %bitcast.155), calls=%async_computation.10 | async-start | bytes 8388608
  419.4 20.8 %slice-start.4 = ((s8[6291456]{0:T(1024)(128)(4,1)}), s8[4194304]{0:T(1024)(128)(4,1)S(1)}, s32[]{:S(2)}) async-start(s8[6291456]{0:T(1024)(128)(4,1)} %bitcast.181), calls=%async_computation.14 | async-start | bytes 8388608
  423.9 16.3 %slice-start.1 = ((s8[8388608]{0:T(1024)(128)(4,1)}), s8[4194304]{0:T(1024)(128)(4,1)S(1)}, s32[]{:S(2)}) async-start(s8[8388608]{0:T(1024)(128)(4,1)} %bitcast.155), calls=%async_computation.11 | async-start | bytes 8388608
  423.9 16.3 %copy-start.40 = (f32[2048]{0:T(1024)S(1)}, f32[2048]{0:T(1024)}, u32[]{:S(2)}) copy-start(f32[2048]{0:T(1024)} %param.17) | copy-start | bytes 24580
  423.9 16.3 %slice-start.5 = ((s8[6291456]{0:T(1024)(128)(4,1)}), s8[2097152]{0:T(1024)(128)(4,1)S(1)}, s32[]{:S(2)}) async-start(s8[6291456]{0:T(1024)(128)(4,1)} %bitcast.181), calls=%async_computation.15 | async-start | bytes 4194304
  423.9 16.3 %copy-start.52 = (f32[3,512]{1,0:T(4,128)S(1)}, f32[3,512]{1,0:T(4,128)}, u32[]{:S(2)}) copy-start(f32[3,512]{1,0:T(4,128)} %param.20) | copy-start | bytes 18436
  423.9 16.3 %copy-start.54 = (f32[2048]{0:T(1024)S(1)}, f32[2048]{0:T(1024)}, u32[]{:S(2)}) copy-start(f32[2048]{0:T(1024)} %param.18) | copy-start | bytes 24580
  450.4 11.8 copy-start.13
  450.4 11.9 copy-start.16
  464.6 8.0 copy-start.32
  514.9 16.2 %copy-start.20 = (bf16[1024,512]{0,1:T(8,128)(2,1)S(1)}, bf16[1024,512]{0,1:T(8,128)(2,1)}, u32[]{:S(2)}) copy-start(bf16[1024,512]{0,1:T(8,128)(2,1)} %convolution_convert_fusion) | copy-start | bytes 3145732
  536.6 15.1 %copy-start.23 = (bf16[1024,1,512]{2,0,1:T(8,128)(2,1)}, bf16[1024,1,512]{2,0,1:T(8,128)(2,1)S(1)}, u32[]{:S(2)}) copy-start(bf16[1024,1,512]{2,0,1:T(8,128)(2,1)S(1)} %copy.75) | copy-start | bytes 3145732
  536.6 15.1 %copy-start.3 = (bf16[1024,2048]{1,0:T(8,128)(2,1)S(1)}, bf16[1024,2048]{1,0:T(8,128)(2,1)}, u32[]{:S(2)}) copy-start(bf16[1024,2048]{1,0:T(8,128)(2,1)} %param.15) | copy-start | bytes 12582916
  536.6 15.1 %copy-start.21 = (bf16[1024,1,512]{2,0,1:T(8,128)(2,1)S(1)}, bf16[1024,1,512]{2,0,1:T(8,128)(2,1)}, u32[]{:S(2)}) copy-start(bf16[1024,1,512]{2,0,1:T(8,128)(2,1)} %copy.73) | copy-start | bytes 3145732
  536.6 15.1 %copy-start.22 = (bf16[1024,1,512]{2,0,1:T(8,128)(2,1)S(1)}, bf16[1024,1,512]{2,0,1:T(8,128)(2,1)}, u32[]{:S(2)}) copy-start(bf16[1024,1,512]{2,0,1:T(8,128)(2,1)} %copy.74) | copy-start | bytes 3145732
  551.7 14.8 %copy-start.36 = (f32[1024]{0:T(1024)S(1)}, f32[1024]{0:T(1024)}, u32[]{:S(2)}) copy-start(f32[1024]{0:T(1024)} %copy-done.35) | copy-start | bytes 12292
  551.7 14.8 %copy-start.38 = (f32[1024]{0:T(1024)S(1)}, f32[1024]{0:T(1024)}, u32[]{:S(2)}) copy-start(f32[1024]{0:T(1024)} %copy-done.37) | copy-start | bytes 12292
  566.5 11.0 copy-start.7
  566.5 11.0 copy-start.8
  584.3 345.4 %reduce-scatter.7.cloned.1.call-start = ((), (), s32[]{:S(2)}) async-start(), calls=%async_computation.7 | async-start | bytes 4718592 | tf_op jit(solution)/shard_map/reduce_scatter | solution.py:176
  596.0 430.5 %reduce-scatter.5.cloned.1.call-start = ((), (), s32[]{:S(2)}) async-start(), calls=%async_computation.6 | async-start | bytes 14155776 | tf_op jit(solution)/shard_map/reduce_scatter | solution.py:175
  610.9 536.0 %reduce-scatter.9.cloned.1.call-start = ((), (), s32[]{:S(2)}) async-start(), calls=%async_computation.8 | async-start | bytes 18874368 | tf_op jit(solution)/shard_map/reduce_scatter | solution.py:177
  628.0 639.4 %reduce-scatter.11.cloned.1.call-start = ((), (), s32[]{:S(2)}) async-start(), calls=%async_computation.9 | async-start | bytes 18874368 | tf_op jit(solution)/shard_map/reduce_scatter | solution.py:178
  682.3 585.7 %copy-start.1 = (bf16[512,2048]{1,0:T(8,128)(2,1)S(1)}, bf16[512,2048]{1,0:T(8,128)(2,1)}, u32[]{:S(2)}) copy-start(bf16[512,2048]{1,0:T(8,128)(2,1)} %param.21) | copy-start | bytes 6291460
  684.4 197.8 %copy-start.47 = (f32[2048]{0:T(1024)S(1)}, f32[2048]{0:T(1024)}, u32[]{:S(2)}) copy-start(f32[2048]{0:T(1024)} %get-tuple-element.82) | copy-start | bytes 24580
  907.6 360.3 %copy-start.48 = (f32[2048]{0:T(1024)}, f32[2048]{0:T(1024)S(1)}, u32[]{:S(2)}) copy-start(f32[2048]{0:T(1024)S(1)} %get-tuple-element.113) | copy-start | bytes 24580
  (38 other events, 154.7 us)
Sparse Core Ops, SparseCore 0:
  113.6 293.5 all-reduce.10
  584.5 290.8 all-reduce.12
  879.3 50.3 reduce-scatter.6
  934.1 92.3 reduce-scatter.4
  1030.9 115.9 reduce-scatter.8
  1151.3 115.9 reduce-scatter.10
where the time goes:
time: 1280 us
  waiting for transfers between devices  834 us (65%)
  matrix products  242 us (19%)
  other arithmetic  88.2 us (7%)
  local copies, waits for them, and re-layouts  48.9 us (4%)
  blocking collectives  44.7 us (3%)
  between operations  16.5 us (1%)
    psum x1, waiting for transfers between devices, local(): total_branch = lax.psum(part, 'tensor')  284 us
    psum x1, waiting for transfers between devices, local(): lax.psum((dx_one + dx_two, gain_one, shift_one, gain_two, shift_two), 'te...  191 us
    reduce_scatter x1, waiting for transfers between devices, local(): lax.psum_scatter(w_out_grad, 'dp', scatter_dimension=1, tiled=True)  120 us
    reduce_scatter x1, waiting for transfers between devices, local(): lax.psum_scatter(w_in_grad, 'dp', scatter_dimension=0, tiled=True)  120 us
    reduce_scatter x1, waiting for transfers between devices, local(): lax.psum_scatter(w_qkv_grad, 'dp', scatter_dimension=0, tiled=True)  96.8 us
    dot_general x1, matrix products, local(): jnp.dot(hidden, w_out, preferred_element_type=jnp.float32)  51.6 us
    dot_general x1, matrix products, local(): jnp.einsum('tf,td->fd', hidden, cotan_low, preferred_element_type=jnp.flo...  34.2 us
  transfers between devices with their start and end apart: 6, of which 6 were waited for; matrix products, arithmetic and copies ran while one was open for 7% of the time, Pallas kernels for 0%

commit v1 on v0

v1 whole, which is shorter than its diff:
```python
import math

import jax
import jax.numpy as jnp
import numpy as np
from jax import lax
from jax.experimental import pallas as pl
from jax.experimental.pallas import tpu as pltpu
from jax.sharding import PartitionSpec as P

HD = 256
ROT = 64
EPS = 1e-05
F32 = jnp.float32
BF16 = jnp.bfloat16
VMEM_LIMIT = 48 * 1024 * 1024
FULL_LIMIT = 56 * 1024 * 1024
SMALL_LIMIT = 8 * 1024 * 1024
NT = (((1,), (1,)), ((), ()))
TN = (((0,), (0,)), ((), ()))


def dot(a, b, dims=(((1,), (0,)), ((), ()))):
    return lax.dot_general(a, b, dims, preferred_element_type=F32)


def params():
    return pltpu.CompilerParams(vmem_limit_bytes=VMEM_LIMIT)


def cost(flops, nbytes, long=False):
    return pl.CostEstimate(flops=int(3e11 if long else 4e10), bytes_accessed=int(nbytes), transcendentals=0)


def light(flops, nbytes):
    return pl.CostEstimate(flops=int(flops), bytes_accessed=int(nbytes), transcendentals=0)


ANY = pl.BlockSpec(memory_space=pl.ANY)
HBM = pl.BlockSpec(memory_space=pltpu.HBM)
VMEM = pl.BlockSpec(memory_space=pltpu.VMEM)
SMEM = pl.BlockSpec(memory_space=pltpu.SMEM)


def shape(dims, dtype):
    return jax.ShapeDtypeStruct(dims, dtype)


TOKEN = shape((8, 128), F32)


def turned(values, cosine, lower, upper):
    head = values[:, :128]
    head = (
        head * cosine
        + pltpu.roll(head, 128 - ROT // 2, 1) * lower
        + pltpu.roll(head, ROT // 2, 1) * upper
    )
    return jnp.concatenate([head, values[:, 128:]], 1)


class Stream:
    def __init__(self, pieces, sems, window=4):
        self.copies = [pltpu.make_async_copy(a, b, sems.at[i]) for i, (a, b) in enumerate(pieces)]
        self.window = window
        self.done = 0
        for copy in self.copies[:window]:
            copy.start()

    def next(self):
        self.copies[self.done].wait()
        ahead = self.done + self.window
        if ahead < len(self.copies):
            self.copies[ahead].start()
        self.done += 1


def forward_rows(start, size, unit, x, lengths, flag, gains, w_three, b_three, w_in, b_in, b_after, w_dense, w_out, tables, held, after):
    rows, width = x.shape
    columns, units = w_dense.shape[0], w_in.shape[1]
    heads = columns // HD
    at = start // size
    piece = min(512, units)
    wide = min(512, width)
    scale = 1.0 / math.sqrt(HD)
    past = start > 0
    steps = 3 + units // piece + 1 + width // wide

    def body(*refs):
        len_ref, flag_ref, x_ref, g1, s1, g2, s2, b3_ref, bi_ref, ba_ref, c_ref, l_ref, u_ref = refs[:13]
        w3_hbm, wi_hbm, wd_hbm, wo_hbm = refs[13:17]
        one_ref, two_ref, qkv_ref, o_ref, hidden_ref, slope_ref, *part_refs, token_ref = refs[-14 - size // unit : -7]
        token_ref[...] = jnp.zeros_like(token_ref)
        w3, wi, wd, wo, kv_ref, sems, kv_sem = refs[-7:]
        if past:
            earlier = pltpu.make_async_copy(refs[19].at[pl.ds(1, 2), pl.ds(0, start)], kv_ref, kv_sem)
            earlier.start()
        pieces = [(w3_hbm.at[c], w3.at[c]) for c in range(3)]
        for low in range(0, units, piece):
            here = pl.ds(low, piece)
            pieces.append((wi_hbm.at[:, here], wi.at[:, here]))
        pieces.append((wd_hbm, wd))
        for low in range(0, width, wide):
            here = pl.ds(low, wide)
            pieces.append((wo_hbm.at[:, here], wo.at[:, here]))
        stream = Stream(pieces, sems)
        length = len_ref[0]

        values = x_ref[...].astype(F32)
        center = values - jnp.mean(values, -1, keepdims=True)
        spread = jnp.mean(center * center, -1, keepdims=True)
        normed = center * lax.rsqrt(spread + EPS)
        one_ref[...] = (normed * g1[...] + s1[...]).astype(BF16)
        two_ref[...] = (normed * g2[...] + s2[...]).astype(BF16)

        for c in range(3):
            stream.next()
            acc = dot(one_ref[...], w3[c]) + b3_ref[c]
            for h in range(heads):
                cols = slice(h * HD, (h + 1) * HD)
                one_head = acc[:, cols]
                if c < 2:
                    one_head = turned(one_head, c_ref[...], l_ref[...], u_ref[...])
                qkv_ref[c, :, cols] = one_head.astype(BF16)

        here = lax.broadcasted_iota(jnp.int32, (size, size), 0)
        there = lax.broadcasted_iota(jnp.int32, (size, size), 1)
        seen = (there <= here) & (there + start < length)
        if past:
            inside = lax.broadcasted_iota(jnp.int32, (size, start), 1) < length
            earlier.wait()
        for h in range(heads):
            cols = slice(h * HD, (h + 1) * HD)
            query = qkv_ref[0, :, cols]
            now = jnp.where(seen, dot(query, qkv_ref[1, :, cols], NT) * scale, -1e30)
            top = jnp.max(now, -1, keepdims=True)
            if past:
                old = jnp.where(inside, dot(query, kv_ref[0, :, cols], NT) * scale, -1e30)
                top = jnp.maximum(top, jnp.max(old, -1, keepdims=True))
                old = jnp.exp(old - top)
            now = jnp.exp(now - top)
            total = jnp.sum(now, -1, keepdims=True)
            if past:
                total = total + jnp.sum(old, -1, keepdims=True)
            share = 1.0 / total
            mixed = dot((now * share).astype(BF16), qkv_ref[2, :, cols])
            if past:
                mixed = mixed + dot((old * share).astype(BF16), kv_ref[1, :, cols])
            o_ref[:, cols] = mixed.astype(BF16)

        for low in range(0, units, piece):
            cols = slice(low, low + piece)
            stream.next()
            pre = dot(two_ref[...], wi[:, cols]) + bi_ref[:, cols]
            share = 0.5 + 0.5 * lax.erf(pre * (1.0 / math.sqrt(2.0)))
            hidden_ref[:, cols] = (pre * share).astype(BF16)
            bell = jnp.exp(-0.5 * pre * pre) * (1.0 / math.sqrt(2.0 * math.pi))
            slope_ref[:, cols] = (share + pre * bell).astype(BF16)

        stream.next()
        own = flag_ref[1].astype(F32)
        for low in range(0, width, wide):
            cols = slice(low, low + wide)
            stream.next()
            acc = dot(o_ref[...], wd[:, cols]) + dot(hidden_ref[...], wo[:, cols])
            acc = acc + own * (x_ref[:, cols].astype(F32) + ba_ref[:, cols])
            for i, part_ref in enumerate(part_refs):
                part_ref[:, cols] = acc[i * unit : (i + 1) * unit]

    vec = lambda n: pl.BlockSpec((1, n), lambda i: (0, 0))
    table = pl.BlockSpec((size, 128), lambda i: (at, 0))
    block = lambda n: pl.BlockSpec((size, n), lambda i: (at, 0))
    operands = [lengths, flag, x, *gains, b_three, b_in, b_after, *tables, w_three, w_in, w_dense, w_out]
    specs = [SMEM, SMEM, block(width)] + [vec(width)] * 4
    specs += [pl.BlockSpec((3, 1, columns), lambda i: (0, 0, 0)), vec(units), vec(width)] + [table] * 3 + [HBM] * 4
    aliases = {}
    if past:
        aliases = {len(operands) + i: i for i in range(6)}
        operands += list(held)
        specs += [HBM] * 6
    operands += list(after)
    specs += [ANY] * len(after)
    flops = 2 * size * width * (4 * columns + 2 * units)
    return pl.pallas_call(
        body,
        grid=(1,),
        in_specs=specs,
        out_specs=[
            block(width),
            block(width),
            pl.BlockSpec((3, size, columns), lambda i: (0, at, 0)),
            block(columns),
            block(units),
            block(units),
        ]
        + [pl.BlockSpec((unit, width), lambda i: (0, 0))] * (size // unit)
        + [pl.BlockSpec(TOKEN.shape, lambda i: (0, 0))],
        out_shape=[
            shape((rows, width), BF16),
            shape((rows, width), BF16),
            shape((3, rows, columns), BF16),
            shape((rows, columns), BF16),
            shape((rows, units), BF16),
            shape((rows, units), BF16),
        ]
        + [shape((unit, width), F32)] * (size // unit)
        + [TOKEN],
        scratch_shapes=[
            pltpu.VMEM(w_three.shape, BF16),
            pltpu.VMEM(w_in.shape, BF16),
            pltpu.VMEM(w_dense.shape, BF16),
            pltpu.VMEM(w_out.shape, BF16),
            pltpu.VMEM((2, max(start, 16), columns), BF16),
            pltpu.SemaphoreType.DMA((steps,)),
            pltpu.SemaphoreType.DMA,
        ],
        input_output_aliases=aliases,
        compiler_params=params(),
        cost_estimate=cost(flops, 2 * width * (4 * columns + 2 * units) + size * width * 20),
        name="forward_rows",
    )(*operands)


def mask_rows(lengths, grad_out, after):
    rows, width = grad_out.shape
    step = 256

    def body(*refs):
        len_ref, g_ref = refs[:2]
        out_ref, sum_ref = refs[-2:]
        i = pl.program_id(0)
        here = lax.broadcasted_iota(jnp.int32, (step, 1), 0) + i * step
        valid = (here < len_ref[0]).astype(F32)
        kept = g_ref[...].astype(F32) * valid
        out_ref[...] = kept.astype(BF16)

        @pl.when(i == 0)
        def _():
            sum_ref[...] = jnp.zeros_like(sum_ref)

        sum_ref[...] += jnp.sum(kept, 0, keepdims=True)

    row = pl.BlockSpec((step, width), lambda i: (i, 0))
    return pl.pallas_call(
        body,
        grid=(rows // step,),
        in_specs=[SMEM, row] + [ANY] * len(after),
        out_specs=[row, pl.BlockSpec((1, width), lambda i: (0, 0))],
        out_shape=[shape((rows, width), BF16), shape((1, width), F32)],
        compiler_params=params(),
        cost_estimate=cost(2 * rows * width, 4 * rows * width),
        name="mask_rows",
    )(lengths, grad_out, *after)


def pair_product(lefts, right, slide_left, parity, added, blocks, after, name):
    rows = right.shape[-2]
    many = right.shape[0]
    left_width = sum(left.shape[1] for left in lefts)
    block = (left_width if slide_left else right.shape[2]) // (2 * blocks)
    tall, wide = (block, right.shape[2]) if slide_left else (left_width, block)

    def body(_, *refs):
        right_ref = refs[len(lefts)]
        out_ref, token_ref = refs[-2:]
        token_ref[...] = jnp.zeros_like(token_ref)
        for c in range(many):
            low = 0
            for left_ref in refs[: len(lefts)]:
                here = slice(low, low + left_ref.shape[1])
                low += left_ref.shape[1]
                acc = dot(left_ref[...], right_ref[c], TN)
                if added is not None:
                    acc = acc + refs[len(lefts) + 1][0, c, here]
                out_ref[0, c, here] = acc

    out = pl.BlockSpec((1, many, tall, wide), lambda i, p: (i, 0, 0, 0))
    if slide_left:
        specs = [pl.BlockSpec((rows, block), lambda i, p: (0, 2 * i + p[0]))]
        specs.append(pl.BlockSpec(right.shape, lambda i, p: (0, 0, 0)))
    else:
        specs = [pl.BlockSpec(left.shape, lambda i, p: (0, 0)) for left in lefts]
        specs.append(pl.BlockSpec((many, rows, block), lambda i, p: (0, 0, 2 * i + p[0])))
    operands = [*lefts, right]
    if added is not None:
        operands.append(added)
        specs.append(out)
    return pl.pallas_call(
        body,
        grid_spec=pltpu.PrefetchScalarGridSpec(
            num_scalar_prefetch=1,
            grid=(blocks,),
            in_specs=specs + [ANY] * len(after),
            out_specs=[out, pl.BlockSpec(TOKEN.shape, lambda i, p: (0, 0))],
        ),
        out_shape=[shape((blocks, many, tall, wide), F32), TOKEN],
        compiler_params=params(),
        cost_estimate=cost(2 * rows * blocks * many * tall * wide, 2 * rows * (left_width + many * right.shape[2]) + 4 * blocks * many * tall * wide),
        name=name,
    )(parity, *operands, *after)


def attend_back(lengths, qkv, cotan, w_dense, tables, after):
    rows, columns = qkv.shape[1:]
    width = cotan.shape[1]
    sub = min(256, rows)
    scale = 1.0 / math.sqrt(HD)

    def body(len_ref, q_ref, k_ref, v_ref, g_ref, w_ref, c_ref, l_ref, u_ref, *refs):
        out_ref, bias_ref, dk_ref, dv_ref = refs[-4:]
        length = len_ref[0]
        for low in range(0, rows, sub):
            stop = low + sub
            here = slice(low, stop)
            query, keys, values = q_ref[0, here], k_ref[0, :stop], v_ref[0, :stop]
            scores = dot(query, keys, NT) * scale
            mine = lax.broadcasted_iota(jnp.int32, scores.shape, 0) + low
            there = lax.broadcasted_iota(jnp.int32, scores.shape, 1)
            scores = jnp.where((there <= mine) & (there < length), scores, -1e30)
            expo = jnp.exp(scores - jnp.max(scores, -1, keepdims=True))
            probs = expo * (1.0 / jnp.sum(expo, -1, keepdims=True))
            dmixed = dot(g_ref[here], w_ref[...], NT).astype(BF16)
            dprobs = dot(dmixed, values, NT)
            delta = jnp.sum(probs * dprobs, -1, keepdims=True)
            dscores = (probs * (dprobs - delta)).astype(BF16)
            out_ref[0, here] = turned(
                dot(dscores, keys) * scale, c_ref[here], -l_ref[here], -u_ref[here]
            ).astype(BF16)
            dkey = dot(dscores, query, TN) * scale
            dvalue = dot(probs.astype(BF16), dmixed, TN)
            if low:
                dk_ref[:low] += dkey[:low]
                dv_ref[:low] += dvalue[:low]
            dk_ref[here] = dkey[low:]
            dv_ref[here] = dvalue[low:]
        out_ref[1] = turned(dk_ref[...], c_ref[...], -l_ref[...], -u_ref[...]).astype(BF16)
        out_ref[2] = dv_ref[...].astype(BF16)
        for part in range(3):
            bias_ref[part] = jnp.sum(out_ref[part].astype(F32), 0, keepdims=True)

    part = lambda c: pl.BlockSpec((1, rows, HD), lambda h: (c, 0, h))
    table = pl.BlockSpec((rows, 128), lambda h: (0, 0))
    return pl.pallas_call(
        body,
        grid=(columns // HD,),
        in_specs=[
            SMEM,
            part(0),
            part(1),
            part(2),
            pl.BlockSpec((rows, width), lambda h: (0, 0)),
            pl.BlockSpec((HD, width), lambda h: (h, 0)),
            table,
            table,
            table,
        ]
        + [ANY] * len(after),
        out_specs=[
            pl.BlockSpec((3, rows, HD), lambda h: (0, 0, h)),
            pl.BlockSpec((3, 1, HD), lambda h: (0, 0, h)),
        ],
        out_shape=[shape((3, rows, columns), BF16), shape((3, 1, columns), F32)],
        scratch_shapes=[pltpu.VMEM((rows, HD), F32)] * 2,
        compiler_params=params(),
        cost_estimate=cost(
            2 * rows * columns * width + 10 * rows * rows * columns,
            2 * rows * (width + 7 * columns),
            True,
        ),
        name="attend_back",
    )(lengths, qkv, qkv, qkv, cotan, w_dense, *tables, *after)


def backward_rows(start, size, unit, x, flag, cotan, slope, dqkv, w_three, w_in, w_out, gains, held, after):
    rows, width = x.shape
    columns, units = dqkv.shape[2], slope.shape[1]
    at = start // size
    piece = min(512, units)
    wide = min(512, width)
    steps = units // piece + width // wide

    def body(*refs):
        x_ref, flag_ref, g_ref, slope_ref, q_ref, g1, g2, w3_hbm, wi_hbm, wo_hbm = refs[:10]
        dh_ref, small_ref, bias_ref, *dx_refs = refs[-10 - size // unit : -7]
        w3, wi, wo, one, two, sems, sems3 = refs[-7:]
        pieces = []
        for low in range(0, units, piece):
            here = pl.ds(low, piece)
            pieces.append((wo_hbm.at[here], wo.at[here]))
        for low in range(0, width, wide):
            here = pl.ds(low, wide)
            pieces.append((wi_hbm.at[here], wi.at[here]))
        stream = Stream(pieces, sems)
        three = pltpu.make_async_copy(w3_hbm, w3, sems3)
        for low in range(0, units, piece):
            here = slice(low, low + piece)
            stream.next()
            if low == 0:
                three.start()
            grad = (dot(g_ref[...], wo[here], NT) * slope_ref[:, here].astype(F32)).astype(BF16)
            dh_ref[:, here] = grad
            bias_ref[:, here] = jnp.sum(grad.astype(F32), 0, keepdims=True)
        three.wait()
        for low in range(0, width, wide):
            here = slice(low, low + wide)
            acc = dot(q_ref[0], w3[0, here], NT)
            for c in (1, 2):
                acc = acc + dot(q_ref[c], w3[c, here], NT)
            one[:, here] = acc
            stream.next()
            two[:, here] = dot(dh_ref[...], wi[here], NT)
        gain_one, gain_two = g1[...], g2[...]
        own = flag_ref[1].astype(F32)
        sums = [jnp.zeros((1, width), F32)] * 4
        band = 64
        for low in range(0, size, band):
            here = slice(low, low + band)
            values = x_ref[here].astype(F32)
            center = values - jnp.mean(values, -1, keepdims=True)
            rstd = lax.rsqrt(jnp.mean(center * center, -1, keepdims=True) + EPS)
            normed = center * rstd
            d_one, d_two = one[here], two[here]
            grad = d_one * gain_one + d_two * gain_two
            dx_refs[low // unit][low % unit : low % unit + band] = rstd * (
                grad
                - jnp.mean(grad, -1, keepdims=True)
                - normed * jnp.mean(grad * normed, -1, keepdims=True)
            ) + own * g_ref[here].astype(F32)
            terms = (d_one * normed, d_one, d_two * normed, d_two)
            sums = [s + jnp.sum(t, 0, keepdims=True) for s, t in zip(sums, terms)]
        small_ref[...] = jnp.concatenate(sums + [jnp.zeros((4, width), F32)], 0)

    vec = lambda n: pl.BlockSpec((1, n), lambda i: (0, 0))
    block = lambda n: pl.BlockSpec((size, n), lambda i: (at, 0))
    operands = [x, flag, cotan, slope, dqkv, gains[0], gains[2], w_three, w_in, w_out]
    specs = [block(width), SMEM, block(width), block(units), pl.BlockSpec((3, size, columns), lambda i: (0, at, 0))]
    specs += [vec(width), vec(width)] + [HBM] * 3
    aliases = {}
    if held is not None:
        aliases = {len(operands): 0}
        operands.append(held)
        specs.append(HBM)
    operands += list(after)
    specs += [ANY] * len(after)
    return pl.pallas_call(
        body,
        grid=(1,),
        in_specs=specs,
        out_specs=[
            block(units),
            pl.BlockSpec((8, width), lambda i: (0, 0)),
            vec(units),
        ]
        + [pl.BlockSpec((unit, width), lambda i: (0, 0))] * (size // unit),
        out_shape=[
            shape((rows, units), BF16),
            shape((8, width), F32),
            shape((1, units), F32),
        ]
        + [shape((unit, width), F32)] * (size // unit),
        scratch_shapes=[
            pltpu.VMEM(w_three.shape, BF16),
            pltpu.VMEM(w_in.shape, BF16),
            pltpu.VMEM(w_out.shape, BF16),
            pltpu.VMEM((size, width), F32),
            pltpu.VMEM((size, width), F32),
            pltpu.SemaphoreType.DMA((steps,)),
            pltpu.SemaphoreType.DMA,
        ],
        input_output_aliases=aliases,
        compiler_params=params(),
        cost_estimate=cost(2 * size * width * (2 * units + 3 * columns), 2 * width * (2 * units + 3 * columns) + 16 * size * width, start == 0),
        name="backward_rows",
    )(*operands)


def take_in(flag, unit, came, operand, out, out_at, out_shape, after):
    rows, width = came.shape
    has_unit, has_total = unit is not None, operand is not None

    def body(*refs):
        flag_ref, came_ref = refs[:2]
        if has_total:
            out_ref, rounded, sem = refs[-3:]
            rounded[...] = jnp.where(flag_ref[0] == 1, refs[2 + has_unit][...], came_ref[...]).astype(BF16)
            copy = pltpu.make_async_copy(rounded, out_ref.at[pl.ds(out_at * rows, rows)], sem)
            copy.start()
        if has_unit:
            refs[-4 if has_total else -1][...] = refs[2][...] + came_ref[...]
        if has_total:
            copy.wait()

    operands, specs = [flag, came], [SMEM, VMEM]
    outs, out_specs, aliases, scratch = [], [], {}, []
    if has_unit:
        operands.append(unit)
        specs.append(VMEM)
        outs.append(shape((rows, width), F32))
        out_specs.append(VMEM)
    if has_total:
        operands.append(operand)
        specs.append(VMEM)
        outs.append(shape(out_shape, BF16))
        out_specs.append(HBM)
        scratch = [pltpu.VMEM((rows, width), BF16), pltpu.SemaphoreType.DMA]
        if out is not None:
            aliases = {len(operands): len(outs) - 1}
            operands.append(out)
            specs.append(HBM)
    operands += after
    specs += [ANY] * len(after)
    result = pl.pallas_call(
        body,
        in_specs=specs,
        out_specs=out_specs,
        out_shape=outs,
        scratch_shapes=scratch,
        input_output_aliases=aliases,
        compiler_params=pltpu.CompilerParams(vmem_limit_bytes=SMALL_LIMIT),
        cost_estimate=light(4 * rows * width, 16 * rows * width),
        name="take_in",
    )(*operands)
    held = result[0] if has_unit else None
    return held, (result[-1] if has_total else out)


def pass_on(flag, held, met, unit, after, carried):
    rows, width = held.shape

    def body(flag_ref, held_ref, met_ref, *refs):
        total = held_ref[...] + met_ref[...]
        if unit is not None:
            total = jnp.where(flag_ref[0] == 1, total, refs[0][...])
        refs[-1 - len(carried)][...] = total

    more = [] if unit is None else [unit]
    return pl.pallas_call(
        body,
        in_specs=[SMEM] + [VMEM] * (2 + len(more)) + [HBM] * len(carried) + [ANY] * len(after),
        out_specs=[VMEM] + [HBM] * len(carried),
        out_shape=[shape((rows, width), F32)] + [shape(c.shape, c.dtype) for c in carried],
        input_output_aliases={3 + len(more) + i: 1 + i for i in range(len(carried))},
        compiler_params=pltpu.CompilerParams(vmem_limit_bytes=FULL_LIMIT if carried else SMALL_LIMIT),
        cost_estimate=light(2 * rows * width, 16 * rows * width),
        name="pass_on",
    )(flag, held, met, *more, *carried, *after)


def add_up(arrays, after, long=False):
    def body(*refs):
        total = refs[0][...]
        for ref in refs[1 : len(arrays)]:
            total = total + ref[...]
        refs[-1][...] = total

    return pl.pallas_call(
        body,
        in_specs=[VMEM] * len(arrays) + [ANY] * len(after),
        out_specs=VMEM,
        out_shape=shape(arrays[0].shape, F32),
        compiler_params=pltpu.CompilerParams(vmem_limit_bytes=SMALL_LIMIT),
        cost_estimate=cost(0, 0, True) if long else light(0, 0),
        name="add_up",
    )(*arrays, *after)


def whole_sum(unit, n):
    if n == 1:
        return unit
    if n % 2:
        return lax.psum(unit, "tensor")
    me, half = lax.axis_index("tensor"), n // 2
    held = unit
    for j in range(half - 1):
        held = unit + lax.ppermute(held, "tensor", [(j, j + 1), (n - 1 - j, n - 2 - j)])
    total = held + lax.ppermute(held, "tensor", [(half - 1, half), (half, half - 1)])
    for j in reversed(range(half - 1)):
        came = lax.ppermute(total, "tensor", [(j + 1, j), (n - 2 - j, n - 1 - j)])
        total = jnp.where((me == j) | (me == n - 1 - j), came, total)
    return total


class Line:
    LAG = 3

    def __init__(self, count, flag, finish):
        self.count, self.flag, self.finish = count, flag, finish
        self.units, self.operands, self.came, self.held, self.met = [], {}, {}, {}, {}
        self.step = 0

    def send(self, step, operand):
        pairs = [(0, 1), (3, 2)] * (step < self.count) + [(1, 0), (2, 3)] * (step >= self.LAG)
        self.operands[step] = operand
        self.came[step] = lax.ppermute(operand, "tensor", pairs)

    def pump(self, after, carried=()):
        step = self.step
        self.step += 1
        unit = self.units[step] if step < self.count else None
        held = self.finish(self, step - self.LAG, unit, self.came[step], after)
        if unit is not None:
            self.held[step] = held
            self.met[step] = lax.ppermute(held, "tensor", [(1, 2), (2, 1)])
            after = [held]
        if step == 0:
            self.send(2, self.units[2])
        elif step <= self.count:
            ahead = step + 2
            unit = self.units[ahead] if ahead < self.count else None
            operand, *carried = pass_on(self.flag, self.held[step - 1], self.met[step - 1], unit, after, carried)
            self.send(ahead, operand)
            after = [operand]
        return after, *carried


class SmallSum:
    def __init__(self, values, axis, n):
        self.values, self.axis, self.n, self.apart, self.came = values, axis, n, 1, None

    def exchange(self):
        if self.n & (self.n - 1):
            self.values, self.apart = lax.psum(self.values, self.axis), self.n
        if self.apart >= self.n:
            return False
        self.came = lax.ppermute(self.values, self.axis, [(i, i ^ self.apart) for i in range(self.n)])
        self.apart *= 2
        return True

    def add(self, after):
        self.values = add_up([self.values, self.came], after)
        return [self.values]


def rotary(span):
    half = ROT // 2
    inverse = 10000.0 ** (-(2.0 * np.arange(half)) / ROT)
    angle = np.arange(span)[:, None] * inverse[None, :]
    cosine, sine = np.cos(angle), np.sin(angle)
    ones, zeros = np.ones((span, 128 - ROT)), np.zeros((span, 128 - ROT))
    nil = np.zeros((span, half))
    tables = (
        np.concatenate([cosine, cosine, ones], 1),
        np.concatenate([-sine, nil, zeros], 1),
        np.concatenate([nil, sine, zeros], 1),
    )
    return [jnp.asarray(t, F32) for t in tables]


def make_local(dp, tp):
    def local(
        layer_input,
        lengths,
        ln1_gain,
        ln1_shift,
        w_qkv,
        b_qkv,
        w_dense,
        b_dense,
        ln2_gain,
        ln2_shift,
        w_in,
        b_in,
        w_out,
        b_out,
        grad_out,
    ):
        rows, width = layer_input.shape
        assert lengths.shape[0] == 1
        columns, units = w_dense.shape[0], w_in.shape[1]
        tables = rotary(rows)
        w_three = jnp.transpose(w_qkv, (1, 0, 2))
        vec = lambda v: v.reshape(1, -1)
        gains = (vec(ln1_gain), vec(ln1_shift), vec(ln2_gain), vec(ln2_shift))
        size, unit = 256, 128
        starts = list(range(0, rows, size))
        each = rows // unit
        me = lax.axis_index("tensor")
        flag = jnp.stack([(me == 1) | (me == 2), me == 0]).astype(jnp.int32)
        outs = [None, None]

        def finish(line, done, unit, came, after):
            if done < 0:
                return take_in(flag, unit, came, None, None, 0, None, after)[0]
            which, at = divmod(done, each)
            held, outs[which] = take_in(
                flag, unit, came, line.operands[done + line.LAG], outs[which], at, layer_input.shape, after
            )
            return held

        straight = tp != 4
        line = None if straight else Line(2 * each, flag, finish)
        queue = [] if straight else line.units

        def pump(after, *carried):
            return (after, *carried) if straight else line.pump(after, carried)

        def forward(i, held, after):
            result = forward_rows(
                starts[i], size, unit, layer_input, lengths, flag, gains, w_three, b_qkv[:, None, :], w_in, vec(b_in),
                vec(b_dense + b_out), w_dense, w_out, tables, held, after,
            )
            queue.extend(result[6:-1])
            return result[:6], result[-1:]

        held, after = forward(0, None, [])
        if not straight:
            line.send(0, queue[0])
            line.send(1, queue[1])
        held, after = forward(1, held, [])
        cotan, b_out_grad = mask_rows(lengths, grad_out, after)
        held, after = forward(2, held, pump([b_out_grad])[0])
        held, after = forward(3, held, pump(after)[0])
        a_one, a_two, qkv, mixed, hidden, slope = held

        core = lax.rem(lax.axis_index("dp"), 2).astype(jnp.int32).reshape(1)
        blocks = dp // 2
        pairs = [(i, i ^ 1) for i in range(dp)]
        groups = [[2 * i + c for i in range(blocks)] for c in range(2)]

        def other_half(name, lefts, right, slide_left, after):
            half, token = pair_product(lefts, right, slide_left, 1 - core, None, blocks, after, name)
            return half, [token]

        def own_half(name, lefts, right, slide_left, came, after):
            half, token = pair_product(lefts, right, slide_left, core, came, blocks, after, name)
            return half, [token]

        def swap(half):
            return lax.ppermute(half, "dp", pairs)

        def over_chips(half):
            return lax.psum_scatter(half, "dp", scatter_dimension=0, axis_index_groups=groups, tiled=True)[0]

        out_parts = ([hidden, mixed], cotan[None], False)
        half, after = other_half("w_out_other", *out_parts, pump(after)[0])
        after, half = pump(after, half)
        came_out = swap(half)
        dqkv, b_qkv_grad = attend_back(lengths, qkv, cotan, w_dense, tables, after)
        qkv_parts = ([a_one], dqkv, True)
        out_half, after = own_half("w_out_own", *out_parts, came_out, pump([b_qkv_grad])[0])
        half, after = other_half("w_qkv_other", *qkv_parts, after)
        after, out_half, half = pump(after, out_half, half)
        out_grads = over_chips(out_half)
        came_qkv = swap(half)

        dhpre, smalls, biases = None, [], []

        def backward(i, after):
            nonlocal dhpre
            dhpre, small, bias, *dx = backward_rows(
                starts[i], size, unit, layer_input, flag, cotan, slope, dqkv, w_three, w_in, w_out, gains, dhpre, after
            )
            queue.extend(dx)
            smalls.append(small)
            biases.append(bias)
            return [bias]

        after = backward(0, after)
        qkv_half, after = own_half("w_qkv_own", *qkv_parts, came_qkv, pump(after)[0])
        after, qkv_half = pump(after, qkv_half)
        qkv_grads = over_chips(qkv_half)
        after = backward(1, after)
        after = backward(2, pump(after)[0])
        after = backward(3, pump(after)[0])
        in_parts = ([a_two], dhpre[None], True)
        half, after = other_half("w_in_other", *in_parts, pump(after)[0])
        after, half = pump(after, half)
        came_in = swap(half)

        small = SmallSum(add_up(smalls, after, True), "tensor", tp)
        if small.exchange():
            (after,) = pump([small.values])
            after = small.add(after)
        in_half, after = own_half("w_in_own", *in_parts, came_in, after)
        after, in_half = pump(after, in_half)
        in_grads = over_chips(in_half)
        while small.exchange():
            (after,) = pump(after)
            after = small.add(after)
        flat = jnp.concatenate(
            [small.values[:4].reshape(-1), b_out_grad.reshape(-1), sum(biases).reshape(-1), b_qkv_grad.reshape(-1)]
        )
        small = SmallSum(flat.reshape(-1, 128), "dp", dp)
        while small.exchange():
            (after,) = pump(after)
            after = small.add(after)
        while not straight and line.step < line.count + line.LAG:
            (after,) = pump(after)
        flat = small.values.reshape(-1)
        gain_one, shift_one, gain_two, shift_two, b_out_grad = (
            flat[i * width : (i + 1) * width] for i in range(5)
        )
        b_in_grad = flat[5 * width : 5 * width + units]
        b_qkv_grad = flat[5 * width + units :].reshape(3, columns)
        w_out_grad, w_dense_grad = out_grads[0, :units], out_grads[0, units:]
        w_qkv_grad = jnp.transpose(qkv_grads, (1, 0, 2))
        w_in_grad = in_grads[0]

        if straight:
            totals = [whole_sum(one, tp) for one in queue]
            first, second = jnp.concatenate(totals[:each]), jnp.concatenate(totals[each:])
            outs = [first.astype(BF16), second.astype(BF16)]
        layer_output, input_grad = outs
        return (
            layer_output,
            input_grad,
            gain_one,
            shift_one,
            w_qkv_grad,
            b_qkv_grad,
            w_dense_grad,
            b_out_grad,
            gain_two,
            shift_two,
            w_in_grad,
            b_in_grad,
            w_out_grad,
            b_out_grad,
        )

    return local


def solution(mesh):
    return jax.shard_map(
        make_local(mesh.shape["dp"], mesh.shape["tensor"]),
        mesh=mesh,
        in_specs=(
            P("dp", None),
            P("dp"),
            P(),
            P(),
            P(None, None, "tensor"),
            P(None, "tensor"),
            P("tensor", None),
            P(),
            P(),
            P(),
            P(None, "tensor"),
            P("tensor"),
            P("tensor", None),
            P(),
            P("dp", None),
        ),
        out_specs=(
            P("dp", None),
            P("dp", None),
            P(),
            P(),
            P("dp", None, "tensor"),
            P(None, "tensor"),
            P("tensor", "dp"),
            P(),
            P(),
            P(),
            P("dp", "tensor"),
            P("tensor"),
            P("tensor", "dp"),
            P(),
        ),
        check_vma=False,
    )
```

time: 1280 us -> 535 us (0.42)
  waiting for transfers between devices: 834 us -> 93.3 us
  Pallas kernels: 0 us -> 276 us
  matrix products: 242 us -> 0 us
  starting transfers between devices: 0.25 us -> 99.5 us
  other arithmetic: 88.2 us -> 0.85 us
  blocking collectives: 44.7 us -> 0 us
    psum x2 -> x0, waiting for transfers between devices: 474 us -> none  [the longest x1 284 us: local(): total_branch = lax.psum(part, 'tensor')]
    reduce_scatter x4 -> x0, waiting for transfers between devices: 360 us -> none  [the longest x1 120 us: local(): lax.psum_scatter(w_out_grad, 'dp', scatter_dimension=1, tiled=True)]
    pallas_call x0 -> x57, Pallas kernels: none -> 276 us  [the longest x4 64.1 us: backward_rows(): pl.pallas_call(body, grid=(1,), in_specs=specs, out_specs=[block(units),...]
    dot_general x29 -> x0, matrix products: 242 us -> none  [the longest x1 51.6 us: local(): jnp.dot(hidden, w_out, preferred_element_type=jnp.float32)]
    ppermute x0 -> x43, starting transfers between devices: none -> 98.8 us  [the longest x19 66 us: send(): self.came[step] = lax.ppermute(operand, 'tensor', pairs)]
    ppermute x0 -> x43, waiting for transfers between devices: none -> 93.2 us  [the longest x19 66.9 us: send(): self.came[step] = lax.ppermute(operand, 'tensor', pairs)]
    psum x2 -> x0, blocking collectives: 44.7 us -> none  [the longest x1 25.4 us: local(): lax.psum((gain_one, shift_one, gain_two, shift_two, b_qkv_grad, bias_out_...]
    reduce_sum x9 -> x0, other arithmetic: 39.3 us -> none  [the longest x1 11 us: layer_norm(): return center * lax.rsqrt(spread + EPS) * gain + shift]
  transfers between devices with their start and end apart: 6 -> 46, of which waited for: 6 -> 9; matrix products, arithmetic and copies ran while one was open for 7% -> 1% of each run, Pallas kernels for 0% -> 50%
where the time goes in v1:
time: 535 us; the launch traced here: 526 us
  Pallas kernels  276 us (52%)
  starting transfers between devices  99.5 us (19%)
  waiting for transfers between devices  93.3 us (17%)
  local copies, waits for them, and re-layouts  40.9 us (8%)
  between operations  16.2 us (3%)
    ppermute x19, waiting for transfers between devices, send(): self.came[step] = lax.ppermute(operand, 'tensor', pairs)  66.9 us
    ppermute x19, starting transfers between devices, send(): self.came[step] = lax.ppermute(operand, 'tensor', pairs)  66 us
    pallas_call x4, Pallas kernels, backward_rows(): pl.pallas_call(body, grid=(1,), in_specs=specs, out_specs=[block(units),...  64.1 us
    pallas_call x4, Pallas kernels, forward_rows(): pl.pallas_call(body, grid=(1,), in_specs=specs, out_specs=[block(width),...  60.4 us
    pallas_call x6, Pallas kernels, pair_product(): pl.pallas_call(body, grid_spec=pltpu.PrefetchScalarGridSpec(num_scalar_pr...  59.1 us
    pallas_call x19, Pallas kernels, take_in(): pl.pallas_call(body, in_specs=specs, out_specs=out_specs, out_shape=outs,...  41.7 us
    unnamed x177, local copies, waits for them, and re-layouts  34 us
    pallas_call x16, Pallas kernels, pass_on(): pl.pallas_call(body, in_specs=[SMEM] + [VMEM] * (2 + len(more)) + [HBM] *...  32.1 us
  transfers between devices with their start and end apart: 46, of which 9 were waited for; matrix products, arithmetic and copies ran while one was open for 1% of the time, Pallas kernels for 50%

profile of v1, /device:TPU:0, one launch (start us, length us, event | category | flops | bytes accessed | tf_op | source)
XLA Modules:
  0.0 526.4 jit_solution(9930842776758471877)
XLA Ops:
  16.0 14.8 %forward_rows.4 = (bf16[1024,2048]{1,0:T(8,128)(2,1)}, bf16[1024,2048]{1,0:T(8,128)(2,1)}, bf16[3,1024,512]{2,1,0:T(8,128)(2,1)}, bf16[1024,512]{1,0:T(8,128)(2,...) custom-call(s32[1]{0:T(128)S(6)} %copy.116.refs_0_.len_ref, ...), custom_call_target="tpu_custom_call" | custom-call | flops 40000000000 | bytes 35651584 | tf_op jit(solution)/shard_map/forward_rows/pallas_call | solution.py:184
  30.8 5.0 collective-permute-start.1
  38.3 15.2 %forward_rows.5 = (bf16[1024,2048]{1,0:T(8,128)(2,1)}, bf16[1024,2048]{1,0:T(8,128)(2,1)}, bf16[3,1024,512]{2,1,0:T(8,128)(2,1)}, bf16[1024,512]{1,0:T(8,128)(2,...) custom-call(s32[1]{0:T(128)S(6)} %copy.116.refs_0_.len_ref, ...), custom_call_target="tpu_custom_call", output_to_operand_aliasing={{0}: (17, {}), {1}: (18, {}), {2}: (19, {}), {3}: (20, {}),... | custom-call | flops 40000000000 | bytes 35651584 | tf_op jit(solution)/shard_map/forward_rows/pallas_call | solution.py:184
  56.8 3.5 mask_rows.1
  68.5 15.1 %forward_rows.6 = (bf16[1024,2048]{1,0:T(8,128)(2,1)}, bf16[1024,2048]{1,0:T(8,128)(2,1)}, bf16[3,1024,512]{2,1,0:T(8,128)(2,1)}, bf16[1024,512]{1,0:T(8,128)(2,...) custom-call(s32[1]{0:T(128)S(6)} %copy.116.refs_0_.len_ref, ...), custom_call_target="tpu_custom_call", output_to_operand_aliasing={{0}: (17, {}), {1}: (18, {}), {2}: (19, {}), {3}: (20, {}),... | custom-call | flops 40000000000 | bytes 35651584 | tf_op jit(solution)/shard_map/forward_rows/pallas_call | solution.py:184
  88.7 3.9 collective-permute-start.6
  92.6 15.4 %forward_rows.7 = (bf16[1024,2048]{1,0:T(8,128)(2,1)}, bf16[1024,2048]{1,0:T(8,128)(2,1)}, bf16[3,1024,512]{2,1,0:T(8,128)(2,1)}, bf16[1024,512]{1,0:T(8,128)(2,...) custom-call(s32[1]{0:T(128)S(6)} %copy.116.refs_0_.len_ref, ...), custom_call_target="tpu_custom_call", output_to_operand_aliasing={{0}: (17, {}), {1}: (18, {}), {2}: (19, {}), {3}: (20, {}),... | custom-call | flops 40000000000 | bytes 35651584 | tf_op jit(solution)/shard_map/forward_rows/pallas_call | solution.py:184
  112.8 3.8 collective-permute-start.5
  116.6 10.4 %w_out_other.1 = (f32[4,1,2560,256]{3,2,1,0:T(8,128)}, f32[8,128]{1,0:T(8,128)S(1)}) custom-call(s32[1]{0:T(128)S(6)} %sub.2._, bf16[1024,2048]{1,0:T(8,128)(2,1)} %get-tuple-element.149.refs_0_, bf16[1024,512]{1,0:T(8,128)(2,1)S(1)} %get-tuple-element.150.refs_1_, bf16[1,1024,2048]{2,1,0:T(8,128)(2,1)} %bitcast.74, f32[128,2048]{1,0:T(8,128)} %pass_on.17.refs_3_), custom_call_target="tpu_custom_call" | custom-call | flops 40000000000 | bytes 19922944 | tf_op jit(solution)/shard_map/w_out_other/pallas_call | solution.py:288
  135.5 7.0 %collective-permute-start.11 = (f32[128,2048]{1,0:T(8,128)}, f32[128,2048]{1,0:T(8,128)}, u32[]{:S(2)}, u32[]{:S(2)}) collective-permute-start(f32[128,2048]{1,0:T(8,128)} %get-tuple-element.158.refs_0_.refs_3_), channel_id=1, source_target_pairs={{0,1},{3,2},{1,0},{2,3},{4,5},{7,6},{5,4},{6,7},{8,9},{11,10},{9,8... | collective-permute-start | bytes 3145736 | tf_op jit(solution)/shard_map/ppermute | solution.py:594
  143.7 14.7 %attend_back.1 = (bf16[3,1024,512]{2,1,0:T(8,128)(2,1)}, f32[3,1,512]{2,1,0:T(1,128)S(1)}) custom-call(s32[1]{0:T(128)S(6)} %copy.116.refs_0_.len_ref, bf16[3,1024,512]{2,1,0:T(8,128)(2,1)} %get-tuple-element.154.q_ref.k_ref.v_ref, bf16[3,1024,512]{2,1,0:T(8,128)(2,1)} %get-tuple-element.154.q_ref.k_ref.v_ref, ...), custom_call_target="tpu_custom_call" | custom-call | flops 299999985664 | bytes 11534336 | tf_op jit(solution)/shard_map/attend_back/pallas_call | solution.py:343
  165.5 13.1 %w_out_own.1 = (f32[4,1,2560,256]{3,2,1,0:T(8,128)}, f32[8,128]{1,0:T(8,128)S(1)}) custom-call(s32[1]{0:T(128)} %bitcast.9._, bf16[1024,2048]{1,0:T(8,128)(2,1)} %get-tuple-element.149.refs_0_, bf16[1024,512]{1,0:T(8,128)(2,1)S(1)} %get-tuple-element.150.refs_1_, bf16[1,1024,2048]{2,1,0:T(8,128)(2,1)} %bitcast.75, ...), custom_call_target="tpu_custom_call" | custom-call | flops 40000000000 | bytes 19922944 | tf_op jit(solution)/shard_map/w_out_own/pallas_call | solution.py:288
  178.7 7.1 %w_qkv_other.1 = (f32[4,3,256,512]{3,2,1,0:T(8,128)}, f32[8,128]{1,0:T(8,128)S(1)}) custom-call(s32[1]{0:T(128)S(6)} %sub.2._, bf16[1024,2048]{1,0:T(8,128)(2,1)} %get-tuple-element.165.refs_0_, bf16[3,1024,512]{2,1,0:T(8,128)(2,1)S(1)} %copy-done.75, f32[8,128]{1,0:T(8,128)S(1)} %get-tuple-element.167.refs_2_), custom_call_target="tpu_custom_call" | custom-call | flops 40000000000 | bytes 13631488 | tf_op jit(solution)/shard_map/w_qkv_other/pallas_call | solution.py:288
  198.2 16.4 %backward_rows.4 = (bf16[1024,2048]{1,0:T(8,128)(2,1)}, f32[8,2048]{1,0:T(8,128)S(1)}, f32[1,2048]{1,0:T(1,128)S(1)}, f32[128,2048]{1,0:T(8,128)S(1)}, f32[128,2048]{1,0:T(8,128)S(1)}) custom-call(bf16[1024,2048]{1,0:T(8,128)(2,1)} %refs_0_.12, s32[2]{0:T(128)S(1)} %copy-done.34, bf16[1024,2048]{1,0:T(8,128)(2,1)} %copy-done.61, ...), custom_call_target="tpu_custom_call" | custom-call | flops 299999985664 | bytes 31457280 | tf_op jit(solution)/shard_map/backward_rows/pallas_call | solution.py:445
  223.9 8.8 %w_qkv_own.1 = (f32[4,3,256,512]{3,2,1,0:T(8,128)}, f32[8,128]{1,0:T(8,128)S(1)}) custom-call(s32[1]{0:T(128)} %bitcast.9._, bf16[1024,2048]{1,0:T(8,128)(2,1)} %get-tuple-element.165.refs_0_, bf16[3,1024,512]{2,1,0:T(8,128)(2,1)S(1)} %copy-done.76, f32[4,3,256,512]{3,2,1,0:T(8,128)} %collective-permute-done.14.refs_2_, f32[128,2048]{1,0:T(8,128)S(1)} %pass_on.21.refs_3_), custom_call_target="tpu_custom_call" | custom-call | flops 40000000000 | bytes 13631488 | tf_op jit(solution)/shard_map/w_qkv_own/pallas_call | solution.py:288
  241.7 8.6 %collective-permute-start.20 = (f32[128,2048]{1,0:T(8,128)}, f32[128,2048]{1,0:T(8,128)}, u32[]{:S(2)}, u32[]{:S(2)}) collective-permute-start(f32[128,2048]{1,0:T(8,128)} %get-tuple-element.185.refs_11_.refs_3_), channel_id=1, source_target_pairs={{0,1},{3,2},{1,0},{2,3},{4,5},{7,6},{5,4},{6,7},{8,9},{11,10},{9,8... | collective-permute-start | bytes 3145736 | tf_op jit(solution)/shard_map/ppermute | solution.py:594
  251.5 15.7 %backward_rows.5 = (bf16[1024,2048]{1,0:T(8,128)(2,1)}, f32[8,2048]{1,0:T(8,128)S(1)}, f32[1,2048]{1,0:T(1,128)S(1)}, f32[128,2048]{1,0:T(8,128)S(1)}, f32[128,2048]{1,0:T(8,128)S(1)}) custom-call(bf16[1024,2048]{1,0:T(8,128)(2,1)} %refs_0_.12, s32[2]{0:T(128)S(1)} %copy-done.35, bf16[1024,2048]{1,0:T(8,128)(2,1)} %copy-done.61, ...), custom_call_target="tpu_custom_call", output_to_operand_aliasing={{0}: (10, {})} | custom-call | flops 40000000000 | bytes 31457280 | tf_op jit(solution)/shard_map/backward_rows/pallas_call | solution.py:445
  278.4 16.5 %backward_rows.6 = (bf16[1024,2048]{1,0:T(8,128)(2,1)}, f32[8,2048]{1,0:T(8,128)S(1)}, f32[1,2048]{1,0:T(1,128)S(1)}, f32[128,2048]{1,0:T(8,128)S(1)}, f32[128,2048]{1,0:T(8,128)S(1)}) custom-call(bf16[1024,2048]{1,0:T(8,128)(2,1)} %refs_0_.12, s32[2]{0:T(128)S(1)} %copy-done.35, bf16[1024,2048]{1,0:T(8,128)(2,1)} %copy-done.61, ...), custom_call_target="tpu_custom_call", output_to_operand_aliasing={{0}: (10, {})} | custom-call | flops 40000000000 | bytes 31457280 | tf_op jit(solution)/shard_map/backward_rows/pallas_call | solution.py:445
  301.6 15.5 %backward_rows.7 = (bf16[1024,2048]{1,0:T(8,128)(2,1)}, f32[8,2048]{1,0:T(8,128)S(1)}, f32[1,2048]{1,0:T(1,128)S(1)}, f32[128,2048]{1,0:T(8,128)S(1)}, f32[128,2048]{1,0:T(8,128)S(1)}) custom-call(bf16[1024,2048]{1,0:T(8,128)(2,1)} %refs_0_.12, s32[2]{0:T(128)S(1)} %copy-done.35, bf16[1024,2048]{1,0:T(8,128)(2,1)} %copy-done.61, ...), custom_call_target="tpu_custom_call", output_to_operand_aliasing={{0}: (10, {})} | custom-call | flops 40000000000 | bytes 31457280 | tf_op jit(solution)/shard_map/backward_rows/pallas_call | solution.py:445
  321.0 4.6 collective-permute-start.23
  328.2 8.9 %w_in_other.1 = (f32[4,1,256,2048]{3,2,1,0:T(8,128)}, f32[8,128]{1,0:T(8,128)S(1)}) custom-call(s32[1]{0:T(128)S(6)} %sub.2._, bf16[1024,2048]{1,0:T(8,128)(2,1)S(1)} %copy-done.73, bf16[1,1024,2048]{2,1,0:T(8,128)(2,1)} %bitcast.90, f32[128,2048]{1,0:T(8,128)} %pass_on.25.refs_2_.refs_3_), custom_call_target="tpu_custom_call" | custom-call | flops 40000000000 | bytes 16777216 | tf_op jit(solution)/shard_map/w_in_other/pallas_call | solution.py:288
  345.4 5.8 %collective-permute-start.28 = (f32[8,2048]{1,0:T(8,128)S(1)}, f32[8,2048]{1,0:T(8,128)S(1)}, u32[]{:S(2)}, u32[]{:S(2)}) collective-permute-start(f32[8,2048]{1,0:T(8,128)S(1)} %add_up.6.refs_5_.refs_0_), channel_id=1, source_target_pairs={{0,1},{1,0},{2,3},{3,2},{4,5},{5,4},{6,7},{7,6},{8,9},{9,8},{10,11... | collective-permute-start | bytes 196616 | tf_op jit(solution)/shard_map/ppermute | solution.py:625
  358.8 10.8 %w_in_own.1 = (f32[4,1,256,2048]{3,2,1,0:T(8,128)}, f32[8,128]{1,0:T(8,128)S(1)}) custom-call(s32[1]{0:T(128)} %bitcast.9._, bf16[1024,2048]{1,0:T(8,128)(2,1)S(1)} %copy-done.74, bf16[1,1024,2048]{2,1,0:T(8,128)(2,1)} %bitcast.91, f32[4,1,256,2048]{3,2,1,0:T(8,128)} %collective-permute-done.27.refs_2_, f32[8,2048]{1,0:T(8,128)S(1)} %add_up.7.refs_3_.refs_0_), custom_call_target="tpu_custom_call" | custom-call | flops 40000000000 | bytes 16777216 | tf_op jit(solution)/shard_map/w_in_own/pallas_call | solution.py:288
  369.7 7.0 %collective-permute-done.30.refs_1_ = f32[128,2048]{1,0:T(8,128)S(1)} collective-permute-done((f32[128,2048]{1,0:T(8,128)}, f32[128,2048]{1,0:T(8,128)S(1)}, u32[]{:S(2)}, u32[]{:S(2)}) %collective-permute-start.30) | collective-permute-done | bytes 1048608 | tf_op jit(solution)/shard_map/ppermute | solution.py:594
  383.9 10.5 %collective-permute-start.32 = (f32[128,2048]{1,0:T(8,128)S(1)}, f32[128,2048]{1,0:T(8,128)S(1)}, u32[]{:S(2)}, u32[]{:S(2)}) collective-permute-start(f32[128,2048]{1,0:T(8,128)S(1)} %pass_on.27.refs_2_.refs_3_), channel_id=1, source_target_pairs={{0,1},{3,2},{1,0},{2,3},{4,5},{7,6},{5,4},{6,7},{8,9},{11,10},{9,8... | collective-permute-start | bytes 3145736 | tf_op jit(solution)/shard_map/ppermute | solution.py:594
  395.1 3.2 collective-permute-start.31
  398.3 20.2 %collective-permute-done.32.refs_1_ = f32[128,2048]{1,0:T(8,128)S(1)} collective-permute-done((f32[128,2048]{1,0:T(8,128)S(1)}, f32[128,2048]{1,0:T(8,128)S(1)}, u32[]{:S(2)}, u32[]{:S(2)}) %collective-permute-start.32) | collective-permute-done | bytes 1048608 | tf_op jit(solution)/shard_map/ppermute | solution.py:594
  422.0 5.0 collective-permute-start.33
  427.7 21.9 %collective-permute-done.33.refs_1_ = f32[8,2048]{1,0:T(8,128)S(1)} collective-permute-done((f32[8,2048]{1,0:T(8,128)S(1)}, f32[8,2048]{1,0:T(8,128)S(1)}, u32[]{:S(2)}, u32[]{:S(2)}) %collective-permute-start.33) | collective-permute-done | bytes 65568 | tf_op jit(solution)/shard_map/ppermute | solution.py:625
  466.5 14.5 %collective-permute-done.40.refs_1_ = f32[128,2048]{1,0:T(8,128)} collective-permute-done((f32[128,2048]{1,0:T(8,128)S(1)}, f32[128,2048]{1,0:T(8,128)}, u32[]{:S(2)}, u32[]{:S(2)}) %collective-permute-start.40) | collective-permute-done | bytes 1048608 | tf_op jit(solution)/shard_map/ppermute | solution.py:594
  483.1 20.3 %collective-permute-done.39.refs_1_ = f32[128,2048]{1,0:T(8,128)} collective-permute-done((f32[128,2048]{1,0:T(8,128)S(1)}, f32[128,2048]{1,0:T(8,128)}, u32[]{:S(2)}, u32[]{:S(2)}) %collective-permute-start.39) | collective-permute-done | bytes 1048608 | tf_op jit(solution)/shard_map/ppermute | solution.py:594
  511.8 4.8 collective-permute-done.38.refs_1_
  (309 shorter events, 162.3 us)
Async XLA Ops:
  7.2 499.7 %reduce-scatter.12.cloned.1.call-start = ((), (), s32[]{:S(2)}) async-start(), calls=%async_computation.4 | async-start | bytes 13107200
  30.8 31.6 %collective-permute-start.1 = (f32[128,2048]{1,0:T(8,128)S(1)}, f32[128,2048]{1,0:T(8,128)S(1)}, u32[]{:S(2)}, u32[]{:S(2)}) collective-permute-start(f32[128,2048]{1,0:T(8,128)S(1)} %get-tuple-element.135.refs_2_), channel_id=1, source_target_pairs={{0,1},{3,2},{4,5},{7,6},{8,9},{11,10},{12,13},{15,14},{16,17},{19,... | collective-permute-start | bytes 3145736 | tf_op jit(solution)/shard_map/ppermute | solution.py:594
  35.8 48.8 %collective-permute-start = (f32[128,2048]{1,0:T(8,128)}, f32[128,2048]{1,0:T(8,128)}, u32[]{:S(2)}, u32[]{:S(2)}) collective-permute-start(f32[128,2048]{1,0:T(8,128)} %get-tuple-element.122.refs_2_), channel_id=1, source_target_pairs={{0,1},{3,2},{4,5},{7,6},{8,9},{11,10},{12,13},{15,14},{16,17},{19,... | collective-permute-start | bytes 3145736 | tf_op jit(solution)/shard_map/ppermute | solution.py:594
  54.5 53.5 %collective-permute-start.3 = (f32[128,2048]{1,0:T(8,128)}, f32[128,2048]{1,0:T(8,128)}, u32[]{:S(2)}, u32[]{:S(2)}) collective-permute-start(f32[128,2048]{1,0:T(8,128)} %get-tuple-element.140.refs_2_), channel_id=1, source_target_pairs={{0,1},{3,2},{4,5},{7,6},{8,9},{11,10},{12,13},{15,14},{16,17},{19,... | collective-permute-start | bytes 3145736 | tf_op jit(solution)/shard_map/ppermute | solution.py:594
  88.7 38.3 %collective-permute-start.6 = (f32[128,2048]{1,0:T(8,128)S(1)}, f32[128,2048]{1,0:T(8,128)S(1)}, u32[]{:S(2)}, u32[]{:S(2)}) collective-permute-start(f32[128,2048]{1,0:T(8,128)S(1)} %pass_on.16.refs_23_.refs_3_), channel_id=1, source_target_pairs={{0,1},{3,2},{1,0},{2,3},{4,5},{7,6},{5,4},{6,7},{8,9},{11,10},{9,8... | collective-permute-start | bytes 3145736 | tf_op jit(solution)/shard_map/ppermute | solution.py:594
  112.8 45.6 %collective-permute-start.5 = (f32[128,2048]{1,0:T(8,128)}, f32[128,2048]{1,0:T(8,128)}, u32[]{:S(2)}, u32[]{:S(2)}) collective-permute-start(f32[128,2048]{1,0:T(8,128)} %pass_on.17.refs_3_), channel_id=1, source_target_pairs={{0,1},{3,2},{1,0},{2,3},{4,5},{7,6},{5,4},{6,7},{8,9},{11,10},{9,8... | collective-permute-start | bytes 3145736 | tf_op jit(solution)/shard_map/ppermute | solution.py:594
  129.4 32.2 %collective-permute-start.10 = (f32[128,2048]{1,0:T(8,128)}, f32[128,2048]{1,0:T(8,128)}, u32[]{:S(2)}, u32[]{:S(2)}) collective-permute-start(f32[128,2048]{1,0:T(8,128)} %get-tuple-element.157.refs_2_.held_ref), channel_id=1, source_target_pairs={{1,2},{2,1},{5,6},{6,5},{9,10},{10,9},{13,14},{14,13},{17,18},{18,... | collective-permute-start | bytes 3145736 | tf_op jit(solution)/shard_map/ppermute | solution.py:603
  135.5 30.1 %collective-permute-start.9 = (f32[4,1,2560,256]{3,2,1,0:T(8,128)}, f32[4,1,2560,256]{3,2,1,0:T(8,128)}, u32[]{:S(2)}, u32[]{:S(2)}) collective-permute-start(f32[4,1,2560,256]{3,2,1,0:T(8,128)} %get-tuple-element.162), channel_id=1, source_target_pairs={{0,4},{4,0},{8,12},{12,8},{16,20},{20,16},{24,28},{28,24},{1,5},{5... | collective-permute-start | bytes 31457288 | tf_op jit(solution)/shard_map/ppermute | solution.py:729
  135.5 50.3 %collective-permute-start.11 = (f32[128,2048]{1,0:T(8,128)}, f32[128,2048]{1,0:T(8,128)}, u32[]{:S(2)}, u32[]{:S(2)}) collective-permute-start(f32[128,2048]{1,0:T(8,128)} %get-tuple-element.158.refs_0_.refs_3_), channel_id=1, source_target_pairs={{0,1},{3,2},{1,0},{2,3},{4,5},{7,6},{5,4},{6,7},{8,9},{11,10},{9,8... | collective-permute-start | bytes 3145736 | tf_op jit(solution)/shard_map/ppermute | solution.py:594
  160.9 29.6 %collective-permute-start.8 = (f32[128,2048]{1,0:T(8,128)S(1)}, f32[128,2048]{1,0:T(8,128)S(1)}, u32[]{:S(2)}, u32[]{:S(2)}) collective-permute-start(f32[128,2048]{1,0:T(8,128)S(1)} %get-tuple-element.160.refs_1_.held_ref), channel_id=1, source_target_pairs={{1,2},{2,1},{5,6},{6,5},{9,10},{10,9},{13,14},{14,13},{17,18},{18,... | collective-permute-start | bytes 3145736 | tf_op jit(solution)/shard_map/ppermute | solution.py:603
  164.3 51.3 %collective-permute-start.13 = (f32[128,2048]{1,0:T(8,128)}, f32[128,2048]{1,0:T(8,128)}, u32[]{:S(2)}, u32[]{:S(2)}) collective-permute-start(f32[128,2048]{1,0:T(8,128)} %pass_on.19.refs_4_.refs_3_), channel_id=1, source_target_pairs={{0,1},{3,2},{1,0},{2,3},{4,5},{7,6},{5,4},{6,7},{8,9},{11,10},{9,8... | collective-permute-start | bytes 3145736 | tf_op jit(solution)/shard_map/ppermute | solution.py:594
  188.9 30.1 %collective-permute-start.15 = (f32[128,2048]{1,0:T(8,128)}, f32[128,2048]{1,0:T(8,128)}, u32[]{:S(2)}, u32[]{:S(2)}) collective-permute-start(f32[128,2048]{1,0:T(8,128)} %get-tuple-element.171.refs_3_.held_ref), channel_id=1, source_target_pairs={{1,2},{2,1},{5,6},{6,5},{9,10},{10,9},{13,14},{14,13},{17,18},{18,... | collective-permute-start | bytes 3145736 | tf_op jit(solution)/shard_map/ppermute | solution.py:603
  194.5 29.4 %collective-permute-start.14 = (f32[4,3,256,512]{3,2,1,0:T(8,128)}, f32[4,3,256,512]{3,2,1,0:T(8,128)}, u32[]{:S(2)}, u32[]{:S(2)}) collective-permute-start(f32[4,3,256,512]{3,2,1,0:T(8,128)} %get-tuple-element.177), channel_id=1, source_target_pairs={{0,4},{4,0},{8,12},{12,8},{16,20},{20,16},{24,28},{28,24},{1,5},{5... | collective-permute-start | bytes 18874376 | tf_op jit(solution)/shard_map/ppermute | solution.py:729
  194.8 38.0 %collective-permute-start.12 = (f32[128,2048]{1,0:T(8,128)}, f32[128,2048]{1,0:T(8,128)}, u32[]{:S(2)}, u32[]{:S(2)}) collective-permute-start(f32[128,2048]{1,0:T(8,128)} %get-tuple-element.172.refs_10_.refs_3_), channel_id=1, source_target_pairs={{0,1},{3,2},{1,0},{2,3},{4,5},{7,6},{5,4},{6,7},{8,9},{11,10},{9,8... | collective-permute-start | bytes 3145736 | tf_op jit(solution)/shard_map/ppermute | solution.py:594
  197.0 321.7 %reduce-scatter.10.cloned.1.call-start = ((), (), s32[]{:S(2)}) async-start(), calls=%async_computation.3 | async-start | bytes 7864320
  221.2 46.1 %collective-permute-start.18 = (f32[128,2048]{1,0:T(8,128)S(1)}, f32[128,2048]{1,0:T(8,128)S(1)}, u32[]{:S(2)}, u32[]{:S(2)}) collective-permute-start(f32[128,2048]{1,0:T(8,128)S(1)} %pass_on.21.refs_3_), channel_id=1, source_target_pairs={{0,1},{3,2},{1,0},{2,3},{4,5},{7,6},{5,4},{6,7},{8,9},{11,10},{9,8... | collective-permute-start | bytes 3145736 | tf_op jit(solution)/shard_map/ppermute | solution.py:594
  235.9 37.9 %collective-permute-start.16 = (f32[128,2048]{1,0:T(8,128)}, f32[128,2048]{1,0:T(8,128)}, u32[]{:S(2)}, u32[]{:S(2)}) collective-permute-start(f32[128,2048]{1,0:T(8,128)} %get-tuple-element.181.refs_2_.held_ref), channel_id=1, source_target_pairs={{1,2},{2,1},{5,6},{6,5},{9,10},{10,9},{13,14},{14,13},{17,18},{18,... | collective-permute-start | bytes 3145736 | tf_op jit(solution)/shard_map/ppermute | solution.py:603
  241.7 53.2 %collective-permute-start.20 = (f32[128,2048]{1,0:T(8,128)}, f32[128,2048]{1,0:T(8,128)}, u32[]{:S(2)}, u32[]{:S(2)}) collective-permute-start(f32[128,2048]{1,0:T(8,128)} %get-tuple-element.185.refs_11_.refs_3_), channel_id=1, source_target_pairs={{0,1},{3,2},{1,0},{2,3},{4,5},{7,6},{5,4},{6,7},{8,9},{11,10},{9,8... | collective-permute-start | bytes 3145736 | tf_op jit(solution)/shard_map/ppermute | solution.py:594
  273.5 245.3 %reduce-scatter.14.cloned.1.call-start = ((), (), s32[]{:S(2)}) async-start(), calls=%async_computation.5 | async-start | bytes 10485760
  275.5 41.6 %collective-permute-start.19 = (f32[128,2048]{1,0:T(8,128)S(1)}, f32[128,2048]{1,0:T(8,128)S(1)}, u32[]{:S(2)}, u32[]{:S(2)}) collective-permute-start(f32[128,2048]{1,0:T(8,128)S(1)} %pass_on.23.refs_11_.refs_3_), channel_id=1, source_target_pairs={{0,1},{3,2},{1,0},{2,3},{4,5},{7,6},{5,4},{6,7},{8,9},{11,10},{9,8... | collective-permute-start | bytes 3145736 | tf_op jit(solution)/shard_map/ppermute | solution.py:594
  299.9 37.3 %collective-permute-start.24 = (f32[128,2048]{1,0:T(8,128)S(1)}, f32[128,2048]{1,0:T(8,128)S(1)}, u32[]{:S(2)}, u32[]{:S(2)}) collective-permute-start(f32[128,2048]{1,0:T(8,128)S(1)} %pass_on.24.refs_11_.refs_3_), channel_id=1, source_target_pairs={{0,1},{3,2},{1,0},{2,3},{4,5},{7,6},{5,4},{6,7},{8,9},{11,10},{9,8... | collective-permute-start | bytes 3145736 | tf_op jit(solution)/shard_map/ppermute | solution.py:594
  321.0 30.2 %collective-permute-start.23 = (f32[128,2048]{1,0:T(8,128)}, f32[128,2048]{1,0:T(8,128)}, u32[]{:S(2)}, u32[]{:S(2)}) collective-permute-start(f32[128,2048]{1,0:T(8,128)} %pass_on.25.refs_2_.refs_3_), channel_id=1, source_target_pairs={{0,1},{3,2},{1,0},{2,3},{4,5},{7,6},{5,4},{6,7},{8,9},{11,10},{9,8... | collective-permute-start | bytes 3145736 | tf_op jit(solution)/shard_map/ppermute | solution.py:594
  353.7 26.2 %collective-permute-start.26 = (f32[128,2048]{1,0:T(8,128)S(1)}, f32[128,2048]{1,0:T(8,128)S(1)}, u32[]{:S(2)}, u32[]{:S(2)}) collective-permute-start(f32[128,2048]{1,0:T(8,128)S(1)} %get-tuple-element.213.refs_1_.held_ref), channel_id=1, source_target_pairs={{1,2},{2,1},{5,6},{6,5},{9,10},{10,9},{13,14},{14,13},{17,18},{18,... | collective-permute-start | bytes 3145736 | tf_op jit(solution)/shard_map/ppermute | solution.py:603
  383.9 34.6 %collective-permute-start.32 = (f32[128,2048]{1,0:T(8,128)S(1)}, f32[128,2048]{1,0:T(8,128)S(1)}, u32[]{:S(2)}, u32[]{:S(2)}) collective-permute-start(f32[128,2048]{1,0:T(8,128)S(1)} %pass_on.27.refs_2_.refs_3_), channel_id=1, source_target_pairs={{0,1},{3,2},{1,0},{2,3},{4,5},{7,6},{5,4},{6,7},{8,9},{11,10},{9,8... | collective-permute-start | bytes 3145736 | tf_op jit(solution)/shard_map/ppermute | solution.py:594
  394.4 32.6 %collective-permute-start.34 = (f32[128,2048]{1,0:T(8,128)S(1)}, f32[128,2048]{1,0:T(8,128)S(1)}, u32[]{:S(2)}, u32[]{:S(2)}) collective-permute-start(f32[128,2048]{1,0:T(8,128)S(1)} %copy-done.8), channel_id=1, source_target_pairs={{1,2},{2,1},{5,6},{6,5},{9,10},{10,9},{13,14},{14,13},{17,18},{18,... | collective-permute-start | bytes 3145736 | tf_op jit(solution)/shard_map/ppermute | solution.py:603
  395.1 54.5 %collective-permute-start.31 = (f32[128,2048]{1,0:T(8,128)}, f32[128,2048]{1,0:T(8,128)S(1)}, u32[]{:S(2)}, u32[]{:S(2)}) collective-permute-start(f32[128,2048]{1,0:T(8,128)} %get-tuple-element.221.refs_5_.refs_3_), channel_id=1, source_target_pairs={{0,1},{3,2},{1,0},{2,3},{4,5},{7,6},{5,4},{6,7},{8,9},{11,10},{9,8... | collective-permute-start | bytes 3145736 | tf_op jit(solution)/shard_map/ppermute | solution.py:594
  421.2 33.0 %collective-permute-start.37 = (f32[128,2048]{1,0:T(8,128)S(1)}, f32[128,2048]{1,0:T(8,128)S(1)}, u32[]{:S(2)}, u32[]{:S(2)}) collective-permute-start(f32[128,2048]{1,0:T(8,128)S(1)} %get-tuple-element.224.refs_0_.held_ref), channel_id=1, source_target_pairs={{1,2},{2,1},{5,6},{6,5},{9,10},{10,9},{13,14},{14,13},{17,18},{18,... | collective-permute-start | bytes 3145736 | tf_op jit(solution)/shard_map/ppermute | solution.py:603
  422.0 27.6 %collective-permute-start.33 = (f32[8,2048]{1,0:T(8,128)S(1)}, f32[8,2048]{1,0:T(8,128)S(1)}, u32[]{:S(2)}, u32[]{:S(2)}) collective-permute-start(f32[8,2048]{1,0:T(8,128)S(1)} %add_up.7.refs_3_.refs_0_), channel_id=1, source_target_pairs={{0,2},{1,3},{2,0},{3,1},{4,6},{5,7},{6,4},{7,5},{8,10},{9,11},{10,... | collective-permute-start | bytes 196616 | tf_op jit(solution)/shard_map/ppermute | solution.py:625
  452.9 28.1 %collective-permute-start.40 = (f32[128,2048]{1,0:T(8,128)S(1)}, f32[128,2048]{1,0:T(8,128)}, u32[]{:S(2)}, u32[]{:S(2)}) collective-permute-start(f32[128,2048]{1,0:T(8,128)S(1)} %pass_on.29.refs_2_), channel_id=1, source_target_pairs={{1,0},{2,3},{5,4},{6,7},{9,8},{10,11},{13,12},{14,15},{17,16},{18,... | collective-permute-start | bytes 3145736 | tf_op jit(solution)/shard_map/ppermute | solution.py:594
  454.8 48.6 %collective-permute-start.39 = (f32[128,2048]{1,0:T(8,128)S(1)}, f32[128,2048]{1,0:T(8,128)}, u32[]{:S(2)}, u32[]{:S(2)}) collective-permute-start(f32[128,2048]{1,0:T(8,128)S(1)} %pass_on.30.refs_2_), channel_id=1, source_target_pairs={{1,0},{2,3},{5,4},{6,7},{9,8},{10,11},{13,12},{14,15},{17,16},{18,... | collective-permute-start | bytes 3145736 | tf_op jit(solution)/shard_map/ppermute | solution.py:594
  463.4 42.2 %collective-permute-start.42 = (f32[108,128]{1,0:T(8,128)S(1)}, f32[108,128]{1,0:T(8,128)S(1)}, u32[]{:S(2)}, u32[]{:S(2)}) collective-permute-start(f32[108,128]{1,0:T(8,128)S(1)} %add_up.10.refs_4_.refs_0_.refs_2_), channel_id=1, source_target_pairs={{0,16},{4,20},{8,24},{12,28},{16,0},{20,4},{24,8},{28,12},{1,17},{... | collective-permute-start | bytes 165896 | tf_op jit(solution)/shard_map/ppermute | solution.py:625
  465.2 51.4 %collective-permute-start.38 = (f32[128,2048]{1,0:T(8,128)S(1)}, f32[128,2048]{1,0:T(8,128)}, u32[]{:S(2)}, u32[]{:S(2)}) collective-permute-start(f32[128,2048]{1,0:T(8,128)S(1)} %pass_on.31.refs_2_), channel_id=1, source_target_pairs={{1,0},{2,3},{5,4},{6,7},{9,8},{10,11},{13,12},{14,15},{17,16},{18,... | collective-permute-start | bytes 3145736 | tf_op jit(solution)/shard_map/ppermute | solution.py:594
  (101 other events, 1072.2 us)
Sparse Core Ops, SparseCore 0:
  197.1 102.8 reduce-scatter.11
  303.6 70.1 reduce-scatter.9
  384.0 96.1 reduce-scatter.13

commit v2 on v1

--- a/solution.py
+++ b/solution.py
@@ -13,8 +13,6 @@
 EPS = 1e-05
 F32 = jnp.float32
 BF16 = jnp.bfloat16
-VMEM_LIMIT = 48 * 1024 * 1024
-FULL_LIMIT = 56 * 1024 * 1024
 SMALL_LIMIT = 8 * 1024 * 1024
 NT = (((1,), (1,)), ((), ()))
 TN = (((0,), (0,)), ((), ()))
@@ -24,8 +22,8 @@
     return lax.dot_general(a, b, dims, preferred_element_type=F32)
 
 
-def params():
-    return pltpu.CompilerParams(vmem_limit_bytes=VMEM_LIMIT)
+def params(mebibytes):
+    return pltpu.CompilerParams(vmem_limit_bytes=mebibytes * 1024 * 1024)
 
 
 def cost(flops, nbytes, long=False):
@@ -47,6 +45,14 @@
 
 
 TOKEN = shape((8, 128), F32)
+
+
+def in_hbm(array):
+    return pltpu.with_memory_space_constraint(array, pltpu.HBM)
+
+
+def in_vmem(array):
+    return pltpu.with_memory_space_constraint(array, pltpu.VMEM)
 
 
 def turned(values, cosine, lower, upper):
@@ -75,26 +81,52 @@
         self.done += 1
 
 
-def forward_rows(start, size, unit, x, lengths, flag, gains, w_three, b_three, w_in, b_in, b_after, w_dense, w_out, tables, held, after):
+class Out:
+    def __init__(self, sems):
+        self.sems, self.copies = sems, []
+
+    def send(self, source, target):
+        copy = pltpu.make_async_copy(source, target, self.sems.at[len(self.copies)])
+        copy.start()
+        self.copies.append(copy)
+
+    def finish(self):
+        for copy in self.copies:
+            copy.wait()
+
+
+def forward_rows(start, size, unit, x, lengths, flag, gains, w_three, b_three, w_in, b_in, b_after, w_dense, w_out, tables, held, after, carried=()):
     rows, width = x.shape
     columns, units = w_dense.shape[0], w_in.shape[1]
     heads = columns // HD
-    at = start // size
     piece = min(512, units)
     wide = min(512, width)
     scale = 1.0 / math.sqrt(HD)
     past = start > 0
+    band = min(256, size)
+    bands = size // band
+    parts = size // unit
     steps = 3 + units // piece + 1 + width // wide
+    first = 4
+    sends = 4 + 2 * (units // piece) + (band // unit) * (width // wide)
+    vecs = 8 + len(b_after)
 
     def body(*refs):
-        len_ref, flag_ref, x_ref, g1, s1, g2, s2, b3_ref, bi_ref, ba_ref, c_ref, l_ref, u_ref = refs[:13]
-        w3_hbm, wi_hbm, wd_hbm, wo_hbm = refs[13:17]
-        one_ref, two_ref, qkv_ref, o_ref, hidden_ref, slope_ref, *part_refs, token_ref = refs[-14 - size // unit : -7]
+        len_ref, flag_ref, g1, s1, g2, s2, b3_ref, bi_ref, *ba_refs = refs[:vecs]
+        x_hbm, c_hbm, l_hbm, u_hbm, w3_hbm, wi_hbm, wd_hbm, wo_hbm = refs[vecs : vecs + 8]
+        outs = refs[-24 - parts - len(carried) : -17]
+        one_hbm, two_hbm, qkv_hbm, o_hbm, hidden_hbm, slope_hbm = outs[:6]
+        part_hbms, token_ref = outs[6 : 6 + parts], outs[6 + parts]
+        x_ref, c_ref, l_ref, u_ref, w3, wi, wd, wo, kv_ref = refs[-17:-8]
+        one_ref, two_ref, qkv_ref, o_ref, hidden_ref, slope_ref, part_ref, sems = refs[-8:]
         token_ref[...] = jnp.zeros_like(token_ref)
-        w3, wi, wd, wo, kv_ref, sems, kv_sem = refs[-7:]
-        if past:
-            earlier = pltpu.make_async_copy(refs[19].at[pl.ds(1, 2), pl.ds(0, start)], kv_ref, kv_sem)
-            earlier.start()
+        mine = pl.ds(start, size)
+        heads_in = [
+            pltpu.make_async_copy(a.at[mine], b, sems.at[i])
+            for i, (a, b) in enumerate(((x_hbm, x_ref), (c_hbm, c_ref), (l_hbm, l_ref), (u_hbm, u_ref)))
+        ]
+        for copy in heads_in:
+            copy.start()
         pieces = [(w3_hbm.at[c], w3.at[c]) for c in range(3)]
         for low in range(0, units, piece):
             here = pl.ds(low, piece)
@@ -103,119 +135,154 @@
         for low in range(0, width, wide):
             here = pl.ds(low, wide)
             pieces.append((wo_hbm.at[:, here], wo.at[:, here]))
-        stream = Stream(pieces, sems)
-        length = len_ref[0]
-
-        values = x_ref[...].astype(F32)
-        center = values - jnp.mean(values, -1, keepdims=True)
-        spread = jnp.mean(center * center, -1, keepdims=True)
-        normed = center * lax.rsqrt(spread + EPS)
-        one_ref[...] = (normed * g1[...] + s1[...]).astype(BF16)
-        two_ref[...] = (normed * g2[...] + s2[...]).astype(BF16)
-
-        for c in range(3):
-            stream.next()
-            acc = dot(one_ref[...], w3[c]) + b3_ref[c]
+        stream = Stream(pieces, sems.at[pl.ds(first, steps)])
+        if past:
+            earlier = pltpu.make_async_copy(
+                refs[vecs + 10].at[pl.ds(1, 2), pl.ds(0, start)],
+                kv_ref.at[:, pl.ds(0, start)],
+                sems.at[first + steps + bands * sends],
+            )
+            earlier.start()
+        def block(index, row, local, mine, out):
+            values = x_ref[local].astype(F32)
+            center = values - jnp.mean(values, -1, keepdims=True)
+            spread = jnp.mean(center * center, -1, keepdims=True)
+            normed = center * lax.rsqrt(spread + EPS)
+            one_ref[...] = (normed * g1[...] + s1[...]).astype(BF16)
+            two_ref[...] = (normed * g2[...] + s2[...]).astype(BF16)
+            out.send(one_ref, one_hbm.at[mine])
+            out.send(two_ref, two_hbm.at[mine])
+            if index == 0:
+                for copy in heads_in[1:]:
+                    copy.wait()
+
+            def place(c, acc):
+                for h in range(heads):
+                    cols = slice(h * HD, (h + 1) * HD)
+                    one_head = acc[:, cols] + b3_ref[c : c + 1, cols]
+                    if c < 2:
+                        one_head = turned(one_head, c_ref[local], l_ref[local], u_ref[local])
+                    qkv_ref[c, :, cols] = one_head.astype(BF16)
+
+            before = None
+            for c in range(3):
+                if index == 0:
+                    stream.next()
+                acc = dot(one_ref[...], w3[c])
+                if before is not None:
+                    place(c - 1, before)
+                before = acc
+            place(2, before)
+            out.send(qkv_ref, qkv_hbm.at[:, mine])
+            if index + 1 < bands:
+                kv_ref[:, row : row + band] = qkv_ref[1:]
+
+            here = lax.broadcasted_iota(jnp.int32, (band, band), 0)
+            there = lax.broadcasted_iota(jnp.int32, (band, band), 1)
+            seen = (there <= here) & (there + row < length)
+            if row:
+                inside = lax.broadcasted_iota(jnp.int32, (band, row), 1) < length
+                if index == 0:
+                    earlier.wait()
             for h in range(heads):
                 cols = slice(h * HD, (h + 1) * HD)
-                one_head = acc[:, cols]
-                if c < 2:
-                    one_head = turned(one_head, c_ref[...], l_ref[...], u_ref[...])
-                qkv_ref[c, :, cols] = one_head.astype(BF16)
-
-        here = lax.broadcasted_iota(jnp.int32, (size, size), 0)
-        there = lax.broadcasted_iota(jnp.int32, (size, size), 1)
-        seen = (there <= here) & (there + start < length)
-        if past:
-            inside = lax.broadcasted_iota(jnp.int32, (size, start), 1) < length
-            earlier.wait()
-        for h in range(heads):
-            cols = slice(h * HD, (h + 1) * HD)
-            query = qkv_ref[0, :, cols]
-            now = jnp.where(seen, dot(query, qkv_ref[1, :, cols], NT) * scale, -1e30)
-            top = jnp.max(now, -1, keepdims=True)
-            if past:
-                old = jnp.where(inside, dot(query, kv_ref[0, :, cols], NT) * scale, -1e30)
-                top = jnp.maximum(top, jnp.max(old, -1, keepdims=True))
-                old = jnp.exp(old - top)
-            now = jnp.exp(now - top)
-            total = jnp.sum(now, -1, keepdims=True)
-            if past:
-                total = total + jnp.sum(old, -1, keepdims=True)
-            share = 1.0 / total
-            mixed = dot((now * share).astype(BF16), qkv_ref[2, :, cols])
-            if past:
-                mixed = mixed + dot((old * share).astype(BF16), kv_ref[1, :, cols])
-            o_ref[:, cols] = mixed.astype(BF16)
-
-        for low in range(0, units, piece):
-            cols = slice(low, low + piece)
-            stream.next()
-            pre = dot(two_ref[...], wi[:, cols]) + bi_ref[:, cols]
-            share = 0.5 + 0.5 * lax.erf(pre * (1.0 / math.sqrt(2.0)))
-            hidden_ref[:, cols] = (pre * share).astype(BF16)
-            bell = jnp.exp(-0.5 * pre * pre) * (1.0 / math.sqrt(2.0 * math.pi))
-            slope_ref[:, cols] = (share + pre * bell).astype(BF16)
-
-        stream.next()
+                query = qkv_ref[0, :, cols]
+                now = jnp.where(seen, dot(query, qkv_ref[1, :, cols], NT) * scale, -1e30)
+                top = jnp.max(now, -1, keepdims=True)
+                if row:
+                    old = jnp.where(inside, dot(query, kv_ref[0, :row, cols], NT) * scale, -1e30)
+                    top = jnp.maximum(top, jnp.max(old, -1, keepdims=True))
+                    old = jnp.exp(old - top)
+                now = jnp.exp(now - top)
+                total = jnp.sum(now, -1, keepdims=True)
+                if row:
+                    total = total + jnp.sum(old, -1, keepdims=True)
+                share = 1.0 / total
+                mixed = dot((now * share).astype(BF16), qkv_ref[2, :, cols])
+                if row:
+                    mixed = mixed + dot((old * share).astype(BF16), kv_ref[1, :row, cols])
+                o_ref[:, cols] = mixed.astype(BF16)
+            out.send(o_ref, o_hbm.at[mine])
+
+            def bend(low, acc):
+                cols = slice(low, low + piece)
+                pre = acc + bi_ref[:, cols]
+                share = 0.5 + 0.5 * lax.erf(pre * (1.0 / math.sqrt(2.0)))
+                hidden_ref[:, cols] = (pre * share).astype(BF16)
+                bell = jnp.exp(-0.5 * pre * pre) * (1.0 / math.sqrt(2.0 * math.pi))
+                slope_ref[:, cols] = (share + pre * bell).astype(BF16)
+                there = pl.ds(low, piece)
+                out.send(hidden_ref.at[:, there], hidden_hbm.at[mine, there])
+                out.send(slope_ref.at[:, there], slope_hbm.at[mine, there])
+
+            before = None
+            for low in range(0, units, piece):
+                if index == 0:
+                    stream.next()
+                acc = dot(two_ref[...], wi[:, low : low + piece])
+                if before is not None:
+                    bend(low - piece, before)
+                before = acc
+            bend(units - piece, before)
+
+            if index == 0:
+                stream.next()
+            for low in range(0, width, wide):
+                cols = slice(low, low + wide)
+                if index == 0:
+                    stream.next()
+                acc = dot(o_ref[...], wd[:, cols]) + dot(hidden_ref[...], wo[:, cols])
+                more = x_ref[local, cols].astype(F32)
+                for ba_ref in ba_refs:
+                    more = more + ba_ref[:, cols]
+                part_ref[:, cols] = acc + own * more
+                for i, part_hbm in enumerate(part_hbms[index * (band // unit) : (index + 1) * (band // unit)]):
+                    there = pl.ds(low, wide)
+                    out.send(part_ref.at[pl.ds(i * unit, unit), there], part_hbm.at[:, there])
+
+        length = len_ref[0]
         own = flag_ref[1].astype(F32)
-        for low in range(0, width, wide):
-            cols = slice(low, low + wide)
-            stream.next()
-            acc = dot(o_ref[...], wd[:, cols]) + dot(hidden_ref[...], wo[:, cols])
-            acc = acc + own * (x_ref[:, cols].astype(F32) + ba_ref[:, cols])
-            for i, part_ref in enumerate(part_refs):
-                part_ref[:, cols] = acc[i * unit : (i + 1) * unit]
-
-    vec = lambda n: pl.BlockSpec((1, n), lambda i: (0, 0))
-    table = pl.BlockSpec((size, 128), lambda i: (at, 0))
-    block = lambda n: pl.BlockSpec((size, n), lambda i: (at, 0))
-    operands = [lengths, flag, x, *gains, b_three, b_in, b_after, *tables, w_three, w_in, w_dense, w_out]
-    specs = [SMEM, SMEM, block(width)] + [vec(width)] * 4
-    specs += [pl.BlockSpec((3, 1, columns), lambda i: (0, 0, 0)), vec(units), vec(width)] + [table] * 3 + [HBM] * 4
+        heads_in[0].wait()
+        for index in range(bands):
+            row = start + index * band
+            local = slice(index * band, (index + 1) * band)
+            mine = pl.ds(row, band)
+            out = Out(sems.at[pl.ds(first + steps + index * sends, sends)])
+            block(index, row, local, mine, out)
+            out.finish()
+
+    flat = lambda v: v.reshape(1, -1)
+    small = [*gains, b_three, flat(b_in), *map(flat, b_after)]
+    operands = [lengths, flag, *map(in_hbm, small), *map(in_hbm, (x, *tables, w_three, w_in, w_dense, w_out))]
+    specs = [SMEM, SMEM] + [pl.BlockSpec(v.shape, lambda i: (0, 0)) for v in small] + [HBM] * 8
     aliases = {}
     if past:
         aliases = {len(operands) + i: i for i in range(6)}
-        operands += list(held)
+        operands += [in_hbm(array) for array in held]
         specs += [HBM] * 6
+    for i, array in enumerate(carried):
+        aliases[len(operands)] = 7 + parts + i
+        operands.append(in_hbm(array))
+        specs.append(HBM)
     operands += list(after)
     specs += [ANY] * len(after)
     flops = 2 * size * width * (4 * columns + 2 * units)
+    whole = [(rows, width), (rows, width), (3, rows, columns), (rows, columns), (rows, units), (rows, units)]
+    mine = [(band, width), (band, width), (3, band, columns), (band, columns), (band, units), (band, units)]
     return pl.pallas_call(
         body,
         grid=(1,),
         in_specs=specs,
-        out_specs=[
-            block(width),
-            block(width),
-            pl.BlockSpec((3, size, columns), lambda i: (0, at, 0)),
-            block(columns),
-            block(units),
-            block(units),
-        ]
-        + [pl.BlockSpec((unit, width), lambda i: (0, 0))] * (size // unit)
-        + [pl.BlockSpec(TOKEN.shape, lambda i: (0, 0))],
-        out_shape=[
-            shape((rows, width), BF16),
-            shape((rows, width), BF16),
-            shape((3, rows, columns), BF16),
-            shape((rows, columns), BF16),
-            shape((rows, units), BF16),
-            shape((rows, units), BF16),
-        ]
-        + [shape((unit, width), F32)] * (size // unit)
-        + [TOKEN],
-        scratch_shapes=[
-            pltpu.VMEM(w_three.shape, BF16),
-            pltpu.VMEM(w_in.shape, BF16),
-            pltpu.VMEM(w_dense.shape, BF16),
-            pltpu.VMEM(w_out.shape, BF16),
-            pltpu.VMEM((2, max(start, 16), columns), BF16),
-            pltpu.SemaphoreType.DMA((steps,)),
-            pltpu.SemaphoreType.DMA,
-        ],
+        out_specs=[HBM] * (6 + parts) + [pl.BlockSpec(TOKEN.shape, lambda i: (0, 0))] + [HBM] * len(carried),
+        out_shape=[pltpu.HBM(dims, BF16) for dims in whole] + [pltpu.HBM((unit, width), F32)] * parts + [TOKEN] + [pltpu.HBM(c.shape, c.dtype) for c in carried],
+        scratch_shapes=[pltpu.VMEM((size, width), BF16)]
+        + [pltpu.VMEM((size, 128), F32)] * 3
+        + [pltpu.VMEM(w.shape, BF16) for w in (w_three, w_in, w_dense, w_out)]
+        + [pltpu.VMEM((2, max(start + size - band, 16), columns), BF16)]
+        + [pltpu.VMEM(dims, BF16) for dims in mine]
+        + [pltpu.VMEM((band, width), F32), pltpu.SemaphoreType.DMA((first + steps + bands * sends + 1,))],
         input_output_aliases=aliases,
-        compiler_params=params(),
+        compiler_params=params(46),
         cost_estimate=cost(flops, 2 * width * (4 * columns + 2 * units) + size * width * 20),
         name="forward_rows",
     )(*operands)
@@ -246,14 +313,14 @@
         grid=(rows // step,),
         in_specs=[SMEM, row] + [ANY] * len(after),
         out_specs=[row, pl.BlockSpec((1, width), lambda i: (0, 0))],
-        out_shape=[shape((rows, width), BF16), shape((1, width), F32)],
-        compiler_params=params(),
+        out_shape=[pltpu.HBM((rows, width), BF16), shape((1, width), F32)],
+        compiler_params=params(46),
         cost_estimate=cost(2 * rows * width, 4 * rows * width),
         name="mask_rows",
-    )(lengths, grad_out, *after)
-
-
-def pair_product(lefts, right, slide_left, parity, added, blocks, after, name):
+    )(lengths, in_hbm(grad_out), *after)
+
+
+def pair_product(lefts, right, slide_left, parity, added, blocks, after, name, long=False):
     rows = right.shape[-2]
     many = right.shape[0]
     left_width = sum(left.shape[1] for left in lefts)
@@ -293,11 +360,11 @@
             in_specs=specs + [ANY] * len(after),
             out_specs=[out, pl.BlockSpec(TOKEN.shape, lambda i, p: (0, 0))],
         ),
-        out_shape=[shape((blocks, many, tall, wide), F32), TOKEN],
-        compiler_params=params(),
-        cost_estimate=cost(2 * rows * blocks * many * tall * wide, 2 * rows * (left_width + many * right.shape[2]) + 4 * blocks * many * tall * wide),
+        out_shape=[pltpu.HBM((blocks, many, tall, wide), F32), TOKEN],
+        compiler_params=params(46),
+        cost_estimate=cost(2 * rows * blocks * many * tall * wide, 2 * rows * (left_width + many * right.shape[2]) + 4 * blocks * many * tall * wide, long),
         name=name,
-    )(parity, *operands, *after)
+    )(parity, *map(in_hbm, operands), *after)
 
 
 def attend_back(lengths, qkv, cotan, w_dense, tables, after):
@@ -359,30 +426,39 @@
             pl.BlockSpec((3, rows, HD), lambda h: (0, 0, h)),
             pl.BlockSpec((3, 1, HD), lambda h: (0, 0, h)),
         ],
-        out_shape=[shape((3, rows, columns), BF16), shape((3, 1, columns), F32)],
+        out_shape=[pltpu.HBM((3, rows, columns), BF16), shape((3, 1, columns), F32)],
         scratch_shapes=[pltpu.VMEM((rows, HD), F32)] * 2,
-        compiler_params=params(),
+        compiler_params=params(46),
         cost_estimate=cost(
             2 * rows * columns * width + 10 * rows * rows * columns,
             2 * rows * (width + 7 * columns),
             True,
         ),
         name="attend_back",
-    )(lengths, qkv, qkv, qkv, cotan, w_dense, *tables, *after)
+    )(lengths, *map(in_hbm, (qkv, qkv, qkv, cotan, w_dense, *tables)), *after)
 
 
 def backward_rows(start, size, unit, x, flag, cotan, slope, dqkv, w_three, w_in, w_out, gains, held, after):
     rows, width = x.shape
     columns, units = dqkv.shape[2], slope.shape[1]
-    at = start // size
     piece = min(512, units)
     wide = min(512, width)
+    parts = size // unit
     steps = units // piece + width // wide
+    sends = units // piece + parts
 
     def body(*refs):
-        x_ref, flag_ref, g_ref, slope_ref, q_ref, g1, g2, w3_hbm, wi_hbm, wo_hbm = refs[:10]
-        dh_ref, small_ref, bias_ref, *dx_refs = refs[-10 - size // unit : -7]
-        w3, wi, wo, one, two, sems, sems3 = refs[-7:]
+        flag_ref, g1, g2, x_hbm, g_hbm, slope_hbm, q_hbm, w3_hbm, wi_hbm, wo_hbm = refs[:10]
+        dh_hbm, *dx_hbms, small_ref, bias_ref = refs[-16 - parts : -13]
+        x_ref, g_ref, slope_ref, q_ref, w3, wi, wo, one, two, normed_ref, dh_ref, dx_ref, sems = refs[-13:]
+        mine = pl.ds(start, size)
+        sources = (g_hbm.at[mine], slope_hbm.at[mine], x_hbm.at[mine], q_hbm.at[:, mine])
+        inward = [
+            pltpu.make_async_copy(a, b, sems.at[i])
+            for i, (a, b) in enumerate(zip(sources, (g_ref, slope_ref, x_ref, q_ref)))
+        ]
+        for copy in inward[:2]:
+            copy.start()
         pieces = []
         for low in range(0, units, piece):
             here = pl.ds(low, piece)
@@ -390,55 +466,80 @@
         for low in range(0, width, wide):
             here = pl.ds(low, wide)
             pieces.append((wi_hbm.at[here], wi.at[here]))
-        stream = Stream(pieces, sems)
-        three = pltpu.make_async_copy(w3_hbm, w3, sems3)
+        stream = Stream(pieces, sems.at[pl.ds(4, steps)])
+        out = Out(sems.at[pl.ds(4 + steps, sends)])
+        three = pltpu.make_async_copy(w3_hbm, w3, sems.at[4 + steps + sends])
+
+        def slope_times(low, acc):
+            here = slice(low, low + piece)
+            grad = (acc * slope_ref[:, here].astype(F32)).astype(BF16)
+            dh_ref[:, here] = grad
+            bias_ref[:, here] = jnp.sum(grad.astype(F32), 0, keepdims=True)
+            there = pl.ds(low, piece)
+            out.send(dh_ref.at[:, there], dh_hbm.at[mine, there])
+
+        inward[0].wait()
+        before = None
         for low in range(0, units, piece):
-            here = slice(low, low + piece)
             stream.next()
             if low == 0:
+                for copy in inward[2:]:
+                    copy.start()
                 three.start()
-            grad = (dot(g_ref[...], wo[here], NT) * slope_ref[:, here].astype(F32)).astype(BF16)
-            dh_ref[:, here] = grad
-            bias_ref[:, here] = jnp.sum(grad.astype(F32), 0, keepdims=True)
+                inward[1].wait()
+            acc = dot(g_ref[...], wo[low : low + piece], NT)
+            if before is not None:
+                slope_times(low - piece, before)
+            before = acc
+        slope_times(units - piece, before)
+        for copy in inward[2:]:
+            copy.wait()
         three.wait()
+        band = 64
+        rstds = []
+        for low in range(0, size, band):
+            here = slice(low, low + band)
+            values = x_ref[here].astype(F32)
+            center = values - jnp.mean(values, -1, keepdims=True)
+            rstds.append(lax.rsqrt(jnp.mean(center * center, -1, keepdims=True) + EPS))
+            normed_ref[here] = center * rstds[-1]
         for low in range(0, width, wide):
             here = slice(low, low + wide)
             acc = dot(q_ref[0], w3[0, here], NT)
             for c in (1, 2):
                 acc = acc + dot(q_ref[c], w3[c, here], NT)
             one[:, here] = acc
+        for low in range(0, width, wide):
+            here = slice(low, low + wide)
             stream.next()
             two[:, here] = dot(dh_ref[...], wi[here], NT)
         gain_one, gain_two = g1[...], g2[...]
         own = flag_ref[1].astype(F32)
         sums = [jnp.zeros((1, width), F32)] * 4
-        band = 64
-        for low in range(0, size, band):
+        for at, low in enumerate(range(0, size, band)):
             here = slice(low, low + band)
-            values = x_ref[here].astype(F32)
-            center = values - jnp.mean(values, -1, keepdims=True)
-            rstd = lax.rsqrt(jnp.mean(center * center, -1, keepdims=True) + EPS)
-            normed = center * rstd
-            d_one, d_two = one[here], two[here]
+            normed, d_one, d_two = normed_ref[here], one[here], two[here]
             grad = d_one * gain_one + d_two * gain_two
-            dx_refs[low // unit][low % unit : low % unit + band] = rstd * (
+            dx_ref[here] = rstds[at] * (
                 grad
                 - jnp.mean(grad, -1, keepdims=True)
                 - normed * jnp.mean(grad * normed, -1, keepdims=True)
             ) + own * g_ref[here].astype(F32)
             terms = (d_one * normed, d_one, d_two * normed, d_two)
             sums = [s + jnp.sum(t, 0, keepdims=True) for s, t in zip(sums, terms)]
+            if (low + band) % unit == 0:
+                i = low // unit
+                out.send(dx_ref.at[pl.ds(i * unit, unit)], dx_hbms[i])
         small_ref[...] = jnp.concatenate(sums + [jnp.zeros((4, width), F32)], 0)
+        out.finish()
 
     vec = lambda n: pl.BlockSpec((1, n), lambda i: (0, 0))
-    block = lambda n: pl.BlockSpec((size, n), lambda i: (at, 0))
-    operands = [x, flag, cotan, slope, dqkv, gains[0], gains[2], w_three, w_in, w_out]
-    specs = [block(width), SMEM, block(width), block(units), pl.BlockSpec((3, size, columns), lambda i: (0, at, 0))]
-    specs += [vec(width), vec(width)] + [HBM] * 3
+    operands = [flag, *map(in_hbm, (gains[0], gains[2], x, cotan, slope, dqkv, w_three, w_in, w_out))]
+    specs = [SMEM, vec(width), vec(width)] + [HBM] * 7
     aliases = {}
     if held is not None:
         aliases = {len(operands): 0}
-        operands.append(held)
+        operands.append(in_hbm(held))
         specs.append(HBM)
     operands += list(after)
     specs += [ANY] * len(after)
@@ -446,29 +547,27 @@
         body,
         grid=(1,),
         in_specs=specs,
-        out_specs=[
-            block(units),
-            pl.BlockSpec((8, width), lambda i: (0, 0)),
-            vec(units),
-        ]
-        + [pl.BlockSpec((unit, width), lambda i: (0, 0))] * (size // unit),
-        out_shape=[
-            shape((rows, units), BF16),
-            shape((8, width), F32),
-            shape((1, units), F32),
-        ]
-        + [shape((unit, width), F32)] * (size // unit),
+        out_specs=[HBM] * (1 + parts) + [pl.BlockSpec((8, width), lambda i: (0, 0)), vec(units)],
+        out_shape=[pltpu.HBM((rows, units), BF16)]
+        + [pltpu.HBM((unit, width), F32)] * parts
+        + [shape((8, width), F32), shape((1, units), F32)],
         scratch_shapes=[
+            pltpu.VMEM((size, width), BF16),
+            pltpu.VMEM((size, width), BF16),
+            pltpu.VMEM((size, units), BF16),
+            pltpu.VMEM((3, size, columns), BF16),
             pltpu.VMEM(w_three.shape, BF16),
             pltpu.VMEM(w_in.shape, BF16),
             pltpu.VMEM(w_out.shape, BF16),
             pltpu.VMEM((size, width), F32),
             pltpu.VMEM((size, width), F32),
-            pltpu.SemaphoreType.DMA((steps,)),
-            pltpu.SemaphoreType.DMA,
+            pltpu.VMEM((size, width), F32),
+            pltpu.VMEM((size, units), BF16),
+            pltpu.VMEM((size, width), F32),
+            pltpu.SemaphoreType.DMA((4 + steps + sends + 1,)),
         ],
         input_output_aliases=aliases,
-        compiler_params=params(),
+        compiler_params=params(46),
         cost_estimate=cost(2 * size * width * (2 * units + 3 * columns), 2 * width * (2 * units + 3 * columns) + 16 * size * width, start == 0),
         name="backward_rows",
     )(*operands)
@@ -490,22 +589,22 @@
         if has_total:
             copy.wait()
 
-    operands, specs = [flag, came], [SMEM, VMEM]
+    operands, specs = [flag, in_vmem(came)], [SMEM, VMEM]
     outs, out_specs, aliases, scratch = [], [], {}, []
     if has_unit:
         operands.append(unit)
         specs.append(VMEM)
-        outs.append(shape((rows, width), F32))
+        outs.append(pltpu.VMEM((rows, width), F32))
         out_specs.append(VMEM)
     if has_total:
-        operands.append(operand)
+        operands.append(in_vmem(operand))
         specs.append(VMEM)
-        outs.append(shape(out_shape, BF16))
+        outs.append(pltpu.HBM(out_shape, BF16))
         out_specs.append(HBM)
         scratch = [pltpu.VMEM((rows, width), BF16), pltpu.SemaphoreType.DMA]
         if out is not None:
             aliases = {len(operands): len(outs) - 1}
-            operands.append(out)
+            operands.append(in_hbm(out))
             specs.append(HBM)
     operands += after
     specs += [ANY] * len(after)
@@ -538,12 +637,12 @@
         body,
         in_specs=[SMEM] + [VMEM] * (2 + len(more)) + [HBM] * len(carried) + [ANY] * len(after),
         out_specs=[VMEM] + [HBM] * len(carried),
-        out_shape=[shape((rows, width), F32)] + [shape(c.shape, c.dtype) for c in carried],
+        out_shape=[pltpu.VMEM((rows, width), F32)] + [pltpu.HBM(c.shape, c.dtype) for c in carried],
         input_output_aliases={3 + len(more) + i: 1 + i for i in range(len(carried))},
-        compiler_params=pltpu.CompilerParams(vmem_limit_bytes=FULL_LIMIT if carried else SMALL_LIMIT),
+        compiler_params=pltpu.CompilerParams(vmem_limit_bytes=SMALL_LIMIT),
         cost_estimate=light(2 * rows * width, 16 * rows * width),
         name="pass_on",
-    )(flag, held, met, *more, *carried, *after)
+    )(flag, in_vmem(held), in_vmem(met), *more, *map(in_hbm, carried), *after)
 
 
 def add_up(arrays, after, long=False):
@@ -562,6 +661,54 @@
         cost_estimate=cost(0, 0, True) if long else light(0, 0),
         name="add_up",
     )(*arrays, *after)
+
+
+def split_rows(array, at, after):
+    rows, width = array.shape
+    step = math.gcd(at, rows - at)
+    first = at // step
+
+    def body(in_ref, *refs):
+        one_ref, two_ref = refs[-2:]
+        i = pl.program_id(0)
+
+        @pl.when(i < first)
+        def _():
+            one_ref[...] = in_ref[...]
+
+        @pl.when(i >= first)
+        def _():
+            two_ref[...] = in_ref[...]
+
+    block = (step, width)
+    return pl.pallas_call(
+        body,
+        grid=(rows // step,),
+        in_specs=[pl.BlockSpec(block, lambda i: (i, 0))] + [ANY] * len(after),
+        out_specs=[
+            pl.BlockSpec(block, lambda i: (jnp.minimum(i, first - 1), 0)),
+            pl.BlockSpec(block, lambda i: (jnp.maximum(i - first, 0), 0)),
+        ],
+        out_shape=[pltpu.HBM((at, width), F32), pltpu.HBM((rows - at, width), F32)],
+        compiler_params=pltpu.CompilerParams(vmem_limit_bytes=SMALL_LIMIT),
+        cost_estimate=light(0, 8 * rows * width),
+        name="split_rows",
+    )(in_hbm(array), *after)
+
+
+def rounded(array):
+    def body(in_ref, out_ref):
+        out_ref[...] = in_ref[...].astype(BF16)
+
+    block = pl.BlockSpec((min(128, array.shape[0]), array.shape[1]), lambda i: (i, 0))
+    return pl.pallas_call(
+        body,
+        grid=(array.shape[0] // block.block_shape[0],),
+        in_specs=[block],
+        out_specs=block,
+        out_shape=shape(array.shape, BF16),
+        name="rounded",
+    )(array)
 
 
 def whole_sum(unit, n):
@@ -626,8 +773,9 @@
         self.apart *= 2
         return True
 
-    def add(self, after):
-        self.values = add_up([self.values, self.came], after)
+    def add(self, after, long=False):
+        if self.came is not None:
+            self.values, self.came = add_up([self.values, self.came], after, long), None
         return [self.values]
 
 
@@ -692,24 +840,27 @@
         queue = [] if straight else line.units
 
         def pump(after, *carried):
-            return (after, *carried) if straight else line.pump(after, carried)
-
-        def forward(i, held, after):
+            if straight or line.step == line.count + line.LAG:
+                return (after, *carried)
+            return line.pump(after, carried)
+
+        def forward(start, size, held, after, carried=()):
             result = forward_rows(
-                starts[i], size, unit, layer_input, lengths, flag, gains, w_three, b_qkv[:, None, :], w_in, vec(b_in),
-                vec(b_dense + b_out), w_dense, w_out, tables, held, after,
+                start, size, unit, layer_input, lengths, flag, gains, w_three, b_qkv, w_in, b_in, (b_dense, b_out),
+                w_dense, w_out, tables, held, after, carried,
             )
-            queue.extend(result[6:-1])
-            return result[:6], result[-1:]
-
-        held, after = forward(0, None, [])
+            parts = size // unit
+            queue.extend(result[6 : 6 + parts])
+            return result[:6], [result[6 + parts]], result[7 + parts :]
+
+        held, after, _ = forward(0, size, None, [])
         if not straight:
             line.send(0, queue[0])
+        held, after, (queue[1],) = forward(size, size, held, [], [queue[1]])
+        if not straight:
             line.send(1, queue[1])
-        held, after = forward(1, held, [])
         cotan, b_out_grad = mask_rows(lengths, grad_out, after)
-        held, after = forward(2, held, pump([b_out_grad])[0])
-        held, after = forward(3, held, pump(after)[0])
+        held, after, _ = forward(2 * size, rows - 2 * size, held, pump([b_out_grad])[0])
         a_one, a_two, qkv, mixed, hidden, slope = held
 
         core = lax.rem(lax.axis_index("dp"), 2).astype(jnp.int32).reshape(1)
@@ -717,12 +868,12 @@
         pairs = [(i, i ^ 1) for i in range(dp)]
         groups = [[2 * i + c for i in range(blocks)] for c in range(2)]
 
-        def other_half(name, lefts, right, slide_left, after):
-            half, token = pair_product(lefts, right, slide_left, 1 - core, None, blocks, after, name)
+        def other_half(name, lefts, right, slide_left, after, long=False):
+            half, token = pair_product(lefts, right, slide_left, 1 - core, None, blocks, after, name, long)
             return half, [token]
 
-        def own_half(name, lefts, right, slide_left, came, after):
-            half, token = pair_product(lefts, right, slide_left, core, came, blocks, after, name)
+        def own_half(name, lefts, right, slide_left, came, after, long=False):
+            half, token = pair_product(lefts, right, slide_left, core, came, blocks, after, name, long)
             return half, [token]
 
         def swap(half):
@@ -738,16 +889,14 @@
         dqkv, b_qkv_grad = attend_back(lengths, qkv, cotan, w_dense, tables, after)
         qkv_parts = ([a_one], dqkv, True)
         out_half, after = own_half("w_out_own", *out_parts, came_out, pump([b_qkv_grad])[0])
-        half, after = other_half("w_qkv_other", *qkv_parts, after)
-        after, out_half, half = pump(after, out_half, half)
+        after, out_half = pump(after, out_half)
         out_grads = over_chips(out_half)
-        came_qkv = swap(half)
 
         dhpre, smalls, biases = None, [], []
 
         def backward(i, after):
             nonlocal dhpre
-            dhpre, small, bias, *dx = backward_rows(
+            dhpre, *dx, small, bias = backward_rows(
                 starts[i], size, unit, layer_input, flag, cotan, slope, dqkv, w_three, w_in, w_out, gains, dhpre, after
             )
             queue.extend(dx)
@@ -756,26 +905,31 @@
             return [bias]
 
         after = backward(0, after)
-        qkv_half, after = own_half("w_qkv_own", *qkv_parts, came_qkv, pump(after)[0])
+        after = backward(1, pump(after)[0])
+        after = backward(2, pump(after)[0])
+        after = backward(3, pump(after)[0])
+
+        small = SmallSum(add_up(smalls, after), "tensor", tp)
+        after = [small.values]
+        more = small.exchange()
+        half, after = other_half("w_qkv_other", *qkv_parts, pump(after)[0])
+        after, half = pump(after, half)
+        came_qkv = swap(half)
+        in_parts = ([a_two], dhpre[None], True)
+        half, after = other_half("w_in_other", *in_parts, after, True)
+        after, half = pump(after, half)
+        came_in = swap(half)
+        after = small.add(after)
+        more = more and small.exchange()
+        qkv_half, after = own_half("w_qkv_own", *qkv_parts, came_qkv, after, True)
         after, qkv_half = pump(after, qkv_half)
         qkv_grads = over_chips(qkv_half)
-        after = backward(1, after)
-        after = backward(2, pump(after)[0])
-        after = backward(3, pump(after)[0])
-        in_parts = ([a_two], dhpre[None], True)
-        half, after = other_half("w_in_other", *in_parts, pump(after)[0])
-        after, half = pump(after, half)
-        came_in = swap(half)
-
-        small = SmallSum(add_up(smalls, after, True), "tensor", tp)
-        if small.exchange():
-            (after,) = pump([small.values])
-            after = small.add(after)
-        in_half, after = own_half("w_in_own", *in_parts, came_in, after)
+        in_half, after = own_half("w_in_own", *in_parts, came_in, after, True)
         after, in_half = pump(after, in_half)
         in_grads = over_chips(in_half)
-        while small.exchange():
-            (after,) = pump(after)
+        after = small.add(after, True)
+        while more and small.exchange():
+            after = pump(pump(after)[0])[0]
             after = small.add(after)
         flat = jnp.concatenate(
             [small.values[:4].reshape(-1), b_out_grad.reshape(-1), sum(biases).reshape(-1), b_qkv_grad.reshape(-1)]
@@ -784,6 +938,8 @@
         while small.exchange():
             (after,) = pump(after)
             after = small.add(after)
+        w_out_grad, w_dense_grad = split_rows(out_grads[0], units, after)
+        after = [w_dense_grad]
         while not straight and line.step < line.count + line.LAG:
             (after,) = pump(after)
         flat = small.values.reshape(-1)
@@ -792,14 +948,13 @@
         )
         b_in_grad = flat[5 * width : 5 * width + units]
         b_qkv_grad = flat[5 * width + units :].reshape(3, columns)
-        w_out_grad, w_dense_grad = out_grads[0, :units], out_grads[0, units:]
         w_qkv_grad = jnp.transpose(qkv_grads, (1, 0, 2))
         w_in_grad = in_grads[0]
 
         if straight:
             totals = [whole_sum(one, tp) for one in queue]
             first, second = jnp.concatenate(totals[:each]), jnp.concatenate(totals[each:])
-            outs = [first.astype(BF16), second.astype(BF16)]
+            outs = [rounded(first), rounded(second)]
         layer_output, input_grad = outs
         return (
             layer_output,

time: 535 us -> 506 us (0.946)
  local copies, waits for them, and re-layouts: 40.9 us -> 7.84 us
  waiting for transfers between devices: 93.3 us -> 77.9 us
  Pallas kernels: 276 us -> 287 us
  starting transfers between devices: 99.5 us -> 109 us
    unnamed x177 -> x91, local copies, waits for them, and re-layouts: 34 us -> 6.6 us
    ppermute x5, waiting for transfers between devices: 24.5 us -> 1.24 us  [exchange(): lax.ppermute(self.values, self.axis, [(i, i ^ self.apart) for i in range(...]
    ppermute x19, starting transfers between devices: 66 us -> 84.2 us  [send(): self.came[step] = lax.ppermute(operand, 'tensor', pairs)]
    ppermute x5, starting transfers between devices: 14.5 us -> 4.36 us  [exchange(): lax.ppermute(self.values, self.axis, [(i, i ^ self.apart) for i in range(...]
    unnamed x6, waiting for transfers between devices: 0.09 us -> 9.97 us
  transfers between devices with their start and end apart: 46 -> 46, of which waited for: 9 -> 6; matrix products, arithmetic and copies ran while one was open for 1% -> 0% of each run, Pallas kernels for 50% -> 55%
where the time goes in v2:
time: 506 us; the launch traced here: 498 us
  Pallas kernels  287 us (57%)
  starting transfers between devices  109 us (22%)
  waiting for transfers between devices  77.9 us (15%)
  between operations  15.9 us (3%)
  local copies, waits for them, and re-layouts  7.84 us (2%)
    ppermute x19, starting transfers between devices, send(): self.came[step] = lax.ppermute(operand, 'tensor', pairs)  84.2 us
    pallas_call x4, Pallas kernels, backward_rows(): pl.pallas_call(body, grid=(1,), in_specs=specs, out_specs=[HBM] * (1 + pa...  67.1 us
    ppermute x19, waiting for transfers between devices, send(): self.came[step] = lax.ppermute(operand, 'tensor', pairs)  66.7 us
    pallas_call x6, Pallas kernels, pair_product(): pl.pallas_call(body, grid_spec=pltpu.PrefetchScalarGridSpec(num_scalar_pr...  62.4 us
    pallas_call x3, Pallas kernels, forward_rows(): pl.pallas_call(body, grid=(1,), in_specs=specs, out_specs=[HBM] * (6 + pa...  55.4 us
    pallas_call x19, Pallas kernels, take_in(): pl.pallas_call(body, in_specs=specs, out_specs=out_specs, out_shape=outs,...  45.7 us
    pallas_call x16, Pallas kernels, pass_on(): pl.pallas_call(body, in_specs=[SMEM] + [VMEM] * (2 + len(more)) + [HBM] *...  27.7 us
    ppermute x16, starting transfers between devices, pump(): self.met[step] = lax.ppermute(held, 'tensor', [(1, 2), (2, 1)])  20 us
  transfers between devices with their start and end apart: 46, of which 6 were waited for; matrix products, arithmetic and copies ran while one was open for 0% of the time, Pallas kernels for 55%

profile of v2, /device:TPU:0, one launch (start us, length us, event | category | flops | bytes accessed | tf_op | source)
XLA Modules:
  0.0 497.7 jit_solution(10600726739868306578)
XLA Ops:
  8.0 14.9 %forward_rows.3 = (bf16[1024,2048]{1,0:T(8,128)(2,1)}, bf16[1024,2048]{1,0:T(8,128)(2,1)}, bf16[3,1024,512]{2,1,0:T(8,128)(2,1)}, bf16[1024,512]{1,0:T(8,128)(2,...) custom-call(s32[1]{0:T(128)S(6)} %copy.106.refs_0_.len_ref, ...), custom_call_target="tpu_custom_call" | custom-call | flops 40000000000 | bytes 35651584 | tf_op jit(solution)/shard_map/forward_rows/pallas_call | solution.py:272
  22.8 5.2 %collective-permute-start.1 = (f32[128,2048]{1,0:T(8,128)}, f32[128,2048]{1,0:T(8,128)S(1)}, u32[]{:S(2)}, u32[]{:S(2)}) collective-permute-start(f32[128,2048]{1,0:T(8,128)} %get-tuple-element.133.refs_2_), channel_id=1, source_target_pairs={{0,1},{3,2},{4,5},{7,6},{8,9},{11,10},{12,13},{15,14},{16,17},{19,... | collective-permute-start | bytes 3145736 | tf_op jit(solution)/shard_map/ppermute | solution.py:741
  28.1 14.8 %forward_rows.4 = (bf16[1024,2048]{1,0:T(8,128)(2,1)}, bf16[1024,2048]{1,0:T(8,128)(2,1)}, bf16[3,1024,512]{2,1,0:T(8,128)(2,1)}, bf16[1024,512]{1,0:T(8,128)(2,...) custom-call(s32[1]{0:T(128)S(6)} %copy.106.refs_0_.len_ref, ...), custom_call_target="tpu_custom_call", output_to_operand_aliasing={{0}: (18, {}), {1}: (19, {}), {2}: (20, {}), {3}: (21, {}),... | custom-call | flops 40000000000 | bytes 35651584 | tf_op jit(solution)/shard_map/forward_rows/pallas_call | solution.py:272
  46.5 5.1 %mask_rows.1 = (bf16[1024,2048]{1,0:T(8,128)(2,1)}, f32[1,2048]{1,0:T(1,128)S(1)}) custom-call(s32[1]{0:T(128)S(6)} %copy.106.refs_0_.len_ref, bf16[1024,2048]{1,0:T(8,128)(2,1)} %refs_1_.1, f32[8,128]{1,0:T(8,128)S(1)} %get-tuple-element.134.refs_2_), custom_call_target="tpu_custom_call" | custom-call | flops 40000000000 | bytes 8388608 | tf_op jit(solution)/shard_map/mask_rows/pallas_call | solution.py:311
  53.5 25.8 %forward_rows.5 = (bf16[1024,2048]{1,0:T(8,128)(2,1)}, bf16[1024,2048]{1,0:T(8,128)(2,1)}, bf16[3,1024,512]{2,1,0:T(8,128)(2,1)}, bf16[1024,512]{1,0:T(8,128)(2,...) custom-call(s32[1]{0:T(128)S(6)} %copy.106.refs_0_.len_ref, ...), custom_call_target="tpu_custom_call", output_to_operand_aliasing={{0}: (18, {}), {1}: (19, {}), {2}: (20, {}), {3}: (21, {}),... | custom-call | flops 40000000000 | bytes 46137344 | tf_op jit(solution)/shard_map/forward_rows/pallas_call | solution.py:272
  83.1 6.8 %collective-permute-start.6 = (f32[128,2048]{1,0:T(8,128)}, f32[128,2048]{1,0:T(8,128)}, u32[]{:S(2)}, u32[]{:S(2)}) collective-permute-start(f32[128,2048]{1,0:T(8,128)} %pass_on.16.refs_3_), channel_id=1, source_target_pairs={{0,1},{3,2},{1,0},{2,3},{4,5},{7,6},{5,4},{6,7},{8,9},{11,10},{9,8... | collective-permute-start | bytes 3145736 | tf_op jit(solution)/shard_map/ppermute | solution.py:741
  89.9 10.8 %w_out_other.1 = (f32[4,1,2560,256]{3,2,1,0:T(8,128)}, f32[8,128]{1,0:T(8,128)S(1)}) custom-call(s32[1]{0:T(128)S(6)} %sub.2._, bf16[1024,2048]{1,0:T(8,128)(2,1)} %get-tuple-element.138.refs_0_, bf16[1024,512]{1,0:T(8,128)(2,1)} %get-tuple-element.139.refs_1_, bf16[1,1024,2048]{2,1,0:T(8,128)(2,1)} %bitcast.80, f32[128,2048]{1,0:T(8,128)} %pass_on.16.refs_3_), custom_call_target="tpu_custom_call" | custom-call | flops 40000000000 | bytes 19922944 | tf_op jit(solution)/shard_map/w_out_other/pallas_call | solution.py:355
  105.8 9.6 %collective-permute-start.5 = (f32[128,2048]{1,0:T(8,128)}, f32[128,2048]{1,0:T(8,128)}, u32[]{:S(2)}, u32[]{:S(2)}) collective-permute-start(f32[128,2048]{1,0:T(8,128)} %get-tuple-element.145.refs_0_.refs_3_), channel_id=1, source_target_pairs={{0,1},{3,2},{1,0},{2,3},{4,5},{7,6},{5,4},{6,7},{8,9},{11,10},{9,8... | collective-permute-start | bytes 3145736 | tf_op jit(solution)/shard_map/ppermute | solution.py:741
  115.5 15.3 %attend_back.1 = (bf16[3,1024,512]{2,1,0:T(8,128)(2,1)}, f32[3,1,512]{2,1,0:T(1,128)S(1)}) custom-call(s32[1]{0:T(128)S(6)} %copy.106.refs_0_.len_ref, bf16[3,1024,512]{2,1,0:T(8,128)(2,1)} %get-tuple-element.146.q_ref.k_ref.v_ref, bf16[3,1024,512]{2,1,0:T(8,128)(2,1)} %get-tuple-element.146.q_ref.k_ref.v_ref, ...), custom_call_target="tpu_custom_call" | custom-call | flops 299999985664 | bytes 11534336 | tf_op jit(solution)/shard_map/attend_back/pallas_call | solution.py:410
  138.4 13.3 %w_out_own.1 = (f32[4,1,2560,256]{3,2,1,0:T(8,128)}, f32[8,128]{1,0:T(8,128)S(1)}) custom-call(s32[1]{0:T(128)} %bitcast.10._, bf16[1024,2048]{1,0:T(8,128)(2,1)} %get-tuple-element.138.refs_0_, bf16[1024,512]{1,0:T(8,128)(2,1)} %get-tuple-element.139.refs_1_, bf16[1,1024,2048]{2,1,0:T(8,128)(2,1)} %bitcast.81, ...), custom_call_target="tpu_custom_call" | custom-call | flops 40000000000 | bytes 19922944 | tf_op jit(solution)/shard_map/w_out_own/pallas_call | solution.py:355
  151.7 3.5 take_in.23
  158.8 4.1 collective-permute-start.13
  162.9 17.0 %backward_rows.4 = (bf16[1024,2048]{1,0:T(8,128)(2,1)}, f32[128,2048]{1,0:T(8,128)}, f32[128,2048]{1,0:T(8,128)}, f32[8,2048]{1,0:T(8,128)S(1)}, f32[1,2048]{1,0:T(1,128)S(1)}) custom-call(s32[2]{0:T(128)S(1)} %add_convert_fusion.refs_1_.refs_0_.flag_ref, f32[1,2048]{1,0:T(1,128)} %bitcast.69, f32[1,2048]{1,0:T(1,128)} %bitcast.76, ...), custom_call_target="tpu_custom_call" | custom-call | flops 299999985664 | bytes 31457280 | tf_op jit(solution)/shard_map/backward_rows/pallas_call | solution.py:546
  187.5 17.0 %backward_rows.5 = (bf16[1024,2048]{1,0:T(8,128)(2,1)}, f32[128,2048]{1,0:T(8,128)}, f32[128,2048]{1,0:T(8,128)}, f32[8,2048]{1,0:T(8,128)S(1)}, f32[1,2048]{1,0:T(1,128)S(1)}) custom-call(s32[2]{0:T(128)S(1)} %add_convert_fusion.refs_1_.refs_0_.flag_ref, f32[1,2048]{1,0:T(1,128)} %bitcast.70, f32[1,2048]{1,0:T(1,128)} %bitcast.77, ...), custom_call_target="tpu_custom_call", output_to_operand_aliasing={{0}: (10, {})} | custom-call | flops 40000000000 | bytes 31457280 | tf_op jit(solution)/shard_map/backward_rows/pallas_call | solution.py:546
  211.5 16.7 %backward_rows.6 = (bf16[1024,2048]{1,0:T(8,128)(2,1)}, f32[128,2048]{1,0:T(8,128)}, f32[128,2048]{1,0:T(8,128)}, f32[8,2048]{1,0:T(8,128)S(1)}, f32[1,2048]{1,0:T(1,128)S(1)}) custom-call(s32[2]{0:T(128)S(1)} %add_convert_fusion.refs_1_.refs_0_.flag_ref, f32[1,2048]{1,0:T(1,128)} %bitcast.71, f32[1,2048]{1,0:T(1,128)} %bitcast.78, ...), custom_call_target="tpu_custom_call", output_to_operand_aliasing={{0}: (10, {})} | custom-call | flops 40000000000 | bytes 31457280 | tf_op jit(solution)/shard_map/backward_rows/pallas_call | solution.py:546
  234.4 16.5 %backward_rows.7 = (bf16[1024,2048]{1,0:T(8,128)(2,1)}, f32[128,2048]{1,0:T(8,128)}, f32[128,2048]{1,0:T(8,128)}, f32[8,2048]{1,0:T(8,128)S(1)}, f32[1,2048]{1,0:T(1,128)S(1)}) custom-call(s32[2]{0:T(128)S(1)} %add_convert_fusion.refs_1_.refs_0_.flag_ref, f32[1,2048]{1,0:T(1,128)} %bitcast.72, f32[1,2048]{1,0:T(1,128)} %bitcast.79, ...), custom_call_target="tpu_custom_call", output_to_operand_aliasing={{0}: (10, {})} | custom-call | flops 40000000000 | bytes 31457280 | tf_op jit(solution)/shard_map/backward_rows/pallas_call | solution.py:546
  255.5 5.3 %collective-permute-start.18 = (f32[128,2048]{1,0:T(8,128)}, f32[128,2048]{1,0:T(8,128)}, u32[]{:S(2)}, u32[]{:S(2)}) collective-permute-start(f32[128,2048]{1,0:T(8,128)} %pass_on.23.refs_2_.refs_3_), channel_id=1, source_target_pairs={{0,1},{3,2},{1,0},{2,3},{4,5},{7,6},{5,4},{6,7},{8,9},{11,10},{9,8... | collective-permute-start | bytes 3145736 | tf_op jit(solution)/shard_map/ppermute | solution.py:741
  260.8 7.9 %w_qkv_other.1 = (f32[4,3,256,512]{3,2,1,0:T(8,128)}, f32[8,128]{1,0:T(8,128)S(1)}) custom-call(s32[1]{0:T(128)S(6)} %sub.2._, bf16[1024,2048]{1,0:T(8,128)(2,1)} %get-tuple-element.183.refs_0_, bf16[3,1024,512]{2,1,0:T(8,128)(2,1)} %get-tuple-element.157.refs_6_.refs_1_, f32[128,2048]{1,0:T(8,128)} %pass_on.23.refs_2_.refs_3_), custom_call_target="tpu_custom_call" | custom-call | flops 40000000000 | bytes 13631488 | tf_op jit(solution)/shard_map/w_qkv_other/pallas_call | solution.py:355
  274.5 10.3 %collective-permute-start.23 = (f32[128,2048]{1,0:T(8,128)}, f32[128,2048]{1,0:T(8,128)}, u32[]{:S(2)}, u32[]{:S(2)}) collective-permute-start(f32[128,2048]{1,0:T(8,128)} %get-tuple-element.191.refs_2_.refs_3_), channel_id=1, source_target_pairs={{0,1},{3,2},{1,0},{2,3},{4,5},{7,6},{5,4},{6,7},{8,9},{11,10},{9,8... | collective-permute-start | bytes 3145736 | tf_op jit(solution)/shard_map/ppermute | solution.py:741
  284.8 9.2 %w_in_other.1 = (f32[4,1,256,2048]{3,2,1,0:T(8,128)}, f32[8,128]{1,0:T(8,128)S(1)}) custom-call(s32[1]{0:T(128)S(6)} %sub.2._, bf16[1024,2048]{1,0:T(8,128)(2,1)} %get-tuple-element.186.refs_0_, bf16[1,1024,2048]{2,1,0:T(8,128)(2,1)} %bitcast.82, f32[128,2048]{1,0:T(8,128)} %get-tuple-element.191.refs_2_.refs_3_), custom_call_target="tpu_custom_call" | custom-call | flops 299999985664 | bytes 16777216 | tf_op jit(solution)/shard_map/w_in_other/pallas_call | solution.py:355
  294.1 3.5 take_in.29
  308.0 9.5 %w_qkv_own.1 = (f32[4,3,256,512]{3,2,1,0:T(8,128)}, f32[8,128]{1,0:T(8,128)S(1)}) custom-call(s32[1]{0:T(128)} %bitcast.10._, bf16[1024,2048]{1,0:T(8,128)(2,1)} %get-tuple-element.183.refs_0_, bf16[3,1024,512]{2,1,0:T(8,128)(2,1)} %get-tuple-element.157.refs_6_.refs_1_, f32[4,3,256,512]{3,2,1,0:T(8,128)} %collective-permute-done.24.refs_2_, ...), custom_call_target="tpu_custom_call" | custom-call | flops 299999985664 | bytes 13631488 | tf_op jit(solution)/shard_map/w_qkv_own/pallas_call | solution.py:355
  328.9 11.8 %w_in_own.1 = (f32[4,1,256,2048]{3,2,1,0:T(8,128)}, f32[8,128]{1,0:T(8,128)S(1)}) custom-call(s32[1]{0:T(128)} %bitcast.10._, bf16[1024,2048]{1,0:T(8,128)(2,1)} %get-tuple-element.186.refs_0_, bf16[1,1024,2048]{2,1,0:T(8,128)(2,1)} %bitcast.83, f32[4,1,256,2048]{3,2,1,0:T(8,128)} %collective-permute-done.26.refs_2_, f32[128,2048]{1,0:T(8,128)} %get-tuple-element.205.refs_3_), custom_call_target="tpu_custom_call" | custom-call | flops 299999985664 | bytes 16777216 | tf_op jit(solution)/shard_map/w_in_own/pallas_call | solution.py:355
  340.7 3.5 take_in.31
  348.6 6.0 %collective-permute-start.33 = (f32[128,2048]{1,0:T(8,128)}, f32[128,2048]{1,0:T(8,128)}, u32[]{:S(2)}, u32[]{:S(2)}) collective-permute-start(f32[128,2048]{1,0:T(8,128)} %get-tuple-element.212.refs_2_.refs_3_), channel_id=1, source_target_pairs={{0,1},{3,2},{1,0},{2,3},{4,5},{7,6},{5,4},{6,7},{8,9},{11,10},{9,8... | collective-permute-start | bytes 3145736 | tf_op jit(solution)/shard_map/ppermute | solution.py:741
  362.4 13.8 %collective-permute-start.32 = (f32[128,2048]{1,0:T(8,128)S(1)}, f32[128,2048]{1,0:T(8,128)}, u32[]{:S(2)}, u32[]{:S(2)}) collective-permute-start(f32[128,2048]{1,0:T(8,128)S(1)} %pass_on.28.refs_2_.refs_3_), channel_id=1, source_target_pairs={{0,1},{3,2},{1,0},{2,3},{4,5},{7,6},{5,4},{6,7},{8,9},{11,10},{9,8... | collective-permute-start | bytes 3145736 | tf_op jit(solution)/shard_map/ppermute | solution.py:741
  385.1 14.8 %collective-permute-done.32.refs_1_ = f32[128,2048]{1,0:T(8,128)} collective-permute-done((f32[128,2048]{1,0:T(8,128)S(1)}, f32[128,2048]{1,0:T(8,128)}, u32[]{:S(2)}, u32[]{:S(2)}) %collective-permute-start.32) | collective-permute-done | bytes 1048608 | tf_op jit(solution)/shard_map/ppermute | solution.py:741
  408.7 4.9 split_rows.1
  420.8 14.4 %collective-permute-done.42.refs_1_ = f32[128,2048]{1,0:T(8,128)} collective-permute-done((f32[128,2048]{1,0:T(8,128)S(1)}, f32[128,2048]{1,0:T(8,128)}, u32[]{:S(2)}, u32[]{:S(2)}) %collective-permute-start.42) | collective-permute-done | bytes 1048608 | tf_op jit(solution)/shard_map/ppermute | solution.py:741
  438.5 19.2 %collective-permute-done.41.refs_1_ = f32[128,2048]{1,0:T(8,128)} collective-permute-done((f32[128,2048]{1,0:T(8,128)S(1)}, f32[128,2048]{1,0:T(8,128)}, u32[]{:S(2)}, u32[]{:S(2)}) %collective-permute-start.41) | collective-permute-done | bytes 1048608 | tf_op jit(solution)/shard_map/ppermute | solution.py:741
  459.9 18.1 %collective-permute-done.40.refs_1_ = f32[128,2048]{1,0:T(8,128)} collective-permute-done((f32[128,2048]{1,0:T(8,128)S(1)}, f32[128,2048]{1,0:T(8,128)}, u32[]{:S(2)}, u32[]{:S(2)}) %collective-permute-start.40) | collective-permute-done | bytes 1048608 | tf_op jit(solution)/shard_map/ppermute | solution.py:741
  480.3 9.9 %reduce-scatter.14.cloned.1.call-done = f32[1,1,256,2048]{3,2,1,0:T(8,128)} async-done(((f32[4,1,256,2048]{3,2,1,0:T(8,128)}), f32[1,1,256,2048]{3,2,1,0:T(8,128)}) %reduce-scatter.14.cloned.1.call-update) | async-done | bytes 2097168
  (219 shorter events, 123.3 us)
Async XLA Ops:
  7.2 401.5 %reduce-scatter.10.cloned.1.call-start = ((), (), s32[]{:S(2)}) async-start(), calls=%async_computation.3 | async-start | bytes 13107200
  22.8 28.8 %collective-permute-start.1 = (f32[128,2048]{1,0:T(8,128)}, f32[128,2048]{1,0:T(8,128)S(1)}, u32[]{:S(2)}, u32[]{:S(2)}) collective-permute-start(f32[128,2048]{1,0:T(8,128)} %get-tuple-element.133.refs_2_), channel_id=1, source_target_pairs={{0,1},{3,2},{4,5},{7,6},{8,9},{11,10},{12,13},{15,14},{16,17},{19,... | collective-permute-start | bytes 3145736 | tf_op jit(solution)/shard_map/ppermute | solution.py:741
  42.8 36.5 %collective-permute-start = (f32[128,2048]{1,0:T(8,128)}, f32[128,2048]{1,0:T(8,128)}, u32[]{:S(2)}, u32[]{:S(2)}) collective-permute-start(f32[128,2048]{1,0:T(8,128)} %get-tuple-element.126.refs_2_), channel_id=1, source_target_pairs={{0,1},{3,2},{4,5},{7,6},{8,9},{11,10},{12,13},{15,14},{16,17},{19,... | collective-permute-start | bytes 3145736 | tf_op jit(solution)/shard_map/ppermute | solution.py:741
  45.1 55.5 %collective-permute-start.4 = (f32[128,2048]{1,0:T(8,128)}, f32[128,2048]{1,0:T(8,128)S(1)}, u32[]{:S(2)}, u32[]{:S(2)}) collective-permute-start(f32[128,2048]{1,0:T(8,128)} %get-tuple-element.143.refs_2_), channel_id=1, source_target_pairs={{0,1},{3,2},{4,5},{7,6},{8,9},{11,10},{12,13},{15,14},{16,17},{19,... | collective-permute-start | bytes 3145736 | tf_op jit(solution)/shard_map/ppermute | solution.py:741
  52.3 29.1 %collective-permute-start.3 = (f32[128,2048]{1,0:T(8,128)S(1)}, f32[128,2048]{1,0:T(8,128)S(1)}, u32[]{:S(2)}, u32[]{:S(2)}) collective-permute-start(f32[128,2048]{1,0:T(8,128)S(1)} %take_in.19.refs_24_.held_ref), channel_id=1, source_target_pairs={{1,2},{2,1},{5,6},{6,5},{9,10},{10,9},{13,14},{14,13},{17,18},{18,... | collective-permute-start | bytes 3145736 | tf_op jit(solution)/shard_map/ppermute | solution.py:750
  83.1 47.7 %collective-permute-start.6 = (f32[128,2048]{1,0:T(8,128)}, f32[128,2048]{1,0:T(8,128)}, u32[]{:S(2)}, u32[]{:S(2)}) collective-permute-start(f32[128,2048]{1,0:T(8,128)} %pass_on.16.refs_3_), channel_id=1, source_target_pairs={{0,1},{3,2},{1,0},{2,3},{4,5},{7,6},{5,4},{6,7},{8,9},{11,10},{9,8... | collective-permute-start | bytes 3145736 | tf_op jit(solution)/shard_map/ppermute | solution.py:741
  102.3 31.7 %collective-permute-start.8 = (f32[128,2048]{1,0:T(8,128)}, f32[128,2048]{1,0:T(8,128)}, u32[]{:S(2)}, u32[]{:S(2)}) collective-permute-start(f32[128,2048]{1,0:T(8,128)} %take_in.21.refs_2_.held_ref), channel_id=1, source_target_pairs={{1,2},{2,1},{5,6},{6,5},{9,10},{10,9},{13,14},{14,13},{17,18},{18,... | collective-permute-start | bytes 3145736 | tf_op jit(solution)/shard_map/ppermute | solution.py:750
  105.8 45.8 %collective-permute-start.5 = (f32[128,2048]{1,0:T(8,128)}, f32[128,2048]{1,0:T(8,128)}, u32[]{:S(2)}, u32[]{:S(2)}) collective-permute-start(f32[128,2048]{1,0:T(8,128)} %get-tuple-element.145.refs_0_.refs_3_), channel_id=1, source_target_pairs={{0,1},{3,2},{1,0},{2,3},{4,5},{7,6},{5,4},{6,7},{8,9},{11,10},{9,8... | collective-permute-start | bytes 3145736 | tf_op jit(solution)/shard_map/ppermute | solution.py:741
  136.7 43.3 %collective-permute-start.10 = (f32[128,2048]{1,0:T(8,128)}, f32[128,2048]{1,0:T(8,128)}, u32[]{:S(2)}, u32[]{:S(2)}) collective-permute-start(f32[128,2048]{1,0:T(8,128)} %pass_on.18.refs_4_.refs_3_), channel_id=1, source_target_pairs={{0,1},{3,2},{1,0},{2,3},{4,5},{7,6},{5,4},{6,7},{8,9},{11,10},{9,8... | collective-permute-start | bytes 3145736 | tf_op jit(solution)/shard_map/ppermute | solution.py:741
  155.2 28.7 %collective-permute-start.9 = (f32[128,2048]{1,0:T(8,128)}, f32[128,2048]{1,0:T(8,128)}, u32[]{:S(2)}, u32[]{:S(2)}) collective-permute-start(f32[128,2048]{1,0:T(8,128)} %get-tuple-element.153.refs_2_.held_ref), channel_id=1, source_target_pairs={{1,2},{2,1},{5,6},{6,5},{9,10},{10,9},{13,14},{14,13},{17,18},{18,... | collective-permute-start | bytes 3145736 | tf_op jit(solution)/shard_map/ppermute | solution.py:750
  158.5 321.7 %reduce-scatter.12.cloned.1.call-start = ((), (), s32[]{:S(2)}) async-start(), calls=%async_computation.4 | async-start | bytes 7864320
  158.8 45.7 %collective-permute-start.13 = (f32[128,2048]{1,0:T(8,128)}, f32[128,2048]{1,0:T(8,128)}, u32[]{:S(2)}, u32[]{:S(2)}) collective-permute-start(f32[128,2048]{1,0:T(8,128)} %get-tuple-element.160.refs_10_.refs_3_), channel_id=1, source_target_pairs={{0,1},{3,2},{1,0},{2,3},{4,5},{7,6},{5,4},{6,7},{8,9},{11,10},{9,8... | collective-permute-start | bytes 3145736 | tf_op jit(solution)/shard_map/ppermute | solution.py:741
  182.7 25.4 %collective-permute-start.14 = (f32[128,2048]{1,0:T(8,128)S(1)}, f32[128,2048]{1,0:T(8,128)S(1)}, u32[]{:S(2)}, u32[]{:S(2)}) collective-permute-start(f32[128,2048]{1,0:T(8,128)S(1)} %get-tuple-element.162.refs_1_.held_ref), channel_id=1, source_target_pairs={{1,2},{2,1},{5,6},{6,5},{9,10},{10,9},{13,14},{14,13},{17,18},{18,... | collective-permute-start | bytes 3145736 | tf_op jit(solution)/shard_map/ppermute | solution.py:750
  185.9 42.2 %collective-permute-start.12 = (f32[128,2048]{1,0:T(8,128)S(1)}, f32[128,2048]{1,0:T(8,128)S(1)}, u32[]{:S(2)}, u32[]{:S(2)}) collective-permute-start(f32[128,2048]{1,0:T(8,128)S(1)} %pass_on.20.refs_11_.refs_3_), channel_id=1, source_target_pairs={{0,1},{3,2},{1,0},{2,3},{4,5},{7,6},{5,4},{6,7},{8,9},{11,10},{9,8... | collective-permute-start | bytes 3145736 | tf_op jit(solution)/shard_map/ppermute | solution.py:741
  208.9 42.7 %collective-permute-start.16 = (f32[128,2048]{1,0:T(8,128)S(1)}, f32[128,2048]{1,0:T(8,128)S(1)}, u32[]{:S(2)}, u32[]{:S(2)}) collective-permute-start(f32[128,2048]{1,0:T(8,128)S(1)} %pass_on.21.refs_11_.refs_3_), channel_id=1, source_target_pairs={{0,1},{3,2},{1,0},{2,3},{4,5},{7,6},{5,4},{6,7},{8,9},{11,10},{9,8... | collective-permute-start | bytes 3145736 | tf_op jit(solution)/shard_map/ppermute | solution.py:741
  231.3 37.4 %collective-permute-start.19 = (f32[128,2048]{1,0:T(8,128)S(1)}, f32[128,2048]{1,0:T(8,128)S(1)}, u32[]{:S(2)}, u32[]{:S(2)}) collective-permute-start(f32[128,2048]{1,0:T(8,128)S(1)} %pass_on.22.refs_11_.refs_3_), channel_id=1, source_target_pairs={{0,1},{3,2},{1,0},{2,3},{4,5},{7,6},{5,4},{6,7},{8,9},{11,10},{9,8... | collective-permute-start | bytes 3145736 | tf_op jit(solution)/shard_map/ppermute | solution.py:741
  251.6 53.8 %collective-permute-start.25 = (f32[8,2048]{1,0:T(8,128)}, f32[8,2048]{1,0:T(8,128)}, u32[]{:S(2)}, u32[]{:S(2)}) collective-permute-start(f32[8,2048]{1,0:T(8,128)} %add_up.6.refs_5_.refs_0_), channel_id=1, source_target_pairs={{0,1},{1,0},{2,3},{3,2},{4,5},{5,4},{6,7},{7,6},{8,9},{9,8},{10,11... | collective-permute-start | bytes 196616 | tf_op jit(solution)/shard_map/ppermute | solution.py:772
  255.5 38.6 %collective-permute-start.18 = (f32[128,2048]{1,0:T(8,128)}, f32[128,2048]{1,0:T(8,128)}, u32[]{:S(2)}, u32[]{:S(2)}) collective-permute-start(f32[128,2048]{1,0:T(8,128)} %pass_on.23.refs_2_.refs_3_), channel_id=1, source_target_pairs={{0,1},{3,2},{1,0},{2,3},{4,5},{7,6},{5,4},{6,7},{8,9},{11,10},{9,8... | collective-permute-start | bytes 3145736 | tf_op jit(solution)/shard_map/ppermute | solution.py:741
  271.1 28.4 %collective-permute-start.21 = (f32[128,2048]{1,0:T(8,128)}, f32[128,2048]{1,0:T(8,128)}, u32[]{:S(2)}, u32[]{:S(2)}) collective-permute-start(f32[128,2048]{1,0:T(8,128)} %get-tuple-element.190.refs_2_.held_ref), channel_id=1, source_target_pairs={{1,2},{2,1},{5,6},{6,5},{9,10},{10,9},{13,14},{14,13},{17,18},{18,... | collective-permute-start | bytes 3145736 | tf_op jit(solution)/shard_map/ppermute | solution.py:750
  274.5 43.0 %collective-permute-start.23 = (f32[128,2048]{1,0:T(8,128)}, f32[128,2048]{1,0:T(8,128)}, u32[]{:S(2)}, u32[]{:S(2)}) collective-permute-start(f32[128,2048]{1,0:T(8,128)} %get-tuple-element.191.refs_2_.refs_3_), channel_id=1, source_target_pairs={{0,1},{3,2},{1,0},{2,3},{4,5},{7,6},{5,4},{6,7},{8,9},{11,10},{9,8... | collective-permute-start | bytes 3145736 | tf_op jit(solution)/shard_map/ppermute | solution.py:741
  297.6 25.0 %collective-permute-start.27 = (f32[128,2048]{1,0:T(8,128)}, f32[128,2048]{1,0:T(8,128)}, u32[]{:S(2)}, u32[]{:S(2)}) collective-permute-start(f32[128,2048]{1,0:T(8,128)} %get-tuple-element.196.refs_2_.held_ref), channel_id=1, source_target_pairs={{1,2},{2,1},{5,6},{6,5},{9,10},{10,9},{13,14},{14,13},{17,18},{18,... | collective-permute-start | bytes 3145736 | tf_op jit(solution)/shard_map/ppermute | solution.py:750
  302.2 38.5 %collective-permute-start.22 = (f32[128,2048]{1,0:T(8,128)}, f32[128,2048]{1,0:T(8,128)}, u32[]{:S(2)}, u32[]{:S(2)}) collective-permute-start(f32[128,2048]{1,0:T(8,128)} %get-tuple-element.197.refs_2_.refs_3_), channel_id=1, source_target_pairs={{0,1},{3,2},{1,0},{2,3},{4,5},{7,6},{5,4},{6,7},{8,9},{11,10},{9,8... | collective-permute-start | bytes 3145736 | tf_op jit(solution)/shard_map/ppermute | solution.py:741
  306.8 47.8 %collective-permute-start.30 = (f32[8,2048]{1,0:T(8,128)}, f32[8,2048]{1,0:T(8,128)}, u32[]{:S(2)}, u32[]{:S(2)}) collective-permute-start(f32[8,2048]{1,0:T(8,128)} %add_up.7.refs_3_.refs_0_), channel_id=1, source_target_pairs={{0,2},{1,3},{2,0},{3,1},{4,6},{5,7},{6,4},{7,5},{8,10},{9,11},{10,... | collective-permute-start | bytes 196616 | tf_op jit(solution)/shard_map/ppermute | solution.py:772
  321.0 24.9 %collective-permute-start.31 = (f32[128,2048]{1,0:T(8,128)}, f32[128,2048]{1,0:T(8,128)}, u32[]{:S(2)}, u32[]{:S(2)}) collective-permute-start(f32[128,2048]{1,0:T(8,128)} %get-tuple-element.204.refs_2_.held_ref), channel_id=1, source_target_pairs={{1,2},{2,1},{5,6},{6,5},{9,10},{10,9},{13,14},{14,13},{17,18},{18,... | collective-permute-start | bytes 3145736 | tf_op jit(solution)/shard_map/ppermute | solution.py:750
  325.3 30.3 %collective-permute-start.29 = (f32[128,2048]{1,0:T(8,128)}, f32[128,2048]{1,0:T(8,128)}, u32[]{:S(2)}, u32[]{:S(2)}) collective-permute-start(f32[128,2048]{1,0:T(8,128)} %get-tuple-element.205.refs_3_), channel_id=1, source_target_pairs={{0,1},{3,2},{1,0},{2,3},{4,5},{7,6},{5,4},{6,7},{8,9},{11,10},{9,8... | collective-permute-start | bytes 3145736 | tf_op jit(solution)/shard_map/ppermute | solution.py:741
  328.8 161.3 %reduce-scatter.14.cloned.1.call-start = ((), (), s32[]{:S(2)}) async-start(), calls=%async_computation.5 | async-start | bytes 10485760
  348.6 30.6 %collective-permute-start.33 = (f32[128,2048]{1,0:T(8,128)}, f32[128,2048]{1,0:T(8,128)}, u32[]{:S(2)}, u32[]{:S(2)}) collective-permute-start(f32[128,2048]{1,0:T(8,128)} %get-tuple-element.212.refs_2_.refs_3_), channel_id=1, source_target_pairs={{0,1},{3,2},{1,0},{2,3},{4,5},{7,6},{5,4},{6,7},{8,9},{11,10},{9,8... | collective-permute-start | bytes 3145736 | tf_op jit(solution)/shard_map/ppermute | solution.py:741
  362.4 37.6 %collective-permute-start.32 = (f32[128,2048]{1,0:T(8,128)S(1)}, f32[128,2048]{1,0:T(8,128)}, u32[]{:S(2)}, u32[]{:S(2)}) collective-permute-start(f32[128,2048]{1,0:T(8,128)S(1)} %pass_on.28.refs_2_.refs_3_), channel_id=1, source_target_pairs={{0,1},{3,2},{1,0},{2,3},{4,5},{7,6},{5,4},{6,7},{8,9},{11,10},{9,8... | collective-permute-start | bytes 3145736 | tf_op jit(solution)/shard_map/ppermute | solution.py:741
  381.8 24.9 %collective-permute-start.39 = (f32[128,2048]{1,0:T(8,128)S(1)}, f32[128,2048]{1,0:T(8,128)S(1)}, u32[]{:S(2)}, u32[]{:S(2)}) collective-permute-start(f32[128,2048]{1,0:T(8,128)S(1)} %get-tuple-element.216.refs_0_.held_ref), channel_id=1, source_target_pairs={{1,2},{2,1},{5,6},{6,5},{9,10},{10,9},{13,14},{14,13},{17,18},{18,... | collective-permute-start | bytes 3145736 | tf_op jit(solution)/shard_map/ppermute | solution.py:750
  405.4 29.9 %collective-permute-start.42 = (f32[128,2048]{1,0:T(8,128)S(1)}, f32[128,2048]{1,0:T(8,128)}, u32[]{:S(2)}, u32[]{:S(2)}) collective-permute-start(f32[128,2048]{1,0:T(8,128)S(1)} %pass_on.29.refs_2_), channel_id=1, source_target_pairs={{1,0},{2,3},{5,4},{6,7},{9,8},{10,11},{13,12},{14,15},{17,16},{18,... | collective-permute-start | bytes 3145736 | tf_op jit(solution)/shard_map/ppermute | solution.py:741
  407.3 50.4 %collective-permute-start.41 = (f32[128,2048]{1,0:T(8,128)S(1)}, f32[128,2048]{1,0:T(8,128)}, u32[]{:S(2)}, u32[]{:S(2)}) collective-permute-start(f32[128,2048]{1,0:T(8,128)S(1)} %pass_on.30.refs_2_), channel_id=1, source_target_pairs={{1,0},{2,3},{5,4},{6,7},{9,8},{10,11},{13,12},{14,15},{17,16},{18,... | collective-permute-start | bytes 3145736 | tf_op jit(solution)/shard_map/ppermute | solution.py:741
  418.3 59.8 %collective-permute-start.40 = (f32[128,2048]{1,0:T(8,128)S(1)}, f32[128,2048]{1,0:T(8,128)}, u32[]{:S(2)}, u32[]{:S(2)}) collective-permute-start(f32[128,2048]{1,0:T(8,128)S(1)} %pass_on.31.refs_4_.refs_2_), channel_id=1, source_target_pairs={{1,0},{2,3},{5,4},{6,7},{9,8},{10,11},{13,12},{14,15},{17,16},{18,... | collective-permute-start | bytes 3145736 | tf_op jit(solution)/shard_map/ppermute | solution.py:741
  (58 other events, 777.5 us)
Sparse Core Ops, SparseCore 0:
  158.6 105.2 reduce-scatter.9
  328.9 71.2 reduce-scatter.11
  403.9 86.2 reduce-scatter.13

commit v3 on v2

--- a/solution.py
+++ b/solution.py
@@ -28,6 +28,10 @@
 
 def cost(flops, nbytes, long=False):
     return pl.CostEstimate(flops=int(3e11 if long else 4e10), bytes_accessed=int(nbytes), transcendentals=0)
+
+
+def alone(flops, nbytes):
+    return pl.CostEstimate(flops=int(3e10), bytes_accessed=int(nbytes), transcendentals=0)
 
 
 def light(flops, nbytes):
@@ -320,11 +324,11 @@
     )(lengths, in_hbm(grad_out), *after)
 
 
-def pair_product(lefts, right, slide_left, parity, added, blocks, after, name, long=False):
+def pair_product(lefts, right, slide_left, parity, added, blocks, after, name, long=False, apart=2):
     rows = right.shape[-2]
     many = right.shape[0]
     left_width = sum(left.shape[1] for left in lefts)
-    block = (left_width if slide_left else right.shape[2]) // (2 * blocks)
+    block = (left_width if slide_left else right.shape[2]) // (apart * blocks)
     tall, wide = (block, right.shape[2]) if slide_left else (left_width, block)
 
     def body(_, *refs):
@@ -343,11 +347,11 @@
 
     out = pl.BlockSpec((1, many, tall, wide), lambda i, p: (i, 0, 0, 0))
     if slide_left:
-        specs = [pl.BlockSpec((rows, block), lambda i, p: (0, 2 * i + p[0]))]
+        specs = [pl.BlockSpec((rows, block), lambda i, p: (0, apart * i + p[0]))]
         specs.append(pl.BlockSpec(right.shape, lambda i, p: (0, 0, 0)))
     else:
         specs = [pl.BlockSpec(left.shape, lambda i, p: (0, 0)) for left in lefts]
-        specs.append(pl.BlockSpec((many, rows, block), lambda i, p: (0, 0, 2 * i + p[0])))
+        specs.append(pl.BlockSpec((many, rows, block), lambda i, p: (0, 0, apart * i + p[0])))
     operands = [*lefts, right]
     if added is not None:
         operands.append(added)
@@ -448,9 +452,9 @@
     sends = units // piece + parts
 
     def body(*refs):
-        flag_ref, g1, g2, x_hbm, g_hbm, slope_hbm, q_hbm, w3_hbm, wi_hbm, wo_hbm = refs[:10]
-        dh_hbm, *dx_hbms, small_ref, bias_ref = refs[-16 - parts : -13]
-        x_ref, g_ref, slope_ref, q_ref, w3, wi, wo, one, two, normed_ref, dh_ref, dx_ref, sems = refs[-13:]
+        flag_ref, g1, g2, x_hbm, g_hbm, slope_hbm, q_hbm, w3, wi_hbm, wo_hbm = refs[:10]
+        dh_hbm, *dx_hbms, small_ref, bias_ref = refs[-15 - parts : -12]
+        x_ref, g_ref, slope_ref, q_ref, wi, wo, one, two, normed_ref, dh_ref, dx_ref, sems = refs[-12:]
         mine = pl.ds(start, size)
         sources = (g_hbm.at[mine], slope_hbm.at[mine], x_hbm.at[mine], q_hbm.at[:, mine])
         inward = [
@@ -468,7 +472,6 @@
             pieces.append((wi_hbm.at[here], wi.at[here]))
         stream = Stream(pieces, sems.at[pl.ds(4, steps)])
         out = Out(sems.at[pl.ds(4 + steps, sends)])
-        three = pltpu.make_async_copy(w3_hbm, w3, sems.at[4 + steps + sends])
 
         def slope_times(low, acc):
             here = slice(low, low + piece)
@@ -485,7 +488,6 @@
             if low == 0:
                 for copy in inward[2:]:
                     copy.start()
-                three.start()
                 inward[1].wait()
             acc = dot(g_ref[...], wo[low : low + piece], NT)
             if before is not None:
@@ -494,7 +496,6 @@
         slope_times(units - piece, before)
         for copy in inward[2:]:
             copy.wait()
-        three.wait()
         band = 64
         rstds = []
         for low in range(0, size, band):
@@ -534,8 +535,8 @@
         out.finish()
 
     vec = lambda n: pl.BlockSpec((1, n), lambda i: (0, 0))
-    operands = [flag, *map(in_hbm, (gains[0], gains[2], x, cotan, slope, dqkv, w_three, w_in, w_out))]
-    specs = [SMEM, vec(width), vec(width)] + [HBM] * 7
+    operands = [flag, *map(in_hbm, (gains[0], gains[2], x, cotan, slope, dqkv)), in_vmem(w_three), in_hbm(w_in), in_hbm(w_out)]
+    specs = [SMEM, vec(width), vec(width)] + [HBM] * 4 + [VMEM] + [HBM] * 2
     aliases = {}
     if held is not None:
         aliases = {len(operands): 0}
@@ -556,7 +557,6 @@
             pltpu.VMEM((size, width), BF16),
             pltpu.VMEM((size, units), BF16),
             pltpu.VMEM((3, size, columns), BF16),
-            pltpu.VMEM(w_three.shape, BF16),
             pltpu.VMEM(w_in.shape, BF16),
             pltpu.VMEM(w_out.shape, BF16),
             pltpu.VMEM((size, width), F32),
@@ -564,28 +564,37 @@
             pltpu.VMEM((size, width), F32),
             pltpu.VMEM((size, units), BF16),
             pltpu.VMEM((size, width), F32),
-            pltpu.SemaphoreType.DMA((4 + steps + sends + 1,)),
+            pltpu.SemaphoreType.DMA((4 + steps + sends,)),
         ],
         input_output_aliases=aliases,
-        compiler_params=params(46),
+        compiler_params=params(38),
         cost_estimate=cost(2 * size * width * (2 * units + 3 * columns), 2 * width * (2 * units + 3 * columns) + 16 * size * width, start == 0),
         name="backward_rows",
     )(*operands)
 
 
-def take_in(flag, unit, came, operand, out, out_at, out_shape, after):
+def take_in(flag, unit, came, operand, out, out_at, out_rows, out_shape, after, last):
     rows, width = came.shape
     has_unit, has_total = unit is not None, operand is not None
+    more = 0 if has_unit or not has_total else rows - out_rows
 
     def body(*refs):
         flag_ref, came_ref = refs[:2]
+        results = list(refs[-has_unit - has_total - (more > 0) - 2 * has_total :])
+        if has_unit:
+            held_ref = results.pop(0)
         if has_total:
-            out_ref, rounded, sem = refs[-3:]
-            rounded[...] = jnp.where(flag_ref[0] == 1, refs[2 + has_unit][...], came_ref[...]).astype(BF16)
-            copy = pltpu.make_async_copy(rounded, out_ref.at[pl.ds(out_at * rows, rows)], sem)
+            out_ref = results.pop(0)
+            rounded_ref, sem = results[-2:]
+            part = slice(0, out_rows)
+            mine_ref = refs[2 + has_unit]
+            rounded_ref[...] = jnp.where(flag_ref[0] == 1, mine_ref[part], came_ref[part]).astype(BF16)
+            copy = pltpu.make_async_copy(rounded_ref, out_ref.at[pl.ds(out_at * out_rows, out_rows)], sem)
             copy.start()
+            if more:
+                results[0][...] = jnp.where(flag_ref[0] == 1, mine_ref[out_rows:], came_ref[out_rows:])
         if has_unit:
-            refs[-4 if has_total else -1][...] = refs[2][...] + came_ref[...]
+            held_ref[...] = refs[2][...] + came_ref[...]
         if has_total:
             copy.wait()
 
@@ -601,36 +610,46 @@
         specs.append(VMEM)
         outs.append(pltpu.HBM(out_shape, BF16))
         out_specs.append(HBM)
-        scratch = [pltpu.VMEM((rows, width), BF16), pltpu.SemaphoreType.DMA]
+        scratch = [pltpu.VMEM((out_rows, width), BF16), pltpu.SemaphoreType.DMA]
         if out is not None:
             aliases = {len(operands): len(outs) - 1}
             operands.append(in_hbm(out))
             specs.append(HBM)
+        if more:
+            outs.append(shape((more, width), F32))
+            out_specs.append(VMEM)
     operands += after
     specs += [ANY] * len(after)
-    result = pl.pallas_call(
-        body,
-        in_specs=specs,
-        out_specs=out_specs,
-        out_shape=outs,
-        scratch_shapes=scratch,
-        input_output_aliases=aliases,
-        compiler_params=pltpu.CompilerParams(vmem_limit_bytes=SMALL_LIMIT),
-        cost_estimate=light(4 * rows * width, 16 * rows * width),
-        name="take_in",
-    )(*operands)
-    held = result[0] if has_unit else None
-    return held, (result[-1] if has_total else out)
-
-
-def pass_on(flag, held, met, unit, after, carried):
-    rows, width = held.shape
+    result = list(
+        pl.pallas_call(
+            body,
+            in_specs=specs,
+            out_specs=out_specs,
+            out_shape=outs,
+            scratch_shapes=scratch,
+            input_output_aliases=aliases,
+            compiler_params=pltpu.CompilerParams(vmem_limit_bytes=SMALL_LIMIT),
+            cost_estimate=(alone if last else light)(4 * rows * width, 16 * rows * width),
+            name="take_in",
+        )(*operands)
+    )
+    held = result.pop(0) if has_unit else None
+    out = result.pop(0) if has_total else out
+    return held, out, (result[0] if more else None)
+
+
+def pass_on(flag, held, met, unit, after, carried, last):
+    rows, width = (held if unit is None else unit).shape
+    both = min(rows, held.shape[0])
 
     def body(flag_ref, held_ref, met_ref, *refs):
-        total = held_ref[...] + met_ref[...]
+        out_ref = refs[-1 - len(carried)]
+        total = held_ref[:both] + met_ref[:both]
         if unit is not None:
-            total = jnp.where(flag_ref[0] == 1, total, refs[0][...])
-        refs[-1 - len(carried)][...] = total
+            total = jnp.where(flag_ref[0] == 1, total, refs[0][:both])
+        out_ref[:both] = total
+        if both < rows:
+            out_ref[both:] = refs[0][both:]
 
     more = [] if unit is None else [unit]
     return pl.pallas_call(
@@ -640,9 +659,27 @@
         out_shape=[pltpu.VMEM((rows, width), F32)] + [pltpu.HBM(c.shape, c.dtype) for c in carried],
         input_output_aliases={3 + len(more) + i: 1 + i for i in range(len(carried))},
         compiler_params=pltpu.CompilerParams(vmem_limit_bytes=SMALL_LIMIT),
-        cost_estimate=light(2 * rows * width, 16 * rows * width),
+        cost_estimate=(alone if last else light)(2 * rows * width, 16 * rows * width),
         name="pass_on",
     )(flag, in_vmem(held), in_vmem(met), *more, *map(in_hbm, carried), *after)
+
+
+def append_rows(top, bottom, after):
+    rows, width = top.shape
+
+    def body(top_ref, bottom_ref, *refs):
+        refs[-1][:rows] = top_ref[...]
+        refs[-1][rows:] = bottom_ref[...]
+
+    return pl.pallas_call(
+        body,
+        in_specs=[VMEM] * 2 + [ANY] * len(after),
+        out_specs=VMEM,
+        out_shape=shape((rows + bottom.shape[0], width), F32),
+        compiler_params=pltpu.CompilerParams(vmem_limit_bytes=SMALL_LIMIT),
+        cost_estimate=light(0, 8 * rows * width),
+        name="append_rows",
+    )(top, bottom, *after)
 
 
 def add_up(arrays, after, long=False):
@@ -658,7 +695,7 @@
         out_specs=VMEM,
         out_shape=shape(arrays[0].shape, F32),
         compiler_params=pltpu.CompilerParams(vmem_limit_bytes=SMALL_LIMIT),
-        cost_estimate=cost(0, 0, True) if long else light(0, 0),
+        cost_estimate=light(1e11, 0) if long else light(0, 0),
         name="add_up",
     )(*arrays, *after)
 
@@ -743,8 +780,9 @@
     def pump(self, after, carried=()):
         step = self.step
         self.step += 1
+        last = step >= self.count - 2
         unit = self.units[step] if step < self.count else None
-        held = self.finish(self, step - self.LAG, unit, self.came[step], after)
+        held = self.finish(self, step - self.LAG, unit, self.came[step], after, last)
         if unit is not None:
             self.held[step] = held
             self.met[step] = lax.ppermute(held, "tensor", [(1, 2), (2, 1)])
@@ -754,7 +792,9 @@
         elif step <= self.count:
             ahead = step + 2
             unit = self.units[ahead] if ahead < self.count else None
-            operand, *carried = pass_on(self.flag, self.held[step - 1], self.met[step - 1], unit, after, carried)
+            operand, *carried = pass_on(
+                self.flag, self.held[step - 1], self.met[step - 1], unit, after, carried, last
+            )
             self.send(ahead, operand)
             after = [operand]
         return after, *carried
@@ -826,13 +866,17 @@
         flag = jnp.stack([(me == 1) | (me == 2), me == 0]).astype(jnp.int32)
         outs = [None, None]
 
-        def finish(line, done, unit, came, after):
+        last = []
+
+        def finish(line, done, unit, came, after, final):
             if done < 0:
-                return take_in(flag, unit, came, None, None, 0, None, after)[0]
+                return take_in(flag, unit, came, None, None, 0, 0, None, after, final)[0]
             which, at = divmod(done, each)
-            held, outs[which] = take_in(
-                flag, unit, came, line.operands[done + line.LAG], outs[which], at, layer_input.shape, after
+            held, outs[which], more = take_in(
+                flag, unit, came, line.operands[done + line.LAG], outs[which], at, rows // each, layer_input.shape, after,
+                final,
             )
+            last[:] = [more]
             return held
 
         straight = tp != 4
@@ -860,7 +904,9 @@
         if not straight:
             line.send(1, queue[1])
         cotan, b_out_grad = mask_rows(lengths, grad_out, after)
-        held, after, _ = forward(2 * size, rows - 2 * size, held, pump([b_out_grad])[0])
+        after = [b_out_grad]
+        for start in starts[2:]:
+            held, after, _ = forward(start, size, held, pump(after)[0])
         a_one, a_two, qkv, mixed, hidden, slope = held
 
         core = lax.rem(lax.axis_index("dp"), 2).astype(jnp.int32).reshape(1)
@@ -887,7 +933,6 @@
         after, half = pump(after, half)
         came_out = swap(half)
         dqkv, b_qkv_grad = attend_back(lengths, qkv, cotan, w_dense, tables, after)
-        qkv_parts = ([a_one], dqkv, True)
         out_half, after = own_half("w_out_own", *out_parts, came_out, pump([b_qkv_grad])[0])
         after, out_half = pump(after, out_half)
         out_grads = over_chips(out_half)
@@ -905,47 +950,37 @@
             return [bias]
 
         after = backward(0, after)
-        after = backward(1, pump(after)[0])
+        zero = jnp.zeros(1, jnp.int32)
+        qkv_grads, token = pair_product([a_one], dqkv, True, zero, None, dp, pump(after)[0], "w_qkv_grad", apart=1)
+        after, qkv_grads = pump([token], qkv_grads)
+        qkv_grads = lax.psum_scatter(qkv_grads, "dp", scatter_dimension=0, tiled=True)[0]
+        after = backward(1, after)
         after = backward(2, pump(after)[0])
         after = backward(3, pump(after)[0])
 
-        small = SmallSum(add_up(smalls, after), "tensor", tp)
-        after = [small.values]
-        more = small.exchange()
-        half, after = other_half("w_qkv_other", *qkv_parts, pump(after)[0])
-        after, half = pump(after, half)
-        came_qkv = swap(half)
+        flat = jnp.concatenate(
+            [sum(smalls)[:4].reshape(-1), b_out_grad.reshape(-1), sum(biases).reshape(-1), b_qkv_grad.reshape(-1)]
+        )
+        small = SmallSum(flat.reshape(-1, 128), "dp", dp)
+        small.exchange()
         in_parts = ([a_two], dhpre[None], True)
-        half, after = other_half("w_in_other", *in_parts, after, True)
+        half, after = other_half("w_in_other", *in_parts, pump(after)[0])
         after, half = pump(after, half)
         came_in = swap(half)
-        after = small.add(after)
-        more = more and small.exchange()
-        qkv_half, after = own_half("w_qkv_own", *qkv_parts, came_qkv, after, True)
-        after, qkv_half = pump(after, qkv_half)
-        qkv_grads = over_chips(qkv_half)
-        in_half, after = own_half("w_in_own", *in_parts, came_in, after, True)
+        after = small.add(after + [out_grads], True)
+        while small.exchange():
+            after = small.add(after)
+        flat = small.values.reshape(-1)
+        norms = jnp.concatenate([flat[: 4 * width].reshape(4, width), jnp.zeros((4, width), F32)])
+        queue[-1] = append_rows(queue[-1], norms, after)
+        in_half, after = own_half("w_in_own", *in_parts, came_in, pump([queue[-1]])[0])
         after, in_half = pump(after, in_half)
         in_grads = over_chips(in_half)
-        after = small.add(after, True)
-        while more and small.exchange():
-            after = pump(pump(after)[0])[0]
-            after = small.add(after)
-        flat = jnp.concatenate(
-            [small.values[:4].reshape(-1), b_out_grad.reshape(-1), sum(biases).reshape(-1), b_qkv_grad.reshape(-1)]
-        )
-        small = SmallSum(flat.reshape(-1, 128), "dp", dp)
-        while small.exchange():
-            (after,) = pump(after)
-            after = small.add(after)
-        w_out_grad, w_dense_grad = split_rows(out_grads[0], units, after)
+        w_out_grad, w_dense_grad = split_rows(out_grads[0], units, after + [qkv_grads])
         after = [w_dense_grad]
         while not straight and line.step < line.count + line.LAG:
             (after,) = pump(after)
-        flat = small.values.reshape(-1)
-        gain_one, shift_one, gain_two, shift_two, b_out_grad = (
-            flat[i * width : (i + 1) * width] for i in range(5)
-        )
+        b_out_grad = flat[4 * width : 5 * width]
         b_in_grad = flat[5 * width : 5 * width + units]
         b_qkv_grad = flat[5 * width + units :].reshape(3, columns)
         w_qkv_grad = jnp.transpose(qkv_grads, (1, 0, 2))
@@ -953,8 +988,10 @@
 
         if straight:
             totals = [whole_sum(one, tp) for one in queue]
-            first, second = jnp.concatenate(totals[:each]), jnp.concatenate(totals[each:])
-            outs = [rounded(first), rounded(second)]
+            last = [totals[-1][unit:]]
+            totals[-1] = totals[-1][:unit]
+            outs = [rounded(jnp.concatenate(totals[:each])), rounded(jnp.concatenate(totals[each:]))]
+        gain_one, shift_one, gain_two, shift_two = (last[0][i] for i in range(4))
         layer_output, input_grad = outs
         return (
             layer_output,

time: 506 us -> 485 us (0.958)
  starting transfers between devices: 109 us -> 86.4 us
  Pallas kernels: 287 us -> 269 us
  waiting for transfers between devices: 77.9 us -> 90.1 us
  local copies, waits for them, and re-layouts: 7.84 us -> 15.5 us
    ppermute x19, starting transfers between devices: 84.2 us -> 64.3 us  [send(): self.came[step] = lax.ppermute(operand, 'tensor', pairs)]
    ppermute x19, waiting for transfers between devices: 66.7 us -> 76.8 us  [send(): self.came[step] = lax.ppermute(operand, 'tensor', pairs)]
    unnamed x6 -> x5, waiting for transfers between devices: 9.97 us -> 0.06 us
    pallas_call x4, Pallas kernels: 67.1 us -> 57.6 us  [backward_rows(): pl.pallas_call(body, grid=(1,), in_specs=specs, out_specs=[HBM] * (1 + pa...]
    reduce_scatter x0 -> x1, waiting for transfers between devices: none -> 8.55 us  [local(): lax.psum_scatter(qkv_grads, 'dp', scatter_dimension=0, tiled=True)[0]]
    unnamed x91 -> x72, local copies, waits for them, and re-layouts: 6.6 us -> 13 us
    pallas_call x19, Pallas kernels: 45.7 us -> 40.3 us  [take_in(): pl.pallas_call(body, in_specs=specs, out_specs=out_specs, out_shape=outs,...]
    pallas_call x3 -> x4, Pallas kernels: 55.4 us -> 60.5 us  [forward_rows(): pl.pallas_call(body, grid=(1,), in_specs=specs, out_specs=[HBM] * (6 + pa...]
  transfers between devices with their start and end apart: 46 -> 43, of which waited for: 6 -> 9; matrix products, arithmetic and copies ran while one was open for 0% -> 1% of each run, Pallas kernels for 55% -> 53%
where the time goes in v3:
time: 485 us; the launch traced here: 477 us
  Pallas kernels  269 us (55%)
  waiting for transfers between devices  90.1 us (19%)
  starting transfers between devices  86.4 us (18%)
  between operations  15.8 us (3%)
  local copies, waits for them, and re-layouts  15.5 us (3%)
    ppermute x19, waiting for transfers between devices, send(): self.came[step] = lax.ppermute(operand, 'tensor', pairs)  76.8 us
    ppermute x19, starting transfers between devices, send(): self.came[step] = lax.ppermute(operand, 'tensor', pairs)  64.3 us
    pallas_call x4, Pallas kernels, forward_rows(): pl.pallas_call(body, grid=(1,), in_specs=specs, out_specs=[HBM] * (6 + pa...  60.5 us
    pallas_call x5, Pallas kernels, pair_product(): pl.pallas_call(body, grid_spec=pltpu.PrefetchScalarGridSpec(num_scalar_pr...  59.1 us
    pallas_call x4, Pallas kernels, backward_rows(): pl.pallas_call(body, grid=(1,), in_specs=specs, out_specs=[HBM] * (1 + pa...  57.6 us
    pallas_call x19, Pallas kernels, take_in(): pl.pallas_call(body, in_specs=specs, out_specs=out_specs, out_shape=outs,...  40.3 us
    pallas_call x16, Pallas kernels, pass_on(): pl.pallas_call(body, in_specs=[SMEM] + [VMEM] * (2 + len(more)) + [HBM] *...  26.1 us
    ppermute x16, starting transfers between devices, pump(): self.met[step] = lax.ppermute(held, 'tensor', [(1, 2), (2, 1)])  18.9 us
  transfers between devices with their start and end apart: 43, of which 9 were waited for; matrix products, arithmetic and copies ran while one was open for 1% of the time, Pallas kernels for 53%

profile of v3, /device:TPU:0, one launch (start us, length us, event | category | flops | bytes accessed | tf_op | source)
XLA Modules:
  0.0 477.0 jit_solution(14455277009254781079)
XLA Ops:
  8.0 14.9 %forward_rows.4 = (bf16[1024,2048]{1,0:T(8,128)(2,1)}, bf16[1024,2048]{1,0:T(8,128)(2,1)}, bf16[3,1024,512]{2,1,0:T(8,128)(2,1)}, bf16[1024,512]{1,0:T(8,128)(2,...) custom-call(s32[1]{0:T(128)S(6)} %copy.116.refs_0_.len_ref, ...), custom_call_target="tpu_custom_call" | custom-call | flops 40000000000 | bytes 35651584 | tf_op jit(solution)/shard_map/forward_rows/pallas_call | solution.py:276
  22.8 5.2 %collective-permute-start.1 = (f32[128,2048]{1,0:T(8,128)}, f32[128,2048]{1,0:T(8,128)S(1)}, u32[]{:S(2)}, u32[]{:S(2)}) collective-permute-start(f32[128,2048]{1,0:T(8,128)} %get-tuple-element.138.refs_2_), channel_id=1, source_target_pairs={{0,1},{3,2},{4,5},{7,6},{8,9},{11,10},{12,13},{15,14},{16,17},{19,... | collective-permute-start | bytes 3145736 | tf_op jit(solution)/shard_map/ppermute | solution.py:778
  28.1 14.7 %forward_rows.5 = (bf16[1024,2048]{1,0:T(8,128)(2,1)}, bf16[1024,2048]{1,0:T(8,128)(2,1)}, bf16[3,1024,512]{2,1,0:T(8,128)(2,1)}, bf16[1024,512]{1,0:T(8,128)(2,...) custom-call(s32[1]{0:T(128)S(6)} %copy.116.refs_0_.len_ref, ...), custom_call_target="tpu_custom_call", output_to_operand_aliasing={{0}: (18, {}), {1}: (19, {}), {2}: (20, {}), {3}: (21, {}),... | custom-call | flops 40000000000 | bytes 35651584 | tf_op jit(solution)/shard_map/forward_rows/pallas_call | solution.py:276
  46.4 5.1 %mask_rows.1 = (bf16[1024,2048]{1,0:T(8,128)(2,1)}, f32[1,2048]{1,0:T(1,128)S(1)}) custom-call(s32[1]{0:T(128)S(6)} %copy.116.refs_0_.len_ref, bf16[1024,2048]{1,0:T(8,128)(2,1)} %refs_1_.1, f32[8,128]{1,0:T(8,128)S(1)} %get-tuple-element.139.refs_2_), custom_call_target="tpu_custom_call" | custom-call | flops 40000000000 | bytes 8388608 | tf_op jit(solution)/shard_map/mask_rows/pallas_call | solution.py:315
  53.5 15.2 %forward_rows.6 = (bf16[1024,2048]{1,0:T(8,128)(2,1)}, bf16[1024,2048]{1,0:T(8,128)(2,1)}, bf16[3,1024,512]{2,1,0:T(8,128)(2,1)}, bf16[1024,512]{1,0:T(8,128)(2,...) custom-call(s32[1]{0:T(128)S(6)} %copy.116.refs_0_.len_ref, ...), custom_call_target="tpu_custom_call", output_to_operand_aliasing={{0}: (18, {}), {1}: (19, {}), {2}: (20, {}), {3}: (21, {}),... | custom-call | flops 40000000000 | bytes 35651584 | tf_op jit(solution)/shard_map/forward_rows/pallas_call | solution.py:276
  68.7 5.4 %collective-permute-done.refs_1_ = f32[128,2048]{1,0:T(8,128)} collective-permute-done((f32[128,2048]{1,0:T(8,128)}, f32[128,2048]{1,0:T(8,128)}, u32[]{:S(2)}, u32[]{:S(2)}) %collective-permute-start) | collective-permute-done | bytes 1048608 | tf_op jit(solution)/shard_map/ppermute | solution.py:778
  77.1 5.3 %collective-permute-start.6 = (f32[128,2048]{1,0:T(8,128)S(1)}, f32[128,2048]{1,0:T(8,128)S(1)}, u32[]{:S(2)}, u32[]{:S(2)}) collective-permute-start(f32[128,2048]{1,0:T(8,128)S(1)} %pass_on.16.refs_24_.refs_3_), channel_id=1, source_target_pairs={{0,1},{3,2},{1,0},{2,3},{4,5},{7,6},{5,4},{6,7},{8,9},{11,10},{9,8... | collective-permute-start | bytes 3145736 | tf_op jit(solution)/shard_map/ppermute | solution.py:778
  82.4 15.6 %forward_rows.7 = (bf16[1024,2048]{1,0:T(8,128)(2,1)}, bf16[1024,2048]{1,0:T(8,128)(2,1)}, bf16[3,1024,512]{2,1,0:T(8,128)(2,1)}, bf16[1024,512]{1,0:T(8,128)(2,...) custom-call(s32[1]{0:T(128)S(6)} %copy.116.refs_0_.len_ref, ...), custom_call_target="tpu_custom_call", output_to_operand_aliasing={{0}: (18, {}), {1}: (19, {}), {2}: (20, {}), {3}: (21, {}),... | custom-call | flops 40000000000 | bytes 35651584 | tf_op jit(solution)/shard_map/forward_rows/pallas_call | solution.py:276
  105.2 10.8 %w_out_other.1 = (f32[4,1,2560,256]{3,2,1,0:T(8,128)}, f32[8,128]{1,0:T(8,128)S(1)}) custom-call(s32[1]{0:T(128)S(6)} %sub.4._, bf16[1024,2048]{1,0:T(8,128)(2,1)} %get-tuple-element.152.refs_0_, bf16[1024,512]{1,0:T(8,128)(2,1)} %get-tuple-element.153.refs_1_, bf16[1,1024,2048]{2,1,0:T(8,128)(2,1)} %bitcast.93, f32[128,2048]{1,0:T(8,128)} %pass_on.17.refs_3_), custom_call_target="tpu_custom_call" | custom-call | flops 40000000000 | bytes 19922944 | tf_op jit(solution)/shard_map/w_out_other/pallas_call | solution.py:359
  124.9 4.3 collective-permute-start.11
  129.2 15.3 %attend_back.1 = (bf16[3,1024,512]{2,1,0:T(8,128)(2,1)}, f32[3,1,512]{2,1,0:T(1,128)S(1)}) custom-call(s32[1]{0:T(128)S(6)} %copy.116.refs_0_.len_ref, bf16[3,1024,512]{2,1,0:T(8,128)(2,1)} %get-tuple-element.157.q_ref.k_ref.v_ref, bf16[3,1024,512]{2,1,0:T(8,128)(2,1)} %get-tuple-element.157.q_ref.k_ref.v_ref, ...), custom_call_target="tpu_custom_call" | custom-call | flops 299999985664 | bytes 11534336 | tf_op jit(solution)/shard_map/attend_back/pallas_call | solution.py:414
  152.7 13.3 %w_out_own.1 = (f32[4,1,2560,256]{3,2,1,0:T(8,128)}, f32[8,128]{1,0:T(8,128)S(1)}) custom-call(s32[1]{0:T(128)} %bitcast.10._, bf16[1024,2048]{1,0:T(8,128)(2,1)} %get-tuple-element.152.refs_0_, bf16[1024,512]{1,0:T(8,128)(2,1)} %get-tuple-element.153.refs_1_, bf16[1,1024,2048]{2,1,0:T(8,128)(2,1)} %bitcast.94, ...), custom_call_target="tpu_custom_call" | custom-call | flops 40000000000 | bytes 19922944 | tf_op jit(solution)/shard_map/w_out_own/pallas_call | solution.py:359
  173.3 4.2 collective-permute-start.12
  180.3 14.5 %backward_rows.4 = (bf16[1024,2048]{1,0:T(8,128)(2,1)}, f32[128,2048]{1,0:T(8,128)}, f32[128,2048]{1,0:T(8,128)}, f32[8,2048]{1,0:T(8,128)S(1)}, f32[1,2048]{1,0:T(1,128)S(1)}) custom-call(s32[2]{0:T(128)S(1)} %add_convert_fusion.refs_1_.refs_0_.flag_ref, f32[1,2048]{1,0:T(1,128)} %bitcast.81, f32[1,2048]{1,0:T(1,128)} %bitcast.89, ...), custom_call_target="tpu_custom_call" | custom-call | flops 299999985664 | bytes 31457280 | tf_op jit(solution)/shard_map/backward_rows/pallas_call | solution.py:547
  203.0 13.3 %w_qkv_grad.1 = (f32[8,3,256,512]{3,2,1,0:T(8,128)}, f32[8,128]{1,0:T(8,128)S(1)}) custom-call(s32[1]{0:T(128)} %constant.27.clone.1._, bf16[1024,2048]{1,0:T(8,128)(2,1)} %get-tuple-element.177.refs_0_, bf16[3,1024,512]{2,1,0:T(8,128)(2,1)} %get-tuple-element.174.refs_6_.refs_1_, f32[128,2048]{1,0:T(8,128)} %pass_on.21.refs_2_.refs_3_), custom_call_target="tpu_custom_call" | custom-call | flops 40000000000 | bytes 19922944 | tf_op jit(solution)/shard_map/w_qkv_grad/pallas_call | solution.py:359
  222.6 4.3 collective-permute-start.19
  226.9 14.2 %backward_rows.5 = (bf16[1024,2048]{1,0:T(8,128)(2,1)}, f32[128,2048]{1,0:T(8,128)}, f32[128,2048]{1,0:T(8,128)}, f32[8,2048]{1,0:T(8,128)S(1)}, f32[1,2048]{1,0:T(1,128)S(1)}) custom-call(s32[2]{0:T(128)S(1)} %add_convert_fusion.refs_1_.refs_0_.flag_ref, f32[1,2048]{1,0:T(1,128)} %bitcast.82, f32[1,2048]{1,0:T(1,128)} %bitcast.90, ...), custom_call_target="tpu_custom_call", output_to_operand_aliasing={{0}: (10, {})} | custom-call | flops 40000000000 | bytes 31457280 | tf_op jit(solution)/shard_map/backward_rows/pallas_call | solution.py:547
  251.9 14.8 %backward_rows.6 = (bf16[1024,2048]{1,0:T(8,128)(2,1)}, f32[128,2048]{1,0:T(8,128)}, f32[128,2048]{1,0:T(8,128)}, f32[8,2048]{1,0:T(8,128)S(1)}, f32[1,2048]{1,0:T(1,128)S(1)}) custom-call(s32[2]{0:T(128)S(1)} %add_convert_fusion.refs_1_.refs_0_.flag_ref, f32[1,2048]{1,0:T(1,128)} %bitcast.83, f32[1,2048]{1,0:T(1,128)} %bitcast.91, ...), custom_call_target="tpu_custom_call", output_to_operand_aliasing={{0}: (10, {})} | custom-call | flops 40000000000 | bytes 31457280 | tf_op jit(solution)/shard_map/backward_rows/pallas_call | solution.py:547
  273.9 14.2 %backward_rows.7 = (bf16[1024,2048]{1,0:T(8,128)(2,1)}, f32[128,2048]{1,0:T(8,128)}, f32[128,2048]{1,0:T(8,128)}, f32[8,2048]{1,0:T(8,128)S(1)}, f32[1,2048]{1,0:T(1,128)S(1)}) custom-call(s32[2]{0:T(128)S(1)} %add_convert_fusion.refs_1_.refs_0_.flag_ref, f32[1,2048]{1,0:T(1,128)} %bitcast.84, f32[1,2048]{1,0:T(1,128)} %bitcast.92, ...), custom_call_target="tpu_custom_call", output_to_operand_aliasing={{0}: (10, {})} | custom-call | flops 40000000000 | bytes 31457280 | tf_op jit(solution)/shard_map/backward_rows/pallas_call | solution.py:547
  292.3 5.3 %collective-permute-start.22 = (f32[128,2048]{1,0:T(8,128)}, f32[128,2048]{1,0:T(8,128)}, u32[]{:S(2)}, u32[]{:S(2)}) collective-permute-start(f32[128,2048]{1,0:T(8,128)} %pass_on.25.refs_2_.refs_3_), channel_id=1, source_target_pairs={{0,1},{3,2},{1,0},{2,3},{4,5},{7,6},{5,4},{6,7},{8,9},{11,10},{9,8... | collective-permute-start | bytes 3145736 | tf_op jit(solution)/shard_map/ppermute | solution.py:778
  297.6 10.3 %w_in_other.1 = (f32[4,1,256,2048]{3,2,1,0:T(8,128)}, f32[8,128]{1,0:T(8,128)S(1)}) custom-call(s32[1]{0:T(128)S(6)} %sub.4._, bf16[1024,2048]{1,0:T(8,128)(2,1)} %get-tuple-element.201.refs_0_, bf16[1,1024,2048]{2,1,0:T(8,128)(2,1)} %bitcast.95, f32[128,2048]{1,0:T(8,128)} %pass_on.25.refs_2_.refs_3_), custom_call_target="tpu_custom_call" | custom-call | flops 40000000000 | bytes 16777216 | tf_op jit(solution)/shard_map/w_in_other/pallas_call | solution.py:359
  316.7 4.6 collective-permute-done.26.refs_1_
  322.6 6.7 %collective-permute-start.31 = (f32[128,2048]{1,0:T(8,128)}, f32[128,2048]{1,0:T(8,128)}, u32[]{:S(2)}, u32[]{:S(2)}) collective-permute-start(f32[128,2048]{1,0:T(8,128)} %get-tuple-element.213.refs_2_.refs_3_), channel_id=1, source_target_pairs={{0,1},{3,2},{1,0},{2,3},{4,5},{7,6},{5,4},{6,7},{8,9},{11,10},{9,8... | collective-permute-start | bytes 3145736 | tf_op jit(solution)/shard_map/ppermute | solution.py:778
  339.0 5.8 %collective-permute-start.33 = (f32[128,2048]{1,0:T(8,128)}, f32[128,2048]{1,0:T(8,128)}, u32[]{:S(2)}, u32[]{:S(2)}) collective-permute-start(f32[128,2048]{1,0:T(8,128)} %pass_on.27.refs_3_), channel_id=1, source_target_pairs={{0,1},{3,2},{1,0},{2,3},{4,5},{7,6},{5,4},{6,7},{8,9},{11,10},{9,8... | collective-permute-start | bytes 3145736 | tf_op jit(solution)/shard_map/ppermute | solution.py:778
  344.7 11.6 %w_in_own.1 = (f32[4,1,256,2048]{3,2,1,0:T(8,128)}, f32[8,128]{1,0:T(8,128)S(1)}) custom-call(s32[1]{0:T(128)} %bitcast.10._, bf16[1024,2048]{1,0:T(8,128)(2,1)} %get-tuple-element.201.refs_0_, bf16[1,1024,2048]{2,1,0:T(8,128)(2,1)} %bitcast.96, f32[4,1,256,2048]{3,2,1,0:T(8,128)} %collective-permute-done.29.refs_2_, f32[128,2048]{1,0:T(8,128)} %pass_on.27.refs_3_), custom_call_target="tpu_custom_call" | custom-call | flops 40000000000 | bytes 16777216 | tf_op jit(solution)/shard_map/w_in_own/pallas_call | solution.py:359
  363.4 4.2 collective-permute-start.32
  367.5 8.6 %reduce-scatter.8.cloned.1.call-done = f32[1,3,256,512]{3,2,1,0:T(8,128)} async-done(((f32[8,3,256,512]{3,2,1,0:T(8,128)}), f32[1,3,256,512]{3,2,1,0:T(8,128)}) %reduce-scatter.8.cloned.1.call-update) | async-done | bytes 1572880 | tf_op jit(solution)/shard_map/reduce_scatter | solution.py:956
  377.5 5.0 %split_rows.1 = (f32[2048,256]{1,0:T(8,128)}, f32[512,256]{1,0:T(8,128)}) custom-call(f32[2560,256]{1,0:T(8,128)} %bitcast.35, f32[136,2048]{1,0:T(8,128)S(1)} %get-tuple-element.222.refs_0_.refs_3_, f32[3,256,512]{2,1,0:T(8,128)S(1)} %bitcast.38), custom_call_target="tpu_custom_call" | custom-call | bytes 5242880 | tf_op jit(solution)/shard_map/split_rows/pallas_call | solution.py:721
  389.4 10.6 %collective-permute-done.32.refs_1_ = f32[136,2048]{1,0:T(8,128)} collective-permute-done((f32[136,2048]{1,0:T(8,128)S(1)}, f32[136,2048]{1,0:T(8,128)}, u32[]{:S(2)}, u32[]{:S(2)}) %collective-permute-start.32) | collective-permute-done | bytes 1114144 | tf_op jit(solution)/shard_map/ppermute | solution.py:778
  404.8 17.5 %collective-permute-done.39.refs_1_ = f32[128,2048]{1,0:T(8,128)S(1)} collective-permute-done((f32[128,2048]{1,0:T(8,128)S(1)}, f32[128,2048]{1,0:T(8,128)S(1)}, u32[]{:S(2)}, u32[]{:S(2)}) %collective-permute-start.39) | collective-permute-done | bytes 1048608 | tf_op jit(solution)/shard_map/ppermute | solution.py:778
  425.8 19.1 %collective-permute-done.38.refs_1_ = f32[128,2048]{1,0:T(8,128)S(1)} collective-permute-done((f32[128,2048]{1,0:T(8,128)S(1)}, f32[128,2048]{1,0:T(8,128)S(1)}, u32[]{:S(2)}, u32[]{:S(2)}) %collective-permute-start.38) | collective-permute-done | bytes 1048608 | tf_op jit(solution)/shard_map/ppermute | solution.py:778
  446.3 21.1 %collective-permute-done.37.refs_1_ = f32[136,2048]{1,0:T(8,128)S(1)} collective-permute-done((f32[136,2048]{1,0:T(8,128)S(1)}, f32[136,2048]{1,0:T(8,128)S(1)}, u32[]{:S(2)}, u32[]{:S(2)}) %collective-permute-start.37) | collective-permute-done | bytes 1114144 | tf_op jit(solution)/shard_map/ppermute | solution.py:778
  (198 shorter events, 126.7 us)
Async XLA Ops:
  7.2 306.4 %reduce-scatter.10.cloned.1.call-start = ((), (), s32[]{:S(2)}) async-start(), calls=%async_computation.4 | async-start | bytes 13107200
  22.8 28.8 %collective-permute-start.1 = (f32[128,2048]{1,0:T(8,128)}, f32[128,2048]{1,0:T(8,128)S(1)}, u32[]{:S(2)}, u32[]{:S(2)}) collective-permute-start(f32[128,2048]{1,0:T(8,128)} %get-tuple-element.138.refs_2_), channel_id=1, source_target_pairs={{0,1},{3,2},{4,5},{7,6},{8,9},{11,10},{12,13},{15,14},{16,17},{19,... | collective-permute-start | bytes 3145736 | tf_op jit(solution)/shard_map/ppermute | solution.py:778
  42.8 31.3 %collective-permute-start = (f32[128,2048]{1,0:T(8,128)}, f32[128,2048]{1,0:T(8,128)}, u32[]{:S(2)}, u32[]{:S(2)}) collective-permute-start(f32[128,2048]{1,0:T(8,128)} %get-tuple-element.131.refs_2_), channel_id=1, source_target_pairs={{0,1},{3,2},{4,5},{7,6},{8,9},{11,10},{12,13},{15,14},{16,17},{19,... | collective-permute-start | bytes 3145736 | tf_op jit(solution)/shard_map/ppermute | solution.py:778
  45.1 53.0 %collective-permute-start.3 = (f32[128,2048]{1,0:T(8,128)}, f32[128,2048]{1,0:T(8,128)S(1)}, u32[]{:S(2)}, u32[]{:S(2)}) collective-permute-start(f32[128,2048]{1,0:T(8,128)} %get-tuple-element.143.refs_2_), channel_id=1, source_target_pairs={{0,1},{3,2},{4,5},{7,6},{8,9},{11,10},{12,13},{15,14},{16,17},{19,... | collective-permute-start | bytes 3145736 | tf_op jit(solution)/shard_map/ppermute | solution.py:778
  77.1 41.8 %collective-permute-start.6 = (f32[128,2048]{1,0:T(8,128)S(1)}, f32[128,2048]{1,0:T(8,128)S(1)}, u32[]{:S(2)}, u32[]{:S(2)}) collective-permute-start(f32[128,2048]{1,0:T(8,128)S(1)} %pass_on.16.refs_24_.refs_3_), channel_id=1, source_target_pairs={{0,1},{3,2},{1,0},{2,3},{4,5},{7,6},{5,4},{6,7},{8,9},{11,10},{9,8... | collective-permute-start | bytes 3145736 | tf_op jit(solution)/shard_map/ppermute | solution.py:778
  98.7 24.5 %collective-permute-start.7 = (f32[128,2048]{1,0:T(8,128)S(1)}, f32[128,2048]{1,0:T(8,128)S(1)}, u32[]{:S(2)}, u32[]{:S(2)}) collective-permute-start(f32[128,2048]{1,0:T(8,128)S(1)} %take_in.21.refs_1_.held_ref), channel_id=1, source_target_pairs={{1,2},{2,1},{5,6},{6,5},{9,10},{10,9},{13,14},{14,13},{17,18},{18,... | collective-permute-start | bytes 3145736 | tf_op jit(solution)/shard_map/ppermute | solution.py:788
  101.2 44.0 %collective-permute-start.5 = (f32[128,2048]{1,0:T(8,128)}, f32[128,2048]{1,0:T(8,128)}, u32[]{:S(2)}, u32[]{:S(2)}) collective-permute-start(f32[128,2048]{1,0:T(8,128)} %pass_on.17.refs_3_), channel_id=1, source_target_pairs={{0,1},{3,2},{1,0},{2,3},{4,5},{7,6},{5,4},{6,7},{8,9},{11,10},{9,8... | collective-permute-start | bytes 3145736 | tf_op jit(solution)/shard_map/ppermute | solution.py:778
  121.4 27.0 %collective-permute-start.10 = (f32[128,2048]{1,0:T(8,128)}, f32[128,2048]{1,0:T(8,128)}, u32[]{:S(2)}, u32[]{:S(2)}) collective-permute-start(f32[128,2048]{1,0:T(8,128)} %get-tuple-element.160.refs_2_.held_ref), channel_id=1, source_target_pairs={{1,2},{2,1},{5,6},{6,5},{9,10},{10,9},{13,14},{14,13},{17,18},{18,... | collective-permute-start | bytes 3145736 | tf_op jit(solution)/shard_map/ppermute | solution.py:788
  124.9 41.1 %collective-permute-start.11 = (f32[128,2048]{1,0:T(8,128)}, f32[128,2048]{1,0:T(8,128)}, u32[]{:S(2)}, u32[]{:S(2)}) collective-permute-start(f32[128,2048]{1,0:T(8,128)} %get-tuple-element.161.refs_0_.refs_3_), channel_id=1, source_target_pairs={{0,1},{3,2},{1,0},{2,3},{4,5},{7,6},{5,4},{6,7},{8,9},{11,10},{9,8... | collective-permute-start | bytes 3145736 | tf_op jit(solution)/shard_map/ppermute | solution.py:778
  151.1 43.8 %collective-permute-start.13 = (f32[128,2048]{1,0:T(8,128)}, f32[128,2048]{1,0:T(8,128)}, u32[]{:S(2)}, u32[]{:S(2)}) collective-permute-start(f32[128,2048]{1,0:T(8,128)} %pass_on.19.refs_4_.refs_3_), channel_id=1, source_target_pairs={{0,1},{3,2},{1,0},{2,3},{4,5},{7,6},{5,4},{6,7},{8,9},{11,10},{9,8... | collective-permute-start | bytes 3145736 | tf_op jit(solution)/shard_map/ppermute | solution.py:778
  169.5 28.9 %collective-permute-start.14 = (f32[128,2048]{1,0:T(8,128)}, f32[128,2048]{1,0:T(8,128)}, u32[]{:S(2)}, u32[]{:S(2)}) collective-permute-start(f32[128,2048]{1,0:T(8,128)} %get-tuple-element.170.refs_2_.held_ref), channel_id=1, source_target_pairs={{1,2},{2,1},{5,6},{6,5},{9,10},{10,9},{13,14},{14,13},{17,18},{18,... | collective-permute-start | bytes 3145736 | tf_op jit(solution)/shard_map/ppermute | solution.py:788
  172.9 203.2 %reduce-scatter.8.cloned.1.call-start = ((), (), s32[]{:S(2)}) async-start(), calls=%async_computation.3 | async-start | bytes 14155776 | tf_op jit(solution)/shard_map/reduce_scatter | solution.py:956
  173.3 43.0 %collective-permute-start.12 = (f32[128,2048]{1,0:T(8,128)}, f32[128,2048]{1,0:T(8,128)}, u32[]{:S(2)}, u32[]{:S(2)}) collective-permute-start(f32[128,2048]{1,0:T(8,128)} %get-tuple-element.171.refs_10_.refs_3_), channel_id=1, source_target_pairs={{0,1},{3,2},{1,0},{2,3},{4,5},{7,6},{5,4},{6,7},{8,9},{11,10},{9,8... | collective-permute-start | bytes 3145736 | tf_op jit(solution)/shard_map/ppermute | solution.py:778
  201.4 39.7 %collective-permute-start.17 = (f32[128,2048]{1,0:T(8,128)}, f32[128,2048]{1,0:T(8,128)}, u32[]{:S(2)}, u32[]{:S(2)}) collective-permute-start(f32[128,2048]{1,0:T(8,128)} %pass_on.21.refs_2_.refs_3_), channel_id=1, source_target_pairs={{0,1},{3,2},{1,0},{2,3},{4,5},{7,6},{5,4},{6,7},{8,9},{11,10},{9,8... | collective-permute-start | bytes 3145736 | tf_op jit(solution)/shard_map/ppermute | solution.py:778
  219.1 26.8 %collective-permute-start.15 = (f32[128,2048]{1,0:T(8,128)S(1)}, f32[128,2048]{1,0:T(8,128)}, u32[]{:S(2)}, u32[]{:S(2)}) collective-permute-start(f32[128,2048]{1,0:T(8,128)S(1)} %get-tuple-element.181.refs_2_.held_ref), channel_id=1, source_target_pairs={{1,2},{2,1},{5,6},{6,5},{9,10},{10,9},{13,14},{14,13},{17,18},{18,... | collective-permute-start | bytes 3145736 | tf_op jit(solution)/shard_map/ppermute | solution.py:788
  222.6 44.1 %collective-permute-start.19 = (f32[128,2048]{1,0:T(8,128)}, f32[128,2048]{1,0:T(8,128)}, u32[]{:S(2)}, u32[]{:S(2)}) collective-permute-start(f32[128,2048]{1,0:T(8,128)} %get-tuple-element.185.refs_11_.refs_3_), channel_id=1, source_target_pairs={{0,1},{3,2},{1,0},{2,3},{4,5},{7,6},{5,4},{6,7},{8,9},{11,10},{9,8... | collective-permute-start | bytes 3145736 | tf_op jit(solution)/shard_map/ppermute | solution.py:778
  241.1 228.3 %reduce-scatter.12.cloned.1.call-start = ((), (), s32[]{:S(2)}) async-start(), calls=%async_computation.5 | async-start | bytes 10485760
  244.9 25.4 %collective-permute-start.20 = (f32[128,2048]{1,0:T(8,128)S(1)}, f32[128,2048]{1,0:T(8,128)S(1)}, u32[]{:S(2)}, u32[]{:S(2)}) collective-permute-start(f32[128,2048]{1,0:T(8,128)S(1)} %get-tuple-element.189.refs_1_.held_ref), channel_id=1, source_target_pairs={{1,2},{2,1},{5,6},{6,5},{9,10},{10,9},{13,14},{14,13},{17,18},{18,... | collective-permute-start | bytes 3145736 | tf_op jit(solution)/shard_map/ppermute | solution.py:788
  247.6 40.7 %collective-permute-start.18 = (f32[128,2048]{1,0:T(8,128)S(1)}, f32[128,2048]{1,0:T(8,128)S(1)}, u32[]{:S(2)}, u32[]{:S(2)}) collective-permute-start(f32[128,2048]{1,0:T(8,128)S(1)} %pass_on.23.refs_11_.refs_3_), channel_id=1, source_target_pairs={{0,1},{3,2},{1,0},{2,3},{4,5},{7,6},{5,4},{6,7},{8,9},{11,10},{9,8... | collective-permute-start | bytes 3145736 | tf_op jit(solution)/shard_map/ppermute | solution.py:778
  271.0 36.8 %collective-permute-start.23 = (f32[128,2048]{1,0:T(8,128)S(1)}, f32[128,2048]{1,0:T(8,128)S(1)}, u32[]{:S(2)}, u32[]{:S(2)}) collective-permute-start(f32[128,2048]{1,0:T(8,128)S(1)} %pass_on.24.refs_11_.refs_3_), channel_id=1, source_target_pairs={{0,1},{3,2},{1,0},{2,3},{4,5},{7,6},{5,4},{6,7},{8,9},{11,10},{9,8... | collective-permute-start | bytes 3145736 | tf_op jit(solution)/shard_map/ppermute | solution.py:778
  288.2 25.4 %collective-permute-start.24 = (f32[108,128]{1,0:T(8,128)S(1)}, f32[108,128]{1,0:T(8,128)S(1)}, u32[]{:S(2)}, u32[]{:S(2)}) collective-permute-start(f32[108,128]{1,0:T(8,128)S(1)} %maximum_bitcast_fusion.refs_0_), channel_id=1, source_target_pairs={{0,4},{4,0},{8,12},{12,8},{16,20},{20,16},{24,28},{28,24},{1,5},{5... | collective-permute-start | bytes 165896 | tf_op jit(solution)/shard_map/ppermute | solution.py:812
  292.3 38.4 %collective-permute-start.22 = (f32[128,2048]{1,0:T(8,128)}, f32[128,2048]{1,0:T(8,128)}, u32[]{:S(2)}, u32[]{:S(2)}) collective-permute-start(f32[128,2048]{1,0:T(8,128)} %pass_on.25.refs_2_.refs_3_), channel_id=1, source_target_pairs={{0,1},{3,2},{1,0},{2,3},{4,5},{7,6},{5,4},{6,7},{8,9},{11,10},{9,8... | collective-permute-start | bytes 3145736 | tf_op jit(solution)/shard_map/ppermute | solution.py:778
  310.2 25.9 %collective-permute-start.30 = (f32[128,2048]{1,0:T(8,128)}, f32[128,2048]{1,0:T(8,128)}, u32[]{:S(2)}, u32[]{:S(2)}) collective-permute-start(f32[128,2048]{1,0:T(8,128)} %get-tuple-element.212.refs_2_.held_ref), channel_id=1, source_target_pairs={{1,2},{2,1},{5,6},{6,5},{9,10},{10,9},{13,14},{14,13},{17,18},{18,... | collective-permute-start | bytes 3145736 | tf_op jit(solution)/shard_map/ppermute | solution.py:788
  313.6 31.1 %collective-permute-start.29 = (f32[4,1,256,2048]{3,2,1,0:T(8,128)}, f32[4,1,256,2048]{3,2,1,0:T(8,128)}, u32[]{:S(2)}, u32[]{:S(2)}) collective-permute-start(f32[4,1,256,2048]{3,2,1,0:T(8,128)} %get-tuple-element.216), channel_id=1, source_target_pairs={{0,4},{4,0},{8,12},{12,8},{16,20},{20,16},{24,28},{28,24},{1,5},{5... | collective-permute-start | bytes 25165832 | tf_op jit(solution)/shard_map/ppermute | solution.py:926
  322.6 35.0 %collective-permute-start.31 = (f32[128,2048]{1,0:T(8,128)}, f32[128,2048]{1,0:T(8,128)}, u32[]{:S(2)}, u32[]{:S(2)}) collective-permute-start(f32[128,2048]{1,0:T(8,128)} %get-tuple-element.213.refs_2_.refs_3_), channel_id=1, source_target_pairs={{0,1},{3,2},{1,0},{2,3},{4,5},{7,6},{5,4},{6,7},{8,9},{11,10},{9,8... | collective-permute-start | bytes 3145736 | tf_op jit(solution)/shard_map/ppermute | solution.py:778
  334.2 27.4 %collective-permute-start.28 = (f32[128,2048]{1,0:T(8,128)}, f32[128,2048]{1,0:T(8,128)}, u32[]{:S(2)}, u32[]{:S(2)}) collective-permute-start(f32[128,2048]{1,0:T(8,128)} %get-tuple-element.215.refs_1_.held_ref), channel_id=1, source_target_pairs={{1,2},{2,1},{5,6},{6,5},{9,10},{10,9},{13,14},{14,13},{17,18},{18,... | collective-permute-start | bytes 3145736 | tf_op jit(solution)/shard_map/ppermute | solution.py:788
  339.0 43.5 %collective-permute-start.33 = (f32[128,2048]{1,0:T(8,128)}, f32[128,2048]{1,0:T(8,128)}, u32[]{:S(2)}, u32[]{:S(2)}) collective-permute-start(f32[128,2048]{1,0:T(8,128)} %pass_on.27.refs_3_), channel_id=1, source_target_pairs={{0,1},{3,2},{1,0},{2,3},{4,5},{7,6},{5,4},{6,7},{8,9},{11,10},{9,8... | collective-permute-start | bytes 3145736 | tf_op jit(solution)/shard_map/ppermute | solution.py:778
  360.0 26.7 %collective-permute-start.34 = (f32[128,2048]{1,0:T(8,128)S(1)}, f32[128,2048]{1,0:T(8,128)}, u32[]{:S(2)}, u32[]{:S(2)}) collective-permute-start(f32[128,2048]{1,0:T(8,128)S(1)} %get-tuple-element.221.refs_2_.held_ref), channel_id=1, source_target_pairs={{1,2},{2,1},{5,6},{6,5},{9,10},{10,9},{13,14},{14,13},{17,18},{18,... | collective-permute-start | bytes 3145736 | tf_op jit(solution)/shard_map/ppermute | solution.py:788
  363.4 36.6 %collective-permute-start.32 = (f32[136,2048]{1,0:T(8,128)S(1)}, f32[136,2048]{1,0:T(8,128)}, u32[]{:S(2)}, u32[]{:S(2)}) collective-permute-start(f32[136,2048]{1,0:T(8,128)S(1)} %get-tuple-element.222.refs_0_.refs_3_), channel_id=1, source_target_pairs={{0,1},{3,2},{1,0},{2,3},{4,5},{7,6},{5,4},{6,7},{8,9},{11,10},{9,8... | collective-permute-start | bytes 3342344 | tf_op jit(solution)/shard_map/ppermute | solution.py:778
  388.1 34.3 %collective-permute-start.39 = (f32[128,2048]{1,0:T(8,128)S(1)}, f32[128,2048]{1,0:T(8,128)S(1)}, u32[]{:S(2)}, u32[]{:S(2)}) collective-permute-start(f32[128,2048]{1,0:T(8,128)S(1)} %pass_on.29.refs_5_.refs_2_), channel_id=1, source_target_pairs={{1,0},{2,3},{5,4},{6,7},{9,8},{10,11},{13,12},{14,15},{17,16},{18,... | collective-permute-start | bytes 3145736 | tf_op jit(solution)/shard_map/ppermute | solution.py:778
  403.5 41.3 %collective-permute-start.38 = (f32[128,2048]{1,0:T(8,128)S(1)}, f32[128,2048]{1,0:T(8,128)S(1)}, u32[]{:S(2)}, u32[]{:S(2)}) collective-permute-start(f32[128,2048]{1,0:T(8,128)S(1)} %pass_on.30.refs_0_.refs_4_.refs_2_), channel_id=1, source_target_pairs={{1,0},{2,3},{5,4},{6,7},{9,8},{10,11},{13,12},{14,15},{17,16},{18,... | collective-permute-start | bytes 3145736 | tf_op jit(solution)/shard_map/ppermute | solution.py:778
  424.5 42.9 %collective-permute-start.37 = (f32[136,2048]{1,0:T(8,128)S(1)}, f32[136,2048]{1,0:T(8,128)S(1)}, u32[]{:S(2)}, u32[]{:S(2)}) collective-permute-start(f32[136,2048]{1,0:T(8,128)S(1)} %pass_on.31.refs_4_.refs_2_), channel_id=1, source_target_pairs={{1,0},{2,3},{5,4},{6,7},{9,8},{10,11},{13,12},{14,15},{17,16},{18,... | collective-permute-start | bytes 3342344 | tf_op jit(solution)/shard_map/ppermute | solution.py:778
  (46 other events, 832.4 us)
Sparse Core Ops, SparseCore 0:
  173.0 105.3 reduce-scatter.9
  282.5 93.5 reduce-scatter.7
  379.7 86.3 reduce-scatter.11

commit v4 on v3

--- a/solution.py
+++ b/solution.py
@@ -318,7 +318,7 @@
         in_specs=[SMEM, row] + [ANY] * len(after),
         out_specs=[row, pl.BlockSpec((1, width), lambda i: (0, 0))],
         out_shape=[pltpu.HBM((rows, width), BF16), shape((1, width), F32)],
-        compiler_params=params(46),
+        compiler_params=params(24),
         cost_estimate=cost(2 * rows * width, 4 * rows * width),
         name="mask_rows",
     )(lengths, in_hbm(grad_out), *after)
@@ -365,19 +365,39 @@
             out_specs=[out, pl.BlockSpec(TOKEN.shape, lambda i, p: (0, 0))],
         ),
         out_shape=[pltpu.HBM((blocks, many, tall, wide), F32), TOKEN],
-        compiler_params=params(46),
+        compiler_params=params(30),
         cost_estimate=cost(2 * rows * blocks * many * tall * wide, 2 * rows * (left_width + many * right.shape[2]) + 4 * blocks * many * tall * wide, long),
         name=name,
     )(parity, *map(in_hbm, operands), *after)
 
 
-def attend_back(lengths, qkv, cotan, w_dense, tables, after):
+def mixed_back(cotan, w_dense, after):
+    rows, width = cotan.shape
+    columns = w_dense.shape[0]
+    step = min(256, rows)
+
+    def body(g_ref, w_ref, *refs):
+        refs[-1][...] = dot(g_ref[...], w_ref[...], NT).astype(BF16)
+
+    return pl.pallas_call(
+        body,
+        grid=(rows // step,),
+        in_specs=[pl.BlockSpec((step, width), lambda i: (i, 0)), pl.BlockSpec((columns, width), lambda i: (0, 0))]
+        + [ANY] * len(after),
+        out_specs=pl.BlockSpec((step, columns), lambda i: (i, 0)),
+        out_shape=pltpu.HBM((rows, columns), BF16),
+        compiler_params=params(16),
+        cost_estimate=light(2 * rows * columns * width, 2 * rows * (width + columns)),
+        name="mixed_back",
+    )(in_hbm(cotan), in_hbm(w_dense), *after)
+
+
+def attend_back(lengths, qkv, dmixed, tables, after):
     rows, columns = qkv.shape[1:]
-    width = cotan.shape[1]
     sub = min(256, rows)
     scale = 1.0 / math.sqrt(HD)
 
-    def body(len_ref, q_ref, k_ref, v_ref, g_ref, w_ref, c_ref, l_ref, u_ref, *refs):
+    def body(len_ref, q_ref, k_ref, v_ref, d_ref, c_ref, l_ref, u_ref, *refs):
         out_ref, bias_ref, dk_ref, dv_ref = refs[-4:]
         length = len_ref[0]
         for low in range(0, rows, sub):
@@ -390,15 +410,14 @@
             scores = jnp.where((there <= mine) & (there < length), scores, -1e30)
             expo = jnp.exp(scores - jnp.max(scores, -1, keepdims=True))
             probs = expo * (1.0 / jnp.sum(expo, -1, keepdims=True))
-            dmixed = dot(g_ref[here], w_ref[...], NT).astype(BF16)
-            dprobs = dot(dmixed, values, NT)
+            dprobs = dot(d_ref[here], values, NT)
             delta = jnp.sum(probs * dprobs, -1, keepdims=True)
             dscores = (probs * (dprobs - delta)).astype(BF16)
             out_ref[0, here] = turned(
                 dot(dscores, keys) * scale, c_ref[here], -l_ref[here], -u_ref[here]
             ).astype(BF16)
             dkey = dot(dscores, query, TN) * scale
-            dvalue = dot(probs.astype(BF16), dmixed, TN)
+            dvalue = dot(probs.astype(BF16), d_ref[here], TN)
             if low:
                 dk_ref[:low] += dkey[:low]
                 dv_ref[:low] += dvalue[:low]
@@ -419,8 +438,7 @@
             part(0),
             part(1),
             part(2),
-            pl.BlockSpec((rows, width), lambda h: (0, 0)),
-            pl.BlockSpec((HD, width), lambda h: (h, 0)),
+            pl.BlockSpec((rows, HD), lambda h: (0, h)),
             table,
             table,
             table,
@@ -432,14 +450,14 @@
         ],
         out_shape=[pltpu.HBM((3, rows, columns), BF16), shape((3, 1, columns), F32)],
         scratch_shapes=[pltpu.VMEM((rows, HD), F32)] * 2,
-        compiler_params=params(46),
+        compiler_params=params(36),
         cost_estimate=cost(
-            2 * rows * columns * width + 10 * rows * rows * columns,
-            2 * rows * (width + 7 * columns),
+            10 * rows * rows * columns,
+            14 * rows * columns,
             True,
         ),
         name="attend_back",
-    )(lengths, *map(in_hbm, (qkv, qkv, qkv, cotan, w_dense, *tables)), *after)
+    )(lengths, *map(in_hbm, (qkv, qkv, qkv, dmixed, *tables)), *after)
 
 
 def backward_rows(start, size, unit, x, flag, cotan, slope, dqkv, w_three, w_in, w_out, gains, held, after):
@@ -638,7 +656,7 @@
     return held, out, (result[0] if more else None)
 
 
-def pass_on(flag, held, met, unit, after, carried, last):
+def pass_on(flag, held, met, unit, after, carried, last, long):
     rows, width = (held if unit is None else unit).shape
     both = min(rows, held.shape[0])
 
@@ -659,7 +677,7 @@
         out_shape=[pltpu.VMEM((rows, width), F32)] + [pltpu.HBM(c.shape, c.dtype) for c in carried],
         input_output_aliases={3 + len(more) + i: 1 + i for i in range(len(carried))},
         compiler_params=pltpu.CompilerParams(vmem_limit_bytes=SMALL_LIMIT),
-        cost_estimate=(alone if last else light)(2 * rows * width, 16 * rows * width),
+        cost_estimate=cost(0, 0, True) if long else (alone if last else light)(2 * rows * width, 16 * rows * width),
         name="pass_on",
     )(flag, in_vmem(held), in_vmem(met), *more, *map(in_hbm, carried), *after)
 
@@ -777,7 +795,7 @@
         self.operands[step] = operand
         self.came[step] = lax.ppermute(operand, "tensor", pairs)
 
-    def pump(self, after, carried=()):
+    def pump(self, after, carried=(), long=False):
         step = self.step
         self.step += 1
         last = step >= self.count - 2
@@ -793,7 +811,7 @@
             ahead = step + 2
             unit = self.units[ahead] if ahead < self.count else None
             operand, *carried = pass_on(
-                self.flag, self.held[step - 1], self.met[step - 1], unit, after, carried, last
+                self.flag, self.held[step - 1], self.met[step - 1], unit, after, carried, last, long
             )
             self.send(ahead, operand)
             after = [operand]
@@ -883,10 +901,10 @@
         line = None if straight else Line(2 * each, flag, finish)
         queue = [] if straight else line.units
 
-        def pump(after, *carried):
+        def pump(after, *carried, long=False):
             if straight or line.step == line.count + line.LAG:
                 return (after, *carried)
-            return line.pump(after, carried)
+            return line.pump(after, carried, long)
 
         def forward(start, size, held, after, carried=()):
             result = forward_rows(
@@ -930,12 +948,13 @@
 
         out_parts = ([hidden, mixed], cotan[None], False)
         half, after = other_half("w_out_other", *out_parts, pump(after)[0])
-        after, half = pump(after, half)
+        dmixed = mixed_back(cotan, w_dense, after)
+        after, half = pump([dmixed], half)
         came_out = swap(half)
-        dqkv, b_qkv_grad = attend_back(lengths, qkv, cotan, w_dense, tables, after)
+        dqkv, b_qkv_grad = attend_back(lengths, qkv, dmixed, tables, after)
         out_half, after = own_half("w_out_own", *out_parts, came_out, pump([b_qkv_grad])[0])
-        after, out_half = pump(after, out_half)
         out_grads = over_chips(out_half)
+        (after,) = pump(after, long=True)
 
         dhpre, smalls, biases = None, [], []
 

time: 485 us -> 483 us (level)
    reduce_scatter x1, waiting for transfers between devices: 8.55 us -> 2.09 us  [local(): lax.psum_scatter(qkv_grads, 'dp', scatter_dimension=0, tiled=True)[0]]
    pallas_call x0 -> x1, Pallas kernels: none -> 6.37 us  [mixed_back(): pl.pallas_call(body, grid=(rows // step,), in_specs=[pl.BlockSpec((step,...]
  transfers between devices with their start and end apart: 43 -> 43, of which waited for: 9 -> 8; matrix products, arithmetic and copies ran while one was open for 1% -> 1% of each run, Pallas kernels for 53% -> 54%
where the time goes in v4:
time: 483 us; the launch traced here: 475 us
  Pallas kernels  271 us (56%)
  waiting for transfers between devices  86.2 us (18%)
  starting transfers between devices  85.9 us (18%)
  between operations  15.8 us (3%)
  local copies, waits for them, and re-layouts  15.7 us (3%)
    ppermute x19, waiting for transfers between devices, send(): self.came[step] = lax.ppermute(operand, 'tensor', pairs)  79.7 us
    ppermute x19, starting transfers between devices, send(): self.came[step] = lax.ppermute(operand, 'tensor', pairs)  62.1 us
    pallas_call x4, Pallas kernels, forward_rows(): pl.pallas_call(body, grid=(1,), in_specs=specs, out_specs=[HBM] * (6 + pa...  60.4 us
    pallas_call x5, Pallas kernels, pair_product(): pl.pallas_call(body, grid_spec=pltpu.PrefetchScalarGridSpec(num_scalar_pr...  58.3 us
    pallas_call x4, Pallas kernels, backward_rows(): pl.pallas_call(body, grid=(1,), in_specs=specs, out_specs=[HBM] * (1 + pa...  57.5 us
    pallas_call x19, Pallas kernels, take_in(): pl.pallas_call(body, in_specs=specs, out_specs=out_specs, out_shape=outs,...  40.2 us
    pallas_call x16, Pallas kernels, pass_on(): pl.pallas_call(body, in_specs=[SMEM] + [VMEM] * (2 + len(more)) + [HBM] *...  26.5 us
    ppermute x16, starting transfers between devices, pump(): self.met[step] = lax.ppermute(held, 'tensor', [(1, 2), (2, 1)])  20.2 us
  transfers between devices with their start and end apart: 43, of which 8 were waited for; matrix products, arithmetic and copies ran while one was open for 1% of the time, Pallas kernels for 54%

profile of v4, /device:TPU:0, one launch (start us, length us, event | category | flops | bytes accessed | tf_op | source)
XLA Modules:
  0.0 474.6 jit_solution(1332387944538045670)
XLA Ops:
  8.0 14.9 %forward_rows.4 = (bf16[1024,2048]{1,0:T(8,128)(2,1)}, bf16[1024,2048]{1,0:T(8,128)(2,1)}, bf16[3,1024,512]{2,1,0:T(8,128)(2,1)}, bf16[1024,512]{1,0:T(8,128)(2,...) custom-call(s32[1]{0:T(128)S(6)} %copy.114.refs_0_.len_ref, ...), custom_call_target="tpu_custom_call" | custom-call | flops 40000000000 | bytes 35651584 | tf_op jit(solution)/shard_map/forward_rows/pallas_call | solution.py:276
  22.8 5.2 %collective-permute-start.1 = (f32[128,2048]{1,0:T(8,128)}, f32[128,2048]{1,0:T(8,128)S(1)}, u32[]{:S(2)}, u32[]{:S(2)}) collective-permute-start(f32[128,2048]{1,0:T(8,128)} %get-tuple-element.136.refs_2_), channel_id=1, source_target_pairs={{0,1},{3,2},{4,5},{7,6},{8,9},{11,10},{12,13},{15,14},{16,17},{19,... | collective-permute-start | bytes 3145736 | tf_op jit(solution)/shard_map/ppermute | solution.py:796
  28.1 14.7 %forward_rows.5 = (bf16[1024,2048]{1,0:T(8,128)(2,1)}, bf16[1024,2048]{1,0:T(8,128)(2,1)}, bf16[3,1024,512]{2,1,0:T(8,128)(2,1)}, bf16[1024,512]{1,0:T(8,128)(2,...) custom-call(s32[1]{0:T(128)S(6)} %copy.114.refs_0_.len_ref, ...), custom_call_target="tpu_custom_call", output_to_operand_aliasing={{0}: (18, {}), {1}: (19, {}), {2}: (20, {}), {3}: (21, {}),... | custom-call | flops 40000000000 | bytes 35651584 | tf_op jit(solution)/shard_map/forward_rows/pallas_call | solution.py:276
  46.4 5.1 %mask_rows.1 = (bf16[1024,2048]{1,0:T(8,128)(2,1)}, f32[1,2048]{1,0:T(1,128)S(1)}) custom-call(s32[1]{0:T(128)S(6)} %copy.114.refs_0_.len_ref, bf16[1024,2048]{1,0:T(8,128)(2,1)} %refs_1_.1, f32[8,128]{1,0:T(8,128)S(1)} %get-tuple-element.137.refs_2_), custom_call_target="tpu_custom_call" | custom-call | flops 40000000000 | bytes 8388608 | tf_op jit(solution)/shard_map/mask_rows/pallas_call | solution.py:315
  53.5 15.2 %forward_rows.6 = (bf16[1024,2048]{1,0:T(8,128)(2,1)}, bf16[1024,2048]{1,0:T(8,128)(2,1)}, bf16[3,1024,512]{2,1,0:T(8,128)(2,1)}, bf16[1024,512]{1,0:T(8,128)(2,...) custom-call(s32[1]{0:T(128)S(6)} %copy.114.refs_0_.len_ref, ...), custom_call_target="tpu_custom_call", output_to_operand_aliasing={{0}: (18, {}), {1}: (19, {}), {2}: (20, {}), {3}: (21, {}),... | custom-call | flops 40000000000 | bytes 35651584 | tf_op jit(solution)/shard_map/forward_rows/pallas_call | solution.py:276
  68.7 5.4 %collective-permute-done.refs_1_ = f32[128,2048]{1,0:T(8,128)} collective-permute-done((f32[128,2048]{1,0:T(8,128)}, f32[128,2048]{1,0:T(8,128)}, u32[]{:S(2)}, u32[]{:S(2)}) %collective-permute-start) | collective-permute-done | bytes 1048608 | tf_op jit(solution)/shard_map/ppermute | solution.py:796
  77.1 5.3 %collective-permute-start.6 = (f32[128,2048]{1,0:T(8,128)S(1)}, f32[128,2048]{1,0:T(8,128)S(1)}, u32[]{:S(2)}, u32[]{:S(2)}) collective-permute-start(f32[128,2048]{1,0:T(8,128)S(1)} %pass_on.16.refs_24_.refs_3_), channel_id=1, source_target_pairs={{0,1},{3,2},{1,0},{2,3},{4,5},{7,6},{5,4},{6,7},{8,9},{11,10},{9,8... | collective-permute-start | bytes 3145736 | tf_op jit(solution)/shard_map/ppermute | solution.py:796
  82.4 15.6 %forward_rows.7 = (bf16[1024,2048]{1,0:T(8,128)(2,1)}, bf16[1024,2048]{1,0:T(8,128)(2,1)}, bf16[3,1024,512]{2,1,0:T(8,128)(2,1)}, bf16[1024,512]{1,0:T(8,128)(2,...) custom-call(s32[1]{0:T(128)S(6)} %copy.114.refs_0_.len_ref, ...), custom_call_target="tpu_custom_call", output_to_operand_aliasing={{0}: (18, {}), {1}: (19, {}), {2}: (20, {}), {3}: (21, {}),... | custom-call | flops 40000000000 | bytes 35651584 | tf_op jit(solution)/shard_map/forward_rows/pallas_call | solution.py:276
  101.4 3.8 collective-permute-start.5
  105.2 10.7 %w_out_other.1 = (f32[4,1,2560,256]{3,2,1,0:T(8,128)}, f32[8,128]{1,0:T(8,128)S(1)}) custom-call(s32[1]{0:T(128)S(6)} %sub.4._, bf16[1024,2048]{1,0:T(8,128)(2,1)} %get-tuple-element.151.refs_0_, bf16[1024,512]{1,0:T(8,128)(2,1)} %get-tuple-element.152.refs_1_, bf16[1,1024,2048]{2,1,0:T(8,128)(2,1)} %bitcast.91, f32[128,2048]{1,0:T(8,128)} %pass_on.17.refs_3_), custom_call_target="tpu_custom_call" | custom-call | flops 40000000000 | bytes 19922944 | tf_op jit(solution)/shard_map/w_out_other/pallas_call | solution.py:359
  115.8 6.4 %mixed_back.1.refs_4_.d_ref = bf16[1024,512]{1,0:T(8,128)(2,1)} custom-call(bf16[1024,2048]{1,0:T(8,128)(2,1)} %get-tuple-element.150.g_ref.refs_4_, bf16[512,2048]{1,0:T(8,128)(2,1)} %w_ref.1, f32[8,128]{1,0:T(8,128)S(1)} %get-tuple-element.153.refs_0_), custom_call_target="tpu_custom_call" | custom-call | flops 2147483648 | bytes 5242880 | tf_op jit(solution)/shard_map/mixed_back/pallas_call | solution.py:382
  131.0 11.4 %attend_back.1 = (bf16[3,1024,512]{2,1,0:T(8,128)(2,1)}, f32[3,1,512]{2,1,0:T(1,128)S(1)}) custom-call(s32[1]{0:T(128)S(6)} %copy.114.refs_0_.len_ref, bf16[3,1024,512]{2,1,0:T(8,128)(2,1)} %get-tuple-element.155.q_ref.k_ref.v_ref, bf16[3,1024,512]{2,1,0:T(8,128)(2,1)} %get-tuple-element.155.q_ref.k_ref.v_ref, ...), custom_call_target="tpu_custom_call" | custom-call | flops 299999985664 | bytes 7340032 | tf_op jit(solution)/shard_map/attend_back/pallas_call | solution.py:433
  153.2 13.3 %w_out_own.1 = (f32[4,1,2560,256]{3,2,1,0:T(8,128)}, f32[8,128]{1,0:T(8,128)S(1)}) custom-call(s32[1]{0:T(128)} %bitcast.10._, bf16[1024,2048]{1,0:T(8,128)(2,1)} %get-tuple-element.151.refs_0_, bf16[1024,512]{1,0:T(8,128)(2,1)} %get-tuple-element.152.refs_1_, bf16[1,1024,2048]{2,1,0:T(8,128)(2,1)} %bitcast.92, ...), custom_call_target="tpu_custom_call" | custom-call | flops 40000000000 | bytes 19922944 | tf_op jit(solution)/shard_map/w_out_own/pallas_call | solution.py:359
  177.3 14.4 %backward_rows.4 = (bf16[1024,2048]{1,0:T(8,128)(2,1)}, f32[128,2048]{1,0:T(8,128)}, f32[128,2048]{1,0:T(8,128)}, f32[8,2048]{1,0:T(8,128)S(1)}, f32[1,2048]{1,0:T(1,128)S(1)}) custom-call(s32[2]{0:T(128)S(1)} %add_convert_fusion.refs_1_.refs_0_.flag_ref, f32[1,2048]{1,0:T(1,128)} %bitcast.79, f32[1,2048]{1,0:T(1,128)} %bitcast.87, ...), custom_call_target="tpu_custom_call" | custom-call | flops 299999985664 | bytes 31457280 | tf_op jit(solution)/shard_map/backward_rows/pallas_call | solution.py:565
  197.8 3.9 collective-permute-start.17
  201.7 13.3 %w_qkv_grad.1 = (f32[8,3,256,512]{3,2,1,0:T(8,128)}, f32[8,128]{1,0:T(8,128)S(1)}) custom-call(s32[1]{0:T(128)} %constant.27.clone.1._, bf16[1024,2048]{1,0:T(8,128)(2,1)} %get-tuple-element.173.refs_0_, bf16[3,1024,512]{2,1,0:T(8,128)(2,1)} %get-tuple-element.170.refs_6_.refs_1_, f32[128,2048]{1,0:T(8,128)} %pass_on.21.refs_2_.refs_3_), custom_call_target="tpu_custom_call" | custom-call | flops 40000000000 | bytes 19922944 | tf_op jit(solution)/shard_map/w_qkv_grad/pallas_call | solution.py:359
  223.5 14.3 %backward_rows.5 = (bf16[1024,2048]{1,0:T(8,128)(2,1)}, f32[128,2048]{1,0:T(8,128)}, f32[128,2048]{1,0:T(8,128)}, f32[8,2048]{1,0:T(8,128)S(1)}, f32[1,2048]{1,0:T(1,128)S(1)}) custom-call(s32[2]{0:T(128)S(1)} %add_convert_fusion.refs_1_.refs_0_.flag_ref, f32[1,2048]{1,0:T(1,128)} %bitcast.80, f32[1,2048]{1,0:T(1,128)} %bitcast.88, ...), custom_call_target="tpu_custom_call", output_to_operand_aliasing={{0}: (10, {})} | custom-call | flops 40000000000 | bytes 31457280 | tf_op jit(solution)/shard_map/backward_rows/pallas_call | solution.py:565
  244.3 3.5 collective-permute-start.18
  251.0 14.8 %backward_rows.6 = (bf16[1024,2048]{1,0:T(8,128)(2,1)}, f32[128,2048]{1,0:T(8,128)}, f32[128,2048]{1,0:T(8,128)}, f32[8,2048]{1,0:T(8,128)S(1)}, f32[1,2048]{1,0:T(1,128)S(1)}) custom-call(s32[2]{0:T(128)S(1)} %add_convert_fusion.refs_1_.refs_0_.flag_ref, f32[1,2048]{1,0:T(1,128)} %bitcast.81, f32[1,2048]{1,0:T(1,128)} %bitcast.89, ...), custom_call_target="tpu_custom_call", output_to_operand_aliasing={{0}: (10, {})} | custom-call | flops 40000000000 | bytes 31457280 | tf_op jit(solution)/shard_map/backward_rows/pallas_call | solution.py:565
  271.5 14.0 %backward_rows.7 = (bf16[1024,2048]{1,0:T(8,128)(2,1)}, f32[128,2048]{1,0:T(8,128)}, f32[128,2048]{1,0:T(8,128)}, f32[8,2048]{1,0:T(8,128)S(1)}, f32[1,2048]{1,0:T(1,128)S(1)}) custom-call(s32[2]{0:T(128)S(1)} %add_convert_fusion.refs_1_.refs_0_.flag_ref, f32[1,2048]{1,0:T(1,128)} %bitcast.82, f32[1,2048]{1,0:T(1,128)} %bitcast.90, ...), custom_call_target="tpu_custom_call", output_to_operand_aliasing={{0}: (10, {})} | custom-call | flops 40000000000 | bytes 31457280 | tf_op jit(solution)/shard_map/backward_rows/pallas_call | solution.py:565
  292.1 9.4 %w_in_other.1 = (f32[4,1,256,2048]{3,2,1,0:T(8,128)}, f32[8,128]{1,0:T(8,128)S(1)}) custom-call(s32[1]{0:T(128)S(6)} %sub.4._, bf16[1024,2048]{1,0:T(8,128)(2,1)} %get-tuple-element.197.refs_0_, bf16[1,1024,2048]{2,1,0:T(8,128)(2,1)} %bitcast.93, f32[128,2048]{1,0:T(8,128)} %pass_on.25.refs_2_.refs_3_), custom_call_target="tpu_custom_call" | custom-call | flops 40000000000 | bytes 16777216 | tf_op jit(solution)/shard_map/w_in_other/pallas_call | solution.py:359
  310.7 4.3 collective-permute-done.26.refs_1_
  316.8 10.0 %collective-permute-start.31 = (f32[128,2048]{1,0:T(8,128)}, f32[128,2048]{1,0:T(8,128)}, u32[]{:S(2)}, u32[]{:S(2)}) collective-permute-start(f32[128,2048]{1,0:T(8,128)} %get-tuple-element.209.refs_2_.refs_3_), channel_id=1, source_target_pairs={{0,1},{3,2},{1,0},{2,3},{4,5},{7,6},{5,4},{6,7},{8,9},{11,10},{9,8... | collective-permute-start | bytes 3145736 | tf_op jit(solution)/shard_map/ppermute | solution.py:796
  328.2 3.6 take_in.31
  336.5 4.9 %collective-permute-start.33 = (f32[128,2048]{1,0:T(8,128)}, f32[128,2048]{1,0:T(8,128)}, u32[]{:S(2)}, u32[]{:S(2)}) collective-permute-start(f32[128,2048]{1,0:T(8,128)} %pass_on.27.refs_3_), channel_id=1, source_target_pairs={{0,1},{3,2},{1,0},{2,3},{4,5},{7,6},{5,4},{6,7},{8,9},{11,10},{9,8... | collective-permute-start | bytes 3145736 | tf_op jit(solution)/shard_map/ppermute | solution.py:796
  341.4 11.7 %w_in_own.1 = (f32[4,1,256,2048]{3,2,1,0:T(8,128)}, f32[8,128]{1,0:T(8,128)S(1)}) custom-call(s32[1]{0:T(128)} %bitcast.10._, bf16[1024,2048]{1,0:T(8,128)(2,1)} %get-tuple-element.197.refs_0_, bf16[1,1024,2048]{2,1,0:T(8,128)(2,1)} %bitcast.94, f32[4,1,256,2048]{3,2,1,0:T(8,128)} %collective-permute-done.29.refs_2_, f32[128,2048]{1,0:T(8,128)} %pass_on.27.refs_3_), custom_call_target="tpu_custom_call" | custom-call | flops 40000000000 | bytes 16777216 | tf_op jit(solution)/shard_map/w_in_own/pallas_call | solution.py:359
  360.4 5.2 %collective-permute-start.32 = (f32[136,2048]{1,0:T(8,128)S(1)}, f32[136,2048]{1,0:T(8,128)}, u32[]{:S(2)}, u32[]{:S(2)}) collective-permute-start(f32[136,2048]{1,0:T(8,128)S(1)} %get-tuple-element.218.refs_0_.refs_3_), channel_id=1, source_target_pairs={{0,1},{3,2},{1,0},{2,3},{4,5},{7,6},{5,4},{6,7},{8,9},{11,10},{9,8... | collective-permute-start | bytes 3342344 | tf_op jit(solution)/shard_map/ppermute | solution.py:796
  369.1 5.0 %split_rows.1 = (f32[2048,256]{1,0:T(8,128)}, f32[512,256]{1,0:T(8,128)}) custom-call(f32[2560,256]{1,0:T(8,128)} %bitcast.35, f32[136,2048]{1,0:T(8,128)S(1)} %get-tuple-element.218.refs_0_.refs_3_, f32[3,256,512]{2,1,0:T(8,128)S(1)} %bitcast.38), custom_call_target="tpu_custom_call" | custom-call | bytes 5242880 | tf_op jit(solution)/shard_map/split_rows/pallas_call | solution.py:739
  381.0 16.5 %collective-permute-done.32.refs_1_ = f32[136,2048]{1,0:T(8,128)} collective-permute-done((f32[136,2048]{1,0:T(8,128)S(1)}, f32[136,2048]{1,0:T(8,128)}, u32[]{:S(2)}, u32[]{:S(2)}) %collective-permute-start.32) | collective-permute-done | bytes 1114144 | tf_op jit(solution)/shard_map/ppermute | solution.py:796
  402.4 17.4 %collective-permute-done.39.refs_1_ = f32[128,2048]{1,0:T(8,128)S(1)} collective-permute-done((f32[128,2048]{1,0:T(8,128)S(1)}, f32[128,2048]{1,0:T(8,128)S(1)}, u32[]{:S(2)}, u32[]{:S(2)}) %collective-permute-start.39) | collective-permute-done | bytes 1048608 | tf_op jit(solution)/shard_map/ppermute | solution.py:796
  423.2 19.1 %collective-permute-done.38.refs_1_ = f32[128,2048]{1,0:T(8,128)S(1)} collective-permute-done((f32[128,2048]{1,0:T(8,128)S(1)}, f32[128,2048]{1,0:T(8,128)S(1)}, u32[]{:S(2)}, u32[]{:S(2)}) %collective-permute-start.38) | collective-permute-done | bytes 1048608 | tf_op jit(solution)/shard_map/ppermute | solution.py:796
  443.7 21.2 %collective-permute-done.37.refs_1_ = f32[136,2048]{1,0:T(8,128)S(1)} collective-permute-done((f32[136,2048]{1,0:T(8,128)S(1)}, f32[136,2048]{1,0:T(8,128)S(1)}, u32[]{:S(2)}, u32[]{:S(2)}) %collective-permute-start.37) | collective-permute-done | bytes 1114144 | tf_op jit(solution)/shard_map/ppermute | solution.py:796
  (198 shorter events, 125.5 us)
Async XLA Ops:
  7.2 300.2 %reduce-scatter.10.cloned.1.call-start = ((), (), s32[]{:S(2)}) async-start(), calls=%async_computation.4 | async-start | bytes 13107200
  22.8 28.8 %collective-permute-start.1 = (f32[128,2048]{1,0:T(8,128)}, f32[128,2048]{1,0:T(8,128)S(1)}, u32[]{:S(2)}, u32[]{:S(2)}) collective-permute-start(f32[128,2048]{1,0:T(8,128)} %get-tuple-element.136.refs_2_), channel_id=1, source_target_pairs={{0,1},{3,2},{4,5},{7,6},{8,9},{11,10},{12,13},{15,14},{16,17},{19,... | collective-permute-start | bytes 3145736 | tf_op jit(solution)/shard_map/ppermute | solution.py:796
  42.8 31.3 %collective-permute-start = (f32[128,2048]{1,0:T(8,128)}, f32[128,2048]{1,0:T(8,128)}, u32[]{:S(2)}, u32[]{:S(2)}) collective-permute-start(f32[128,2048]{1,0:T(8,128)} %get-tuple-element.129.refs_2_), channel_id=1, source_target_pairs={{0,1},{3,2},{4,5},{7,6},{8,9},{11,10},{12,13},{15,14},{16,17},{19,... | collective-permute-start | bytes 3145736 | tf_op jit(solution)/shard_map/ppermute | solution.py:796
  45.1 53.0 %collective-permute-start.3 = (f32[128,2048]{1,0:T(8,128)}, f32[128,2048]{1,0:T(8,128)S(1)}, u32[]{:S(2)}, u32[]{:S(2)}) collective-permute-start(f32[128,2048]{1,0:T(8,128)} %get-tuple-element.141.refs_2_), channel_id=1, source_target_pairs={{0,1},{3,2},{4,5},{7,6},{8,9},{11,10},{12,13},{15,14},{16,17},{19,... | collective-permute-start | bytes 3145736 | tf_op jit(solution)/shard_map/ppermute | solution.py:796
  52.3 24.1 %collective-permute-start.4 = (f32[128,2048]{1,0:T(8,128)S(1)}, f32[128,2048]{1,0:T(8,128)S(1)}, u32[]{:S(2)}, u32[]{:S(2)}) collective-permute-start(f32[128,2048]{1,0:T(8,128)S(1)} %take_in.19.refs_24_.held_ref), channel_id=1, source_target_pairs={{1,2},{2,1},{5,6},{6,5},{9,10},{10,9},{13,14},{14,13},{17,18},{18,... | collective-permute-start | bytes 3145736 | tf_op jit(solution)/shard_map/ppermute | solution.py:806
  75.5 24.2 %collective-permute-start.2 = (f32[128,2048]{1,0:T(8,128)S(1)}, f32[128,2048]{1,0:T(8,128)S(1)}, u32[]{:S(2)}, u32[]{:S(2)}) collective-permute-start(f32[128,2048]{1,0:T(8,128)S(1)} %take_in.20.refs_1_.held_ref), channel_id=1, source_target_pairs={{1,2},{2,1},{5,6},{6,5},{9,10},{10,9},{13,14},{14,13},{17,18},{18,... | collective-permute-start | bytes 3145736 | tf_op jit(solution)/shard_map/ppermute | solution.py:806
  77.1 45.1 %collective-permute-start.6 = (f32[128,2048]{1,0:T(8,128)S(1)}, f32[128,2048]{1,0:T(8,128)S(1)}, u32[]{:S(2)}, u32[]{:S(2)}) collective-permute-start(f32[128,2048]{1,0:T(8,128)S(1)} %pass_on.16.refs_24_.refs_3_), channel_id=1, source_target_pairs={{0,1},{3,2},{1,0},{2,3},{4,5},{7,6},{5,4},{6,7},{8,9},{11,10},{9,8... | collective-permute-start | bytes 3145736 | tf_op jit(solution)/shard_map/ppermute | solution.py:796
  98.7 28.8 %collective-permute-start.7 = (f32[128,2048]{1,0:T(8,128)S(1)}, f32[128,2048]{1,0:T(8,128)S(1)}, u32[]{:S(2)}, u32[]{:S(2)}) collective-permute-start(f32[128,2048]{1,0:T(8,128)S(1)} %take_in.21.refs_1_.held_ref), channel_id=1, source_target_pairs={{1,2},{2,1},{5,6},{6,5},{9,10},{10,9},{13,14},{14,13},{17,18},{18,... | collective-permute-start | bytes 3145736 | tf_op jit(solution)/shard_map/ppermute | solution.py:806
  101.4 41.7 %collective-permute-start.5 = (f32[128,2048]{1,0:T(8,128)}, f32[128,2048]{1,0:T(8,128)}, u32[]{:S(2)}, u32[]{:S(2)}) collective-permute-start(f32[128,2048]{1,0:T(8,128)} %pass_on.17.refs_3_), channel_id=1, source_target_pairs={{0,1},{3,2},{1,0},{2,3},{4,5},{7,6},{5,4},{6,7},{8,9},{11,10},{9,8... | collective-permute-start | bytes 3145736 | tf_op jit(solution)/shard_map/ppermute | solution.py:796
  129.1 37.5 %collective-permute-start.9 = (f32[128,2048]{1,0:T(8,128)}, f32[128,2048]{1,0:T(8,128)}, u32[]{:S(2)}, u32[]{:S(2)}) collective-permute-start(f32[128,2048]{1,0:T(8,128)} %get-tuple-element.159.refs_0_.refs_3_), channel_id=1, source_target_pairs={{0,1},{3,2},{1,0},{2,3},{4,5},{7,6},{5,4},{6,7},{8,9},{11,10},{9,8... | collective-permute-start | bytes 3145736 | tf_op jit(solution)/shard_map/ppermute | solution.py:796
  145.5 27.7 %collective-permute-start.8 = (f32[128,2048]{1,0:T(8,128)S(1)}, f32[128,2048]{1,0:T(8,128)}, u32[]{:S(2)}, u32[]{:S(2)}) collective-permute-start(f32[128,2048]{1,0:T(8,128)S(1)} %get-tuple-element.161.refs_1_.held_ref), channel_id=1, source_target_pairs={{1,2},{2,1},{5,6},{6,5},{9,10},{10,9},{13,14},{14,13},{17,18},{18,... | collective-permute-start | bytes 3145736 | tf_op jit(solution)/shard_map/ppermute | solution.py:806
  149.9 41.9 %collective-permute-start.13 = (f32[128,2048]{1,0:T(8,128)}, f32[128,2048]{1,0:T(8,128)}, u32[]{:S(2)}, u32[]{:S(2)}) collective-permute-start(f32[128,2048]{1,0:T(8,128)} %pass_on.19.refs_4_.refs_3_), channel_id=1, source_target_pairs={{0,1},{3,2},{1,0},{2,3},{4,5},{7,6},{5,4},{6,7},{8,9},{11,10},{9,8... | collective-permute-start | bytes 3145736 | tf_op jit(solution)/shard_map/ppermute | solution.py:796
  166.6 201.1 %reduce-scatter.8.cloned.1.call-start = ((), (), s32[]{:S(2)}) async-start(), calls=%async_computation.3 | async-start | bytes 14155776 | tf_op jit(solution)/shard_map/reduce_scatter | solution.py:975
  175.8 39.2 %collective-permute-start.12 = (f32[128,2048]{1,0:T(8,128)}, f32[128,2048]{1,0:T(8,128)}, u32[]{:S(2)}, u32[]{:S(2)}) collective-permute-start(f32[128,2048]{1,0:T(8,128)} %pass_on.20.refs_10_.refs_3_), channel_id=1, source_target_pairs={{0,1},{3,2},{1,0},{2,3},{4,5},{7,6},{5,4},{6,7},{8,9},{11,10},{9,8... | collective-permute-start | bytes 3145736 | tf_op jit(solution)/shard_map/ppermute | solution.py:796
  194.4 25.1 %collective-permute-start.16 = (f32[128,2048]{1,0:T(8,128)S(1)}, f32[128,2048]{1,0:T(8,128)S(1)}, u32[]{:S(2)}, u32[]{:S(2)}) collective-permute-start(f32[128,2048]{1,0:T(8,128)S(1)} %get-tuple-element.175.refs_1_.held_ref), channel_id=1, source_target_pairs={{1,2},{2,1},{5,6},{6,5},{9,10},{10,9},{13,14},{14,13},{17,18},{18,... | collective-permute-start | bytes 3145736 | tf_op jit(solution)/shard_map/ppermute | solution.py:806
  197.8 40.1 %collective-permute-start.17 = (f32[128,2048]{1,0:T(8,128)}, f32[128,2048]{1,0:T(8,128)}, u32[]{:S(2)}, u32[]{:S(2)}) collective-permute-start(f32[128,2048]{1,0:T(8,128)} %pass_on.21.refs_2_.refs_3_), channel_id=1, source_target_pairs={{0,1},{3,2},{1,0},{2,3},{4,5},{7,6},{5,4},{6,7},{8,9},{11,10},{9,8... | collective-permute-start | bytes 3145736 | tf_op jit(solution)/shard_map/ppermute | solution.py:796
  217.7 25.2 %collective-permute-start.15 = (f32[128,2048]{1,0:T(8,128)S(1)}, f32[128,2048]{1,0:T(8,128)}, u32[]{:S(2)}, u32[]{:S(2)}) collective-permute-start(f32[128,2048]{1,0:T(8,128)S(1)} %get-tuple-element.177.refs_2_.held_ref), channel_id=1, source_target_pairs={{1,2},{2,1},{5,6},{6,5},{9,10},{10,9},{13,14},{14,13},{17,18},{18,... | collective-permute-start | bytes 3145736 | tf_op jit(solution)/shard_map/ppermute | solution.py:806
  221.2 44.6 %collective-permute-start.19 = (f32[128,2048]{1,0:T(8,128)}, f32[128,2048]{1,0:T(8,128)}, u32[]{:S(2)}, u32[]{:S(2)}) collective-permute-start(f32[128,2048]{1,0:T(8,128)} %get-tuple-element.181.refs_11_.refs_3_), channel_id=1, source_target_pairs={{0,1},{3,2},{1,0},{2,3},{4,5},{7,6},{5,4},{6,7},{8,9},{11,10},{9,8... | collective-permute-start | bytes 3145736 | tf_op jit(solution)/shard_map/ppermute | solution.py:796
  237.8 229.2 %reduce-scatter.12.cloned.1.call-start = ((), (), s32[]{:S(2)}) async-start(), calls=%async_computation.5 | async-start | bytes 10485760
  242.0 27.4 %collective-permute-start.20 = (f32[128,2048]{1,0:T(8,128)S(1)}, f32[128,2048]{1,0:T(8,128)S(1)}, u32[]{:S(2)}, u32[]{:S(2)}) collective-permute-start(f32[128,2048]{1,0:T(8,128)S(1)} %get-tuple-element.185.refs_1_.held_ref), channel_id=1, source_target_pairs={{1,2},{2,1},{5,6},{6,5},{9,10},{10,9},{13,14},{14,13},{17,18},{18,... | collective-permute-start | bytes 3145736 | tf_op jit(solution)/shard_map/ppermute | solution.py:806
  244.3 41.4 %collective-permute-start.18 = (f32[128,2048]{1,0:T(8,128)S(1)}, f32[128,2048]{1,0:T(8,128)S(1)}, u32[]{:S(2)}, u32[]{:S(2)}) collective-permute-start(f32[128,2048]{1,0:T(8,128)S(1)} %pass_on.23.refs_11_.refs_3_), channel_id=1, source_target_pairs={{0,1},{3,2},{1,0},{2,3},{4,5},{7,6},{5,4},{6,7},{8,9},{11,10},{9,8... | collective-permute-start | bytes 3145736 | tf_op jit(solution)/shard_map/ppermute | solution.py:796
  270.1 31.4 %collective-permute-start.23 = (f32[128,2048]{1,0:T(8,128)S(1)}, f32[128,2048]{1,0:T(8,128)S(1)}, u32[]{:S(2)}, u32[]{:S(2)}) collective-permute-start(f32[128,2048]{1,0:T(8,128)S(1)} %pass_on.24.refs_11_.refs_3_), channel_id=1, source_target_pairs={{0,1},{3,2},{1,0},{2,3},{4,5},{7,6},{5,4},{6,7},{8,9},{11,10},{9,8... | collective-permute-start | bytes 3145736 | tf_op jit(solution)/shard_map/ppermute | solution.py:796
  289.8 38.4 %collective-permute-start.22 = (f32[128,2048]{1,0:T(8,128)}, f32[128,2048]{1,0:T(8,128)}, u32[]{:S(2)}, u32[]{:S(2)}) collective-permute-start(f32[128,2048]{1,0:T(8,128)} %pass_on.25.refs_2_.refs_3_), channel_id=1, source_target_pairs={{0,1},{3,2},{1,0},{2,3},{4,5},{7,6},{5,4},{6,7},{8,9},{11,10},{9,8... | collective-permute-start | bytes 3145736 | tf_op jit(solution)/shard_map/ppermute | solution.py:796
  303.9 29.8 %collective-permute-start.30 = (f32[128,2048]{1,0:T(8,128)}, f32[128,2048]{1,0:T(8,128)}, u32[]{:S(2)}, u32[]{:S(2)}) collective-permute-start(f32[128,2048]{1,0:T(8,128)} %get-tuple-element.208.refs_2_.held_ref), channel_id=1, source_target_pairs={{1,2},{2,1},{5,6},{6,5},{9,10},{10,9},{13,14},{14,13},{17,18},{18,... | collective-permute-start | bytes 3145736 | tf_op jit(solution)/shard_map/ppermute | solution.py:806
  307.3 34.1 %collective-permute-start.29 = (f32[4,1,256,2048]{3,2,1,0:T(8,128)}, f32[4,1,256,2048]{3,2,1,0:T(8,128)}, u32[]{:S(2)}, u32[]{:S(2)}) collective-permute-start(f32[4,1,256,2048]{3,2,1,0:T(8,128)} %get-tuple-element.212), channel_id=1, source_target_pairs={{0,4},{4,0},{8,12},{12,8},{16,20},{20,16},{24,28},{28,24},{1,5},{5... | collective-permute-start | bytes 25165832 | tf_op jit(solution)/shard_map/ppermute | solution.py:944
  316.8 37.6 %collective-permute-start.31 = (f32[128,2048]{1,0:T(8,128)}, f32[128,2048]{1,0:T(8,128)}, u32[]{:S(2)}, u32[]{:S(2)}) collective-permute-start(f32[128,2048]{1,0:T(8,128)} %get-tuple-element.209.refs_2_.refs_3_), channel_id=1, source_target_pairs={{0,1},{3,2},{1,0},{2,3},{4,5},{7,6},{5,4},{6,7},{8,9},{11,10},{9,8... | collective-permute-start | bytes 3145736 | tf_op jit(solution)/shard_map/ppermute | solution.py:796
  331.8 26.8 %collective-permute-start.28 = (f32[128,2048]{1,0:T(8,128)}, f32[128,2048]{1,0:T(8,128)}, u32[]{:S(2)}, u32[]{:S(2)}) collective-permute-start(f32[128,2048]{1,0:T(8,128)} %get-tuple-element.211.refs_1_.held_ref), channel_id=1, source_target_pairs={{1,2},{2,1},{5,6},{6,5},{9,10},{10,9},{13,14},{14,13},{17,18},{18,... | collective-permute-start | bytes 3145736 | tf_op jit(solution)/shard_map/ppermute | solution.py:806
  336.5 37.6 %collective-permute-start.33 = (f32[128,2048]{1,0:T(8,128)}, f32[128,2048]{1,0:T(8,128)}, u32[]{:S(2)}, u32[]{:S(2)}) collective-permute-start(f32[128,2048]{1,0:T(8,128)} %pass_on.27.refs_3_), channel_id=1, source_target_pairs={{0,1},{3,2},{1,0},{2,3},{4,5},{7,6},{5,4},{6,7},{8,9},{11,10},{9,8... | collective-permute-start | bytes 3145736 | tf_op jit(solution)/shard_map/ppermute | solution.py:796
  360.4 37.1 %collective-permute-start.32 = (f32[136,2048]{1,0:T(8,128)S(1)}, f32[136,2048]{1,0:T(8,128)}, u32[]{:S(2)}, u32[]{:S(2)}) collective-permute-start(f32[136,2048]{1,0:T(8,128)S(1)} %get-tuple-element.218.refs_0_.refs_3_), channel_id=1, source_target_pairs={{0,1},{3,2},{1,0},{2,3},{4,5},{7,6},{5,4},{6,7},{8,9},{11,10},{9,8... | collective-permute-start | bytes 3342344 | tf_op jit(solution)/shard_map/ppermute | solution.py:796
  379.7 40.1 %collective-permute-start.39 = (f32[128,2048]{1,0:T(8,128)S(1)}, f32[128,2048]{1,0:T(8,128)S(1)}, u32[]{:S(2)}, u32[]{:S(2)}) collective-permute-start(f32[128,2048]{1,0:T(8,128)S(1)} %pass_on.29.refs_5_.refs_2_), channel_id=1, source_target_pairs={{1,0},{2,3},{5,4},{6,7},{9,8},{10,11},{13,12},{14,15},{17,16},{18,... | collective-permute-start | bytes 3145736 | tf_op jit(solution)/shard_map/ppermute | solution.py:796
  401.1 41.2 %collective-permute-start.38 = (f32[128,2048]{1,0:T(8,128)S(1)}, f32[128,2048]{1,0:T(8,128)S(1)}, u32[]{:S(2)}, u32[]{:S(2)}) collective-permute-start(f32[128,2048]{1,0:T(8,128)S(1)} %pass_on.30.refs_0_.refs_4_.refs_2_), channel_id=1, source_target_pairs={{1,0},{2,3},{5,4},{6,7},{9,8},{10,11},{13,12},{14,15},{17,16},{18,... | collective-permute-start | bytes 3145736 | tf_op jit(solution)/shard_map/ppermute | solution.py:796
  421.9 43.0 %collective-permute-start.37 = (f32[136,2048]{1,0:T(8,128)S(1)}, f32[136,2048]{1,0:T(8,128)S(1)}, u32[]{:S(2)}, u32[]{:S(2)}) collective-permute-start(f32[136,2048]{1,0:T(8,128)S(1)} %pass_on.31.refs_4_.refs_2_), channel_id=1, source_target_pairs={{1,0},{2,3},{5,4},{6,7},{9,8},{10,11},{13,12},{14,15},{17,16},{18,... | collective-permute-start | bytes 3342344 | tf_op jit(solution)/shard_map/ppermute | solution.py:796
  (46 other events, 808.4 us)
Sparse Core Ops, SparseCore 0:
  166.7 103.2 reduce-scatter.9
  274.0 93.6 reduce-scatter.7
  371.4 86.3 reduce-scatter.11

commit v5 on v4

--- a/solution.py
+++ b/solution.py
@@ -987,13 +987,18 @@
         after, half = pump(after, half)
         came_in = swap(half)
         after = small.add(after + [out_grads], True)
+        small.exchange()
+        (after,) = pump(after)
+        after = small.add(after)
+        small.exchange()
+        in_half, after = own_half("w_in_own", *in_parts, came_in, after)
+        after = small.add(after)
         while small.exchange():
             after = small.add(after)
         flat = small.values.reshape(-1)
         norms = jnp.concatenate([flat[: 4 * width].reshape(4, width), jnp.zeros((4, width), F32)])
         queue[-1] = append_rows(queue[-1], norms, after)
-        in_half, after = own_half("w_in_own", *in_parts, came_in, pump([queue[-1]])[0])
-        after, in_half = pump(after, in_half)
+        after, in_half = pump([queue[-1]], in_half)
         in_grads = over_chips(in_half)
         w_out_grad, w_dense_grad = split_rows(out_grads[0], units, after + [qkv_grads])
         after = [w_dense_grad]

time: 483 us -> 478 us (0.990)
  waiting for transfers between devices: 86.2 us -> 76.2 us
  starting transfers between devices: 85.9 us -> 91.7 us
    ppermute x19, starting transfers between devices: 62.1 us -> 68.2 us  [send(): self.came[step] = lax.ppermute(operand, 'tensor', pairs)]
    ppermute x19, waiting for transfers between devices: 79.7 us -> 73.8 us  [send(): self.came[step] = lax.ppermute(operand, 'tensor', pairs)]
    unnamed x72 -> x78, local copies, waits for them, and re-layouts: 13.2 us -> 13.9 us
  transfers between devices with their start and end apart: 43 -> 43, of which waited for: 8 -> 7; matrix products, arithmetic and copies ran while one was open for 1% -> 1% of each run, Pallas kernels for 54% -> 54%
where the time goes in v5:
time: 478 us; the launch traced here: 469 us
  Pallas kernels  269 us (56%)
  starting transfers between devices  91.7 us (19%)
  waiting for transfers between devices  76.2 us (16%)
  local copies, waits for them, and re-layouts  16.4 us (3%)
  between operations  15.8 us (3%)
    ppermute x19, waiting for transfers between devices, send(): self.came[step] = lax.ppermute(operand, 'tensor', pairs)  73.8 us
    ppermute x19, starting transfers between devices, send(): self.came[step] = lax.ppermute(operand, 'tensor', pairs)  68.2 us
    pallas_call x4, Pallas kernels, forward_rows(): pl.pallas_call(body, grid=(1,), in_specs=specs, out_specs=[HBM] * (6 + pa...  60.5 us
    pallas_call x5, Pallas kernels, pair_product(): pl.pallas_call(body, grid_spec=pltpu.PrefetchScalarGridSpec(num_scalar_pr...  58.1 us
    pallas_call x4, Pallas kernels, backward_rows(): pl.pallas_call(body, grid=(1,), in_specs=specs, out_specs=[HBM] * (1 + pa...  57.5 us
    pallas_call x19, Pallas kernels, take_in(): pl.pallas_call(body, in_specs=specs, out_specs=out_specs, out_shape=outs,...  39.4 us
    pallas_call x16, Pallas kernels, pass_on(): pl.pallas_call(body, in_specs=[SMEM] + [VMEM] * (2 + len(more)) + [HBM] *...  26 us
    ppermute x16, starting transfers between devices, pump(): self.met[step] = lax.ppermute(held, 'tensor', [(1, 2), (2, 1)])  20.2 us
  transfers between devices with their start and end apart: 43, of which 7 were waited for; matrix products, arithmetic and copies ran while one was open for 1% of the time, Pallas kernels for 54%

profile of v5, /device:TPU:0, one launch (start us, length us, event | category | flops | bytes accessed | tf_op | source)
XLA Modules:
  0.0 469.4 jit_solution(1281708699464525455)
XLA Ops:
  8.0 14.9 %forward_rows.4 = (bf16[1024,2048]{1,0:T(8,128)(2,1)}, bf16[1024,2048]{1,0:T(8,128)(2,1)}, bf16[3,1024,512]{2,1,0:T(8,128)(2,1)}, bf16[1024,512]{1,0:T(8,128)(2,...) custom-call(s32[1]{0:T(128)S(6)} %copy.114.refs_0_.len_ref, ...), custom_call_target="tpu_custom_call" | custom-call | flops 40000000000 | bytes 35651584 | tf_op jit(solution)/shard_map/forward_rows/pallas_call | solution.py:276
  22.8 5.2 %collective-permute-start.1 = (f32[128,2048]{1,0:T(8,128)}, f32[128,2048]{1,0:T(8,128)S(1)}, u32[]{:S(2)}, u32[]{:S(2)}) collective-permute-start(f32[128,2048]{1,0:T(8,128)} %get-tuple-element.136.refs_2_), channel_id=1, source_target_pairs={{0,1},{3,2},{4,5},{7,6},{8,9},{11,10},{12,13},{15,14},{16,17},{19,... | collective-permute-start | bytes 3145736 | tf_op jit(solution)/shard_map/ppermute | solution.py:796
  28.1 14.7 %forward_rows.5 = (bf16[1024,2048]{1,0:T(8,128)(2,1)}, bf16[1024,2048]{1,0:T(8,128)(2,1)}, bf16[3,1024,512]{2,1,0:T(8,128)(2,1)}, bf16[1024,512]{1,0:T(8,128)(2,...) custom-call(s32[1]{0:T(128)S(6)} %copy.114.refs_0_.len_ref, ...), custom_call_target="tpu_custom_call", output_to_operand_aliasing={{0}: (18, {}), {1}: (19, {}), {2}: (20, {}), {3}: (21, {}),... | custom-call | flops 40000000000 | bytes 35651584 | tf_op jit(solution)/shard_map/forward_rows/pallas_call | solution.py:276
  46.4 5.1 %mask_rows.1 = (bf16[1024,2048]{1,0:T(8,128)(2,1)}, f32[1,2048]{1,0:T(1,128)S(1)}) custom-call(s32[1]{0:T(128)S(6)} %copy.114.refs_0_.len_ref, bf16[1024,2048]{1,0:T(8,128)(2,1)} %refs_1_.1, f32[8,128]{1,0:T(8,128)S(1)} %get-tuple-element.137.refs_2_), custom_call_target="tpu_custom_call" | custom-call | flops 40000000000 | bytes 8388608 | tf_op jit(solution)/shard_map/mask_rows/pallas_call | solution.py:315
  53.5 15.2 %forward_rows.6 = (bf16[1024,2048]{1,0:T(8,128)(2,1)}, bf16[1024,2048]{1,0:T(8,128)(2,1)}, bf16[3,1024,512]{2,1,0:T(8,128)(2,1)}, bf16[1024,512]{1,0:T(8,128)(2,...) custom-call(s32[1]{0:T(128)S(6)} %copy.114.refs_0_.len_ref, ...), custom_call_target="tpu_custom_call", output_to_operand_aliasing={{0}: (18, {}), {1}: (19, {}), {2}: (20, {}), {3}: (21, {}),... | custom-call | flops 40000000000 | bytes 35651584 | tf_op jit(solution)/shard_map/forward_rows/pallas_call | solution.py:276
  68.7 5.4 %collective-permute-done.refs_1_ = f32[128,2048]{1,0:T(8,128)} collective-permute-done((f32[128,2048]{1,0:T(8,128)}, f32[128,2048]{1,0:T(8,128)}, u32[]{:S(2)}, u32[]{:S(2)}) %collective-permute-start) | collective-permute-done | bytes 1048608 | tf_op jit(solution)/shard_map/ppermute | solution.py:796
  77.1 5.3 %collective-permute-start.6 = (f32[128,2048]{1,0:T(8,128)S(1)}, f32[128,2048]{1,0:T(8,128)S(1)}, u32[]{:S(2)}, u32[]{:S(2)}) collective-permute-start(f32[128,2048]{1,0:T(8,128)S(1)} %pass_on.16.refs_24_.refs_3_), channel_id=1, source_target_pairs={{0,1},{3,2},{1,0},{2,3},{4,5},{7,6},{5,4},{6,7},{8,9},{11,10},{9,8... | collective-permute-start | bytes 3145736 | tf_op jit(solution)/shard_map/ppermute | solution.py:796
  82.4 15.6 %forward_rows.7 = (bf16[1024,2048]{1,0:T(8,128)(2,1)}, bf16[1024,2048]{1,0:T(8,128)(2,1)}, bf16[3,1024,512]{2,1,0:T(8,128)(2,1)}, bf16[1024,512]{1,0:T(8,128)(2,...) custom-call(s32[1]{0:T(128)S(6)} %copy.114.refs_0_.len_ref, ...), custom_call_target="tpu_custom_call", output_to_operand_aliasing={{0}: (18, {}), {1}: (19, {}), {2}: (20, {}), {3}: (21, {}),... | custom-call | flops 40000000000 | bytes 35651584 | tf_op jit(solution)/shard_map/forward_rows/pallas_call | solution.py:276
  101.4 3.8 collective-permute-start.5
  105.1 10.7 %w_out_other.1 = (f32[4,1,2560,256]{3,2,1,0:T(8,128)}, f32[8,128]{1,0:T(8,128)S(1)}) custom-call(s32[1]{0:T(128)S(6)} %sub.4._, bf16[1024,2048]{1,0:T(8,128)(2,1)} %get-tuple-element.151.refs_0_, bf16[1024,512]{1,0:T(8,128)(2,1)} %get-tuple-element.152.refs_1_, bf16[1,1024,2048]{2,1,0:T(8,128)(2,1)} %bitcast.91, f32[128,2048]{1,0:T(8,128)} %pass_on.17.refs_3_), custom_call_target="tpu_custom_call" | custom-call | flops 40000000000 | bytes 19922944 | tf_op jit(solution)/shard_map/w_out_other/pallas_call | solution.py:359
  115.8 6.3 %mixed_back.1.refs_4_.d_ref = bf16[1024,512]{1,0:T(8,128)(2,1)} custom-call(bf16[1024,2048]{1,0:T(8,128)(2,1)} %get-tuple-element.150.g_ref.refs_4_, bf16[512,2048]{1,0:T(8,128)(2,1)} %w_ref.1, f32[8,128]{1,0:T(8,128)S(1)} %get-tuple-element.153.refs_0_), custom_call_target="tpu_custom_call" | custom-call | flops 2147483648 | bytes 5242880 | tf_op jit(solution)/shard_map/mixed_back/pallas_call | solution.py:382
  131.0 11.4 %attend_back.1 = (bf16[3,1024,512]{2,1,0:T(8,128)(2,1)}, f32[3,1,512]{2,1,0:T(1,128)S(1)}) custom-call(s32[1]{0:T(128)S(6)} %copy.114.refs_0_.len_ref, bf16[3,1024,512]{2,1,0:T(8,128)(2,1)} %get-tuple-element.155.q_ref.k_ref.v_ref, bf16[3,1024,512]{2,1,0:T(8,128)(2,1)} %get-tuple-element.155.q_ref.k_ref.v_ref, ...), custom_call_target="tpu_custom_call" | custom-call | flops 299999985664 | bytes 7340032 | tf_op jit(solution)/shard_map/attend_back/pallas_call | solution.py:433
  149.9 3.3 collective-permute-start.13
  153.2 13.2 %w_out_own.1 = (f32[4,1,2560,256]{3,2,1,0:T(8,128)}, f32[8,128]{1,0:T(8,128)S(1)}) custom-call(s32[1]{0:T(128)} %bitcast.10._, bf16[1024,2048]{1,0:T(8,128)(2,1)} %get-tuple-element.151.refs_0_, bf16[1024,512]{1,0:T(8,128)(2,1)} %get-tuple-element.152.refs_1_, bf16[1,1024,2048]{2,1,0:T(8,128)(2,1)} %bitcast.92, ...), custom_call_target="tpu_custom_call" | custom-call | flops 40000000000 | bytes 19922944 | tf_op jit(solution)/shard_map/w_out_own/pallas_call | solution.py:359
  167.7 3.4 take_in.24
  177.4 14.4 %backward_rows.4 = (bf16[1024,2048]{1,0:T(8,128)(2,1)}, f32[128,2048]{1,0:T(8,128)}, f32[128,2048]{1,0:T(8,128)}, f32[8,2048]{1,0:T(8,128)S(1)}, f32[1,2048]{1,0:T(1,128)S(1)}) custom-call(s32[2]{0:T(128)S(1)} %add_convert_fusion.refs_1_.refs_0_.flag_ref, f32[1,2048]{1,0:T(1,128)} %bitcast.79, f32[1,2048]{1,0:T(1,128)} %bitcast.87, ...), custom_call_target="tpu_custom_call" | custom-call | flops 299999985664 | bytes 31457280 | tf_op jit(solution)/shard_map/backward_rows/pallas_call | solution.py:565
  197.9 3.9 collective-permute-start.17
  201.7 13.2 %w_qkv_grad.1 = (f32[8,3,256,512]{3,2,1,0:T(8,128)}, f32[8,128]{1,0:T(8,128)S(1)}) custom-call(s32[1]{0:T(128)} %constant.27.clone.1._, bf16[1024,2048]{1,0:T(8,128)(2,1)} %get-tuple-element.173.refs_0_, bf16[3,1024,512]{2,1,0:T(8,128)(2,1)} %get-tuple-element.170.refs_6_.refs_1_, f32[128,2048]{1,0:T(8,128)} %pass_on.21.refs_2_.refs_3_), custom_call_target="tpu_custom_call" | custom-call | flops 40000000000 | bytes 19922944 | tf_op jit(solution)/shard_map/w_qkv_grad/pallas_call | solution.py:359
  223.5 14.2 %backward_rows.5 = (bf16[1024,2048]{1,0:T(8,128)(2,1)}, f32[128,2048]{1,0:T(8,128)}, f32[128,2048]{1,0:T(8,128)}, f32[8,2048]{1,0:T(8,128)S(1)}, f32[1,2048]{1,0:T(1,128)S(1)}) custom-call(s32[2]{0:T(128)S(1)} %add_convert_fusion.refs_1_.refs_0_.flag_ref, f32[1,2048]{1,0:T(1,128)} %bitcast.80, f32[1,2048]{1,0:T(1,128)} %bitcast.88, ...), custom_call_target="tpu_custom_call", output_to_operand_aliasing={{0}: (10, {})} | custom-call | flops 40000000000 | bytes 31457280 | tf_op jit(solution)/shard_map/backward_rows/pallas_call | solution.py:565
  244.3 3.5 collective-permute-start.18
  251.0 14.8 %backward_rows.6 = (bf16[1024,2048]{1,0:T(8,128)(2,1)}, f32[128,2048]{1,0:T(8,128)}, f32[128,2048]{1,0:T(8,128)}, f32[8,2048]{1,0:T(8,128)S(1)}, f32[1,2048]{1,0:T(1,128)S(1)}) custom-call(s32[2]{0:T(128)S(1)} %add_convert_fusion.refs_1_.refs_0_.flag_ref, f32[1,2048]{1,0:T(1,128)} %bitcast.81, f32[1,2048]{1,0:T(1,128)} %bitcast.89, ...), custom_call_target="tpu_custom_call", output_to_operand_aliasing={{0}: (10, {})} | custom-call | flops 40000000000 | bytes 31457280 | tf_op jit(solution)/shard_map/backward_rows/pallas_call | solution.py:565
  271.4 14.0 %backward_rows.7 = (bf16[1024,2048]{1,0:T(8,128)(2,1)}, f32[128,2048]{1,0:T(8,128)}, f32[128,2048]{1,0:T(8,128)}, f32[8,2048]{1,0:T(8,128)S(1)}, f32[1,2048]{1,0:T(1,128)S(1)}) custom-call(s32[2]{0:T(128)S(1)} %add_convert_fusion.refs_1_.refs_0_.flag_ref, f32[1,2048]{1,0:T(1,128)} %bitcast.82, f32[1,2048]{1,0:T(1,128)} %bitcast.90, ...), custom_call_target="tpu_custom_call", output_to_operand_aliasing={{0}: (10, {})} | custom-call | flops 40000000000 | bytes 31457280 | tf_op jit(solution)/shard_map/backward_rows/pallas_call | solution.py:565
  291.9 9.4 %w_in_other.1 = (f32[4,1,256,2048]{3,2,1,0:T(8,128)}, f32[8,128]{1,0:T(8,128)S(1)}) custom-call(s32[1]{0:T(128)S(6)} %sub.4._, bf16[1024,2048]{1,0:T(8,128)(2,1)} %get-tuple-element.197.refs_0_, bf16[1,1024,2048]{2,1,0:T(8,128)(2,1)} %bitcast.93, f32[128,2048]{1,0:T(8,128)S(1)} %pass_on.25.refs_2_.refs_3_), custom_call_target="tpu_custom_call" | custom-call | flops 40000000000 | bytes 16777216 | tf_op jit(solution)/shard_map/w_in_other/pallas_call | solution.py:359
  309.4 11.4 %collective-permute-start.31 = (f32[128,2048]{1,0:T(8,128)}, f32[128,2048]{1,0:T(8,128)}, u32[]{:S(2)}, u32[]{:S(2)}) collective-permute-start(f32[128,2048]{1,0:T(8,128)} %get-tuple-element.208.refs_2_.refs_3_), channel_id=1, source_target_pairs={{0,1},{3,2},{1,0},{2,3},{4,5},{7,6},{5,4},{6,7},{8,9},{11,10},{9,8... | collective-permute-start | bytes 3145736 | tf_op jit(solution)/shard_map/ppermute | solution.py:796
  327.5 13.4 %collective-permute-start.33 = (f32[128,2048]{1,0:T(8,128)}, f32[128,2048]{1,0:T(8,128)}, u32[]{:S(2)}, u32[]{:S(2)}) collective-permute-start(f32[128,2048]{1,0:T(8,128)} %pass_on.27.refs_2_.refs_3_), channel_id=1, source_target_pairs={{0,1},{3,2},{1,0},{2,3},{4,5},{7,6},{5,4},{6,7},{8,9},{11,10},{9,8... | collective-permute-start | bytes 3145736 | tf_op jit(solution)/shard_map/ppermute | solution.py:796
  342.4 11.6 %w_in_own.1 = (f32[4,1,256,2048]{3,2,1,0:T(8,128)}, f32[8,128]{1,0:T(8,128)S(1)}) custom-call(s32[1]{0:T(128)} %bitcast.10._, bf16[1024,2048]{1,0:T(8,128)(2,1)} %get-tuple-element.197.refs_0_, bf16[1,1024,2048]{2,1,0:T(8,128)(2,1)} %bitcast.94, f32[4,1,256,2048]{3,2,1,0:T(8,128)} %collective-permute-done.30.refs_2_, f32[108,128]{1,0:T(8,128)S(1)} %add_up.4.refs_3_.refs_0_), custom_call_target="tpu_custom_call" | custom-call | flops 40000000000 | bytes 16777216 | tf_op jit(solution)/shard_map/w_in_own/pallas_call | solution.py:359
  356.6 3.5 take_in.32
  369.0 4.9 %split_rows.1 = (f32[2048,256]{1,0:T(8,128)}, f32[512,256]{1,0:T(8,128)}) custom-call(f32[2560,256]{1,0:T(8,128)} %bitcast.35, f32[136,2048]{1,0:T(8,128)} %get-tuple-element.218.refs_0_.refs_3_, f32[3,256,512]{2,1,0:T(8,128)S(1)} %bitcast.38), custom_call_target="tpu_custom_call" | custom-call | bytes 5242880 | tf_op jit(solution)/shard_map/split_rows/pallas_call | solution.py:739
  381.1 10.8 %collective-permute-done.32.refs_1_ = f32[136,2048]{1,0:T(8,128)} collective-permute-done((f32[136,2048]{1,0:T(8,128)}, f32[136,2048]{1,0:T(8,128)}, u32[]{:S(2)}, u32[]{:S(2)}) %collective-permute-start.32) | collective-permute-done | bytes 1114144 | tf_op jit(solution)/shard_map/ppermute | solution.py:796
  397.4 18.4 %collective-permute-done.39.refs_1_ = f32[128,2048]{1,0:T(8,128)S(1)} collective-permute-done((f32[128,2048]{1,0:T(8,128)S(1)}, f32[128,2048]{1,0:T(8,128)S(1)}, u32[]{:S(2)}, u32[]{:S(2)}) %collective-permute-start.39) | collective-permute-done | bytes 1048608 | tf_op jit(solution)/shard_map/ppermute | solution.py:796
  419.2 18.5 %collective-permute-done.38.refs_1_ = f32[128,2048]{1,0:T(8,128)S(1)} collective-permute-done((f32[128,2048]{1,0:T(8,128)S(1)}, f32[128,2048]{1,0:T(8,128)S(1)}, u32[]{:S(2)}, u32[]{:S(2)}) %collective-permute-start.38) | collective-permute-done | bytes 1048608 | tf_op jit(solution)/shard_map/ppermute | solution.py:796
  439.1 20.6 %collective-permute-done.37.refs_1_ = f32[136,2048]{1,0:T(8,128)S(1)} collective-permute-done((f32[136,2048]{1,0:T(8,128)S(1)}, f32[136,2048]{1,0:T(8,128)S(1)}, u32[]{:S(2)}, u32[]{:S(2)}) %collective-permute-start.37) | collective-permute-done | bytes 1114144 | tf_op jit(solution)/shard_map/ppermute | solution.py:796
  (204 shorter events, 119.5 us)
Async XLA Ops:
  7.2 298.9 %reduce-scatter.10.cloned.1.call-start = ((), (), s32[]{:S(2)}) async-start(), calls=%async_computation.4 | async-start | bytes 13107200
  22.8 28.8 %collective-permute-start.1 = (f32[128,2048]{1,0:T(8,128)}, f32[128,2048]{1,0:T(8,128)S(1)}, u32[]{:S(2)}, u32[]{:S(2)}) collective-permute-start(f32[128,2048]{1,0:T(8,128)} %get-tuple-element.136.refs_2_), channel_id=1, source_target_pairs={{0,1},{3,2},{4,5},{7,6},{8,9},{11,10},{12,13},{15,14},{16,17},{19,... | collective-permute-start | bytes 3145736 | tf_op jit(solution)/shard_map/ppermute | solution.py:796
  42.8 31.3 %collective-permute-start = (f32[128,2048]{1,0:T(8,128)}, f32[128,2048]{1,0:T(8,128)}, u32[]{:S(2)}, u32[]{:S(2)}) collective-permute-start(f32[128,2048]{1,0:T(8,128)} %get-tuple-element.129.refs_2_), channel_id=1, source_target_pairs={{0,1},{3,2},{4,5},{7,6},{8,9},{11,10},{12,13},{15,14},{16,17},{19,... | collective-permute-start | bytes 3145736 | tf_op jit(solution)/shard_map/ppermute | solution.py:796
  45.1 53.0 %collective-permute-start.3 = (f32[128,2048]{1,0:T(8,128)}, f32[128,2048]{1,0:T(8,128)S(1)}, u32[]{:S(2)}, u32[]{:S(2)}) collective-permute-start(f32[128,2048]{1,0:T(8,128)} %get-tuple-element.141.refs_2_), channel_id=1, source_target_pairs={{0,1},{3,2},{4,5},{7,6},{8,9},{11,10},{12,13},{15,14},{16,17},{19,... | collective-permute-start | bytes 3145736 | tf_op jit(solution)/shard_map/ppermute | solution.py:796
  52.3 24.1 %collective-permute-start.4 = (f32[128,2048]{1,0:T(8,128)S(1)}, f32[128,2048]{1,0:T(8,128)S(1)}, u32[]{:S(2)}, u32[]{:S(2)}) collective-permute-start(f32[128,2048]{1,0:T(8,128)S(1)} %take_in.19.refs_24_.held_ref), channel_id=1, source_target_pairs={{1,2},{2,1},{5,6},{6,5},{9,10},{10,9},{13,14},{14,13},{17,18},{18,... | collective-permute-start | bytes 3145736 | tf_op jit(solution)/shard_map/ppermute | solution.py:806
  75.5 24.2 %collective-permute-start.2 = (f32[128,2048]{1,0:T(8,128)S(1)}, f32[128,2048]{1,0:T(8,128)S(1)}, u32[]{:S(2)}, u32[]{:S(2)}) collective-permute-start(f32[128,2048]{1,0:T(8,128)S(1)} %take_in.20.refs_1_.held_ref), channel_id=1, source_target_pairs={{1,2},{2,1},{5,6},{6,5},{9,10},{10,9},{13,14},{14,13},{17,18},{18,... | collective-permute-start | bytes 3145736 | tf_op jit(solution)/shard_map/ppermute | solution.py:806
  77.1 45.0 %collective-permute-start.6 = (f32[128,2048]{1,0:T(8,128)S(1)}, f32[128,2048]{1,0:T(8,128)S(1)}, u32[]{:S(2)}, u32[]{:S(2)}) collective-permute-start(f32[128,2048]{1,0:T(8,128)S(1)} %pass_on.16.refs_24_.refs_3_), channel_id=1, source_target_pairs={{0,1},{3,2},{1,0},{2,3},{4,5},{7,6},{5,4},{6,7},{8,9},{11,10},{9,8... | collective-permute-start | bytes 3145736 | tf_op jit(solution)/shard_map/ppermute | solution.py:796
  98.8 28.7 %collective-permute-start.7 = (f32[128,2048]{1,0:T(8,128)S(1)}, f32[128,2048]{1,0:T(8,128)S(1)}, u32[]{:S(2)}, u32[]{:S(2)}) collective-permute-start(f32[128,2048]{1,0:T(8,128)S(1)} %take_in.21.refs_1_.held_ref), channel_id=1, source_target_pairs={{1,2},{2,1},{5,6},{6,5},{9,10},{10,9},{13,14},{14,13},{17,18},{18,... | collective-permute-start | bytes 3145736 | tf_op jit(solution)/shard_map/ppermute | solution.py:806
  101.4 41.7 %collective-permute-start.5 = (f32[128,2048]{1,0:T(8,128)}, f32[128,2048]{1,0:T(8,128)}, u32[]{:S(2)}, u32[]{:S(2)}) collective-permute-start(f32[128,2048]{1,0:T(8,128)} %pass_on.17.refs_3_), channel_id=1, source_target_pairs={{0,1},{3,2},{1,0},{2,3},{4,5},{7,6},{5,4},{6,7},{8,9},{11,10},{9,8... | collective-permute-start | bytes 3145736 | tf_op jit(solution)/shard_map/ppermute | solution.py:796
  129.1 37.4 %collective-permute-start.9 = (f32[128,2048]{1,0:T(8,128)}, f32[128,2048]{1,0:T(8,128)}, u32[]{:S(2)}, u32[]{:S(2)}) collective-permute-start(f32[128,2048]{1,0:T(8,128)} %get-tuple-element.159.refs_0_.refs_3_), channel_id=1, source_target_pairs={{0,1},{3,2},{1,0},{2,3},{4,5},{7,6},{5,4},{6,7},{8,9},{11,10},{9,8... | collective-permute-start | bytes 3145736 | tf_op jit(solution)/shard_map/ppermute | solution.py:796
  145.5 27.6 %collective-permute-start.8 = (f32[128,2048]{1,0:T(8,128)S(1)}, f32[128,2048]{1,0:T(8,128)}, u32[]{:S(2)}, u32[]{:S(2)}) collective-permute-start(f32[128,2048]{1,0:T(8,128)S(1)} %get-tuple-element.161.refs_1_.held_ref), channel_id=1, source_target_pairs={{1,2},{2,1},{5,6},{6,5},{9,10},{10,9},{13,14},{14,13},{17,18},{18,... | collective-permute-start | bytes 3145736 | tf_op jit(solution)/shard_map/ppermute | solution.py:806
  149.9 42.0 %collective-permute-start.13 = (f32[128,2048]{1,0:T(8,128)}, f32[128,2048]{1,0:T(8,128)}, u32[]{:S(2)}, u32[]{:S(2)}) collective-permute-start(f32[128,2048]{1,0:T(8,128)} %pass_on.19.refs_4_.refs_3_), channel_id=1, source_target_pairs={{0,1},{3,2},{1,0},{2,3},{4,5},{7,6},{5,4},{6,7},{8,9},{11,10},{9,8... | collective-permute-start | bytes 3145736 | tf_op jit(solution)/shard_map/ppermute | solution.py:796
  166.5 201.1 %reduce-scatter.8.cloned.1.call-start = ((), (), s32[]{:S(2)}) async-start(), calls=%async_computation.3 | async-start | bytes 14155776 | tf_op jit(solution)/shard_map/reduce_scatter | solution.py:975
  175.7 39.3 %collective-permute-start.12 = (f32[128,2048]{1,0:T(8,128)}, f32[128,2048]{1,0:T(8,128)}, u32[]{:S(2)}, u32[]{:S(2)}) collective-permute-start(f32[128,2048]{1,0:T(8,128)} %pass_on.20.refs_10_.refs_3_), channel_id=1, source_target_pairs={{0,1},{3,2},{1,0},{2,3},{4,5},{7,6},{5,4},{6,7},{8,9},{11,10},{9,8... | collective-permute-start | bytes 3145736 | tf_op jit(solution)/shard_map/ppermute | solution.py:796
  194.4 25.1 %collective-permute-start.16 = (f32[128,2048]{1,0:T(8,128)S(1)}, f32[128,2048]{1,0:T(8,128)S(1)}, u32[]{:S(2)}, u32[]{:S(2)}) collective-permute-start(f32[128,2048]{1,0:T(8,128)S(1)} %get-tuple-element.175.refs_1_.held_ref), channel_id=1, source_target_pairs={{1,2},{2,1},{5,6},{6,5},{9,10},{10,9},{13,14},{14,13},{17,18},{18,... | collective-permute-start | bytes 3145736 | tf_op jit(solution)/shard_map/ppermute | solution.py:806
  197.9 40.0 %collective-permute-start.17 = (f32[128,2048]{1,0:T(8,128)}, f32[128,2048]{1,0:T(8,128)}, u32[]{:S(2)}, u32[]{:S(2)}) collective-permute-start(f32[128,2048]{1,0:T(8,128)} %pass_on.21.refs_2_.refs_3_), channel_id=1, source_target_pairs={{0,1},{3,2},{1,0},{2,3},{4,5},{7,6},{5,4},{6,7},{8,9},{11,10},{9,8... | collective-permute-start | bytes 3145736 | tf_op jit(solution)/shard_map/ppermute | solution.py:796
  217.7 25.2 %collective-permute-start.15 = (f32[128,2048]{1,0:T(8,128)S(1)}, f32[128,2048]{1,0:T(8,128)}, u32[]{:S(2)}, u32[]{:S(2)}) collective-permute-start(f32[128,2048]{1,0:T(8,128)S(1)} %get-tuple-element.177.refs_2_.held_ref), channel_id=1, source_target_pairs={{1,2},{2,1},{5,6},{6,5},{9,10},{10,9},{13,14},{14,13},{17,18},{18,... | collective-permute-start | bytes 3145736 | tf_op jit(solution)/shard_map/ppermute | solution.py:806
  221.2 44.6 %collective-permute-start.19 = (f32[128,2048]{1,0:T(8,128)}, f32[128,2048]{1,0:T(8,128)}, u32[]{:S(2)}, u32[]{:S(2)}) collective-permute-start(f32[128,2048]{1,0:T(8,128)} %get-tuple-element.181.refs_11_.refs_3_), channel_id=1, source_target_pairs={{0,1},{3,2},{1,0},{2,3},{4,5},{7,6},{5,4},{6,7},{8,9},{11,10},{9,8... | collective-permute-start | bytes 3145736 | tf_op jit(solution)/shard_map/ppermute | solution.py:796
  237.8 224.0 %reduce-scatter.12.cloned.1.call-start = ((), (), s32[]{:S(2)}) async-start(), calls=%async_computation.5 | async-start | bytes 10485760
  242.0 27.4 %collective-permute-start.20 = (f32[128,2048]{1,0:T(8,128)S(1)}, f32[128,2048]{1,0:T(8,128)S(1)}, u32[]{:S(2)}, u32[]{:S(2)}) collective-permute-start(f32[128,2048]{1,0:T(8,128)S(1)} %get-tuple-element.185.refs_1_.held_ref), channel_id=1, source_target_pairs={{1,2},{2,1},{5,6},{6,5},{9,10},{10,9},{13,14},{14,13},{17,18},{18,... | collective-permute-start | bytes 3145736 | tf_op jit(solution)/shard_map/ppermute | solution.py:806
  244.3 41.3 %collective-permute-start.18 = (f32[128,2048]{1,0:T(8,128)S(1)}, f32[128,2048]{1,0:T(8,128)S(1)}, u32[]{:S(2)}, u32[]{:S(2)}) collective-permute-start(f32[128,2048]{1,0:T(8,128)S(1)} %pass_on.23.refs_11_.refs_3_), channel_id=1, source_target_pairs={{0,1},{3,2},{1,0},{2,3},{4,5},{7,6},{5,4},{6,7},{8,9},{11,10},{9,8... | collective-permute-start | bytes 3145736 | tf_op jit(solution)/shard_map/ppermute | solution.py:796
  270.1 31.2 %collective-permute-start.23 = (f32[128,2048]{1,0:T(8,128)S(1)}, f32[128,2048]{1,0:T(8,128)S(1)}, u32[]{:S(2)}, u32[]{:S(2)}) collective-permute-start(f32[128,2048]{1,0:T(8,128)S(1)} %pass_on.24.refs_11_.refs_3_), channel_id=1, source_target_pairs={{0,1},{3,2},{1,0},{2,3},{4,5},{7,6},{5,4},{6,7},{8,9},{11,10},{9,8... | collective-permute-start | bytes 3145736 | tf_op jit(solution)/shard_map/ppermute | solution.py:796
  289.4 31.4 %collective-permute-start.22 = (f32[128,2048]{1,0:T(8,128)S(1)}, f32[128,2048]{1,0:T(8,128)}, u32[]{:S(2)}, u32[]{:S(2)}) collective-permute-start(f32[128,2048]{1,0:T(8,128)S(1)} %pass_on.25.refs_2_.refs_3_), channel_id=1, source_target_pairs={{0,1},{3,2},{1,0},{2,3},{4,5},{7,6},{5,4},{6,7},{8,9},{11,10},{9,8... | collective-permute-start | bytes 3145736 | tf_op jit(solution)/shard_map/ppermute | solution.py:796
  306.0 36.4 %collective-permute-start.30 = (f32[4,1,256,2048]{3,2,1,0:T(8,128)}, f32[4,1,256,2048]{3,2,1,0:T(8,128)}, u32[]{:S(2)}, u32[]{:S(2)}) collective-permute-start(f32[4,1,256,2048]{3,2,1,0:T(8,128)} %get-tuple-element.213), channel_id=1, source_target_pairs={{0,4},{4,0},{8,12},{12,8},{16,20},{20,16},{24,28},{28,24},{1,5},{5... | collective-permute-start | bytes 25165832 | tf_op jit(solution)/shard_map/ppermute | solution.py:944
  307.8 33.1 %collective-permute-start.27 = (f32[108,128]{1,0:T(8,128)S(1)}, f32[108,128]{1,0:T(8,128)S(1)}, u32[]{:S(2)}, u32[]{:S(2)}) collective-permute-start(f32[108,128]{1,0:T(8,128)S(1)} %add_up.3.refs_5_.refs_0_), channel_id=1, source_target_pairs={{0,8},{4,12},{8,0},{12,4},{16,24},{20,28},{24,16},{28,20},{1,9},{5... | collective-permute-start | bytes 165896 | tf_op jit(solution)/shard_map/ppermute | solution.py:830
  309.4 47.2 %collective-permute-start.31 = (f32[128,2048]{1,0:T(8,128)}, f32[128,2048]{1,0:T(8,128)}, u32[]{:S(2)}, u32[]{:S(2)}) collective-permute-start(f32[128,2048]{1,0:T(8,128)} %get-tuple-element.208.refs_2_.refs_3_), channel_id=1, source_target_pairs={{0,1},{3,2},{1,0},{2,3},{4,5},{7,6},{5,4},{6,7},{8,9},{11,10},{9,8... | collective-permute-start | bytes 3145736 | tf_op jit(solution)/shard_map/ppermute | solution.py:796
  323.1 38.7 %collective-permute-start.26 = (f32[128,2048]{1,0:T(8,128)S(1)}, f32[128,2048]{1,0:T(8,128)}, u32[]{:S(2)}, u32[]{:S(2)}) collective-permute-start(f32[128,2048]{1,0:T(8,128)S(1)} %get-tuple-element.210.refs_1_.held_ref), channel_id=1, source_target_pairs={{1,2},{2,1},{5,6},{6,5},{9,10},{10,9},{13,14},{14,13},{17,18},{18,... | collective-permute-start | bytes 3145736 | tf_op jit(solution)/shard_map/ppermute | solution.py:806
  327.5 46.4 %collective-permute-start.33 = (f32[128,2048]{1,0:T(8,128)}, f32[128,2048]{1,0:T(8,128)}, u32[]{:S(2)}, u32[]{:S(2)}) collective-permute-start(f32[128,2048]{1,0:T(8,128)} %pass_on.27.refs_2_.refs_3_), channel_id=1, source_target_pairs={{0,1},{3,2},{1,0},{2,3},{4,5},{7,6},{5,4},{6,7},{8,9},{11,10},{9,8... | collective-permute-start | bytes 3145736 | tf_op jit(solution)/shard_map/ppermute | solution.py:796
  364.1 27.8 %collective-permute-start.32 = (f32[136,2048]{1,0:T(8,128)}, f32[136,2048]{1,0:T(8,128)}, u32[]{:S(2)}, u32[]{:S(2)}) collective-permute-start(f32[136,2048]{1,0:T(8,128)} %get-tuple-element.218.refs_0_.refs_3_), channel_id=1, source_target_pairs={{0,1},{3,2},{1,0},{2,3},{4,5},{7,6},{5,4},{6,7},{8,9},{11,10},{9,8... | collective-permute-start | bytes 3342344 | tf_op jit(solution)/shard_map/ppermute | solution.py:796
  379.8 35.9 %collective-permute-start.39 = (f32[128,2048]{1,0:T(8,128)S(1)}, f32[128,2048]{1,0:T(8,128)S(1)}, u32[]{:S(2)}, u32[]{:S(2)}) collective-permute-start(f32[128,2048]{1,0:T(8,128)S(1)} %pass_on.29.refs_5_.refs_2_), channel_id=1, source_target_pairs={{1,0},{2,3},{5,4},{6,7},{9,8},{10,11},{13,12},{14,15},{17,16},{18,... | collective-permute-start | bytes 3145736 | tf_op jit(solution)/shard_map/ppermute | solution.py:796
  396.1 41.6 %collective-permute-start.38 = (f32[128,2048]{1,0:T(8,128)S(1)}, f32[128,2048]{1,0:T(8,128)S(1)}, u32[]{:S(2)}, u32[]{:S(2)}) collective-permute-start(f32[128,2048]{1,0:T(8,128)S(1)} %pass_on.30.refs_0_.refs_4_.refs_2_), channel_id=1, source_target_pairs={{1,0},{2,3},{5,4},{6,7},{9,8},{10,11},{13,12},{14,15},{17,16},{18,... | collective-permute-start | bytes 3145736 | tf_op jit(solution)/shard_map/ppermute | solution.py:796
  417.9 41.8 %collective-permute-start.37 = (f32[136,2048]{1,0:T(8,128)S(1)}, f32[136,2048]{1,0:T(8,128)S(1)}, u32[]{:S(2)}, u32[]{:S(2)}) collective-permute-start(f32[136,2048]{1,0:T(8,128)S(1)} %pass_on.31.refs_4_.refs_2_), channel_id=1, source_target_pairs={{1,0},{2,3},{5,4},{6,7},{9,8},{10,11},{13,12},{14,15},{17,16},{18,... | collective-permute-start | bytes 3342344 | tf_op jit(solution)/shard_map/ppermute | solution.py:796
  (49 other events, 820.3 us)
Sparse Core Ops, SparseCore 0:
  166.6 103.3 reduce-scatter.9
  274.0 93.5 reduce-scatter.7
  371.2 86.3 reduce-scatter.11
